TPU v7x, 32 devices: a whole 2x2x4 slice. The times are simulated.
32 devices in a mesh: gx: 16 (over z, y, core), yz: 2 (over x).
Axes of the slice: x: 2, y: 2, z: 4, core: 2. Of those that a mesh axis runs over, the one named last changes fastest.
Arguments:
- log_conductivity: float32 [128, 128, 128], P('gx', 'yz'), may hold values from 4.5 to 7.5
- storage: float32 [128, 128, 128], P('gx', 'yz'), may hold values from 0.3 to 1.5
- head: float32 [128, 128, 128], P('gx', 'yz'), may hold values from -6 to 6
- well_east: int32 [32], replicated, may hold values from 0 to 127
- well_north: int32 [32], replicated, may hold values from 0 to 127
- well_depth: int32 [32], replicated, may hold values from 0 to 127
- pump_rates: float32 [32], replicated, may hold values from -3000 to 3000
- probe_east: int32 [1024], replicated, may hold values from 0 to 127
- probe_north: int32 [1024], replicated, may hold values from 0 to 127
- probe_depth: int32 [1024], replicated, may hold values from 0 to 127
- probe_heads: float32 [1024], replicated, may hold values from -6 to 6
Outputs:
- head_next: float32 [128, 128, 128], P('gx', 'yz')
- log_conductivity_gradient: float32 [128, 128, 128], P('gx', 'yz')
- misfits: float32 [1024], replicated
All inputs are finite; a program needn't handle non-finite values.
Results may differ from a plain program's by a relative error of at most 0.0028.
Values sent between devices are 32-bit elements; how exact they have to be, the bound alone decides.
No kernel may reach another device: no remote copies, remote signals or barrier semaphores. Data moves between devices by JAX's collectives and lax.ppermute only.
A program may use at most 64 MiB of HBM per device.

v0:
```python
import jax
import jax.numpy as jnp
from jax import lax
from jax.experimental import pallas as pl
from jax.experimental.pallas import tpu as pltpu
from jax.sharding import PartitionSpec as P


misfit_weight = 100.0
lanes = 128
chunk = 8


def harmonic(left_cond, right_cond):
    return 2.0 * left_cond * right_cond / (left_cond + right_cond)


def eliminate(entry, links, grounds, loads):
    near_ground = near_load = far_ground = far_load = None
    steps = []
    for link, ground, load in zip(links, grounds, loads):
        if far_ground is not None:
            ground, load = ground + far_ground, load + far_load
        inverse = 1.0 / (entry + link + ground)
        to_near, to_far = entry * inverse, link * inverse
        far_ground, far_load = to_far * ground, to_far * load
        if near_ground is None:
            near_ground, near_load = to_near * ground, to_near * load
        else:
            near_ground, near_load = near_ground + to_near * ground, near_load + to_near * load
        steps.append((inverse, to_near, to_far, inverse * load))
        entry = to_near * link
    return (entry, near_ground, far_ground, near_load, far_load), steps


def eliminate_loads(factors, loads):
    near_load = far_load = None
    scaled = []
    for (inverse, to_near, to_far), load in zip(factors, loads):
        if far_load is not None:
            load = load + far_load
        far_load = to_far * load
        near_load = to_near * load if near_load is None else near_load + to_near * load
        scaled.append(inverse * load)
    return near_load, far_load, scaled


def expand(steps, near, far):
    values = []
    for _, to_near, to_far, scaled in reversed(steps):
        far = scaled + to_near * near + to_far * far
        values.append(far)
    return values[::-1]


def combine(blocks):
    pairs = list(zip(blocks[:-1], blocks[1:]))
    (entry, near_ground, far_ground, near_load, far_load), steps = eliminate(
        blocks[0][0],
        [after[0] for _, after in pairs],
        [before[2] + after[1] for before, after in pairs],
        [before[4] + after[3] for before, after in pairs],
    )
    joined = (
        entry,
        blocks[0][1] + near_ground,
        blocks[-1][2] + far_ground,
        blocks[0][3] + near_load,
        blocks[-1][4] + far_load,
    )
    return joined, steps


def combine_loads(blocks, factors):
    near_load, far_load, scaled = eliminate_loads(
        factors, [before[1] + after[0] for before, after in zip(blocks[:-1], blocks[1:])]
    )
    return (blocks[0][0] + near_load, blocks[-1][1] + far_load), scaled


def with_scaled(factors, scaled):
    return [factor + (value,) for factor, value in zip(factors, scaled)]


def factors_of(ref):
    return [(ref[i, 0], ref[i, 1], ref[i, 2]) for i in range(ref.shape[0])]


def steps_of(ref):
    return [(None, ref[i, 1], ref[i, 2], ref[i, 3]) for i in range(ref.shape[0])]


def keep_steps(ref, steps):
    for i, step in enumerate(steps):
        for j, value in enumerate(step):
            ref[i, j] = value


def face_gradient(left_cond, right_cond, adjoint_drop, head_drop):
    total = 1.0 / (left_cond + right_cond)
    flow = -(adjoint_drop * head_drop) * (2.0 * left_cond * right_cond * total) * total
    return flow * right_cond, flow * left_cond


def exact_parts(values):
    parts = []
    for _ in range(3):
        part = values.astype(jnp.bfloat16)
        parts.append(part)
        values = values - part.astype(jnp.float32)
    return parts


def run(body, outs, ins, scratch=(), smem=(), flops=1000000, limit=48):
    shapes = [jax.ShapeDtypeStruct(shape, jnp.float32) for shape in outs]
    size = 4 * (sum(x.size for x in ins) + sum(x.size for x in shapes))
    return pl.pallas_call(
        body,
        out_shape=shapes,
        in_specs=[pl.BlockSpec(memory_space=pltpu.VMEM)] * len(ins),
        out_specs=[pl.BlockSpec(memory_space=pltpu.VMEM)] * len(outs),
        scratch_shapes=[pltpu.VMEM(shape, kind) for shape, kind in scratch],
        compiler_params=pltpu.CompilerParams(vmem_limit_bytes=limit * 1024 * 1024),
        cost_estimate=pl.CostEstimate(flops=flops, bytes_accessed=size, transcendentals=0),
    )(*ins)


f32 = jnp.float32


def place(scratch, arrivals, stride):
    count = len(arrivals)
    position = lax.rem(lax.axis_index("gx") // stride, count)
    for turn, arrival in enumerate(arrivals):
        scratch[position ^ turn] = arrival[...]
    return position


def exchange(value, axis, stride, count):
    size = lax.axis_size(axis)
    return [value] + [
        lax.ppermute(value, axis, [(i, i ^ (turn * stride)) for i in range(size)])
        for turn in range(1, count)
    ]


def own_edges(scratch, position, near, faces, far):
    for i, value in enumerate([near] + faces + [far]):
        scratch[i] = value
    return scratch[position], scratch[position + 1]


def x_ends(cond):
    me, count = lax.axis_index("gx"), lax.axis_size("gx")
    depth = cond.shape[0]
    near = jnp.where(me == 0, 0.0, 2.0) * cond[0]
    far = jnp.where(me == count - 1, 0.0, 2.0) * cond[depth - 1]
    return near, far


def x_reduce(log_cond, storage, head, east, north, depth, rates,
             cond, steps_ref, own, send, five):
    cells, rows, _ = cond.shape
    me, group = lax.axis_index("gx"), lax.axis_index("yz")
    wells = rates.shape[1]
    cond[...] = jnp.exp(log_cond[...])
    local_east = east[...] - me * cells
    local_north = north[...] - group * rows
    inside = (
        (local_east >= 0) & (local_east < cells) & (local_north >= 0) & (local_north < rows)
    )
    spot = jnp.where(inside, local_east * rows + local_north, -1)
    at_row = jnp.where(
        lax.broadcasted_iota(jnp.int32, (cells * rows, wells), 0) == spot, 1.0, 0.0
    ).astype(jnp.bfloat16)
    at_depth = lax.broadcasted_iota(jnp.int32, (lanes, wells), 0) == depth[...]
    sources = sum(
        lax.dot_general(
            at_row, part, (((1,), (1,)), ((), ())), preferred_element_type=f32
        )
        for part in exact_parts(jnp.where(at_depth, rates[...], 0.0))
    ).reshape(cells, rows, lanes)
    near, far = x_ends(cond)
    links = [harmonic(cond[i], cond[i + 1]) for i in range(cells - 1)] + [far]
    block, steps = eliminate(
        near,
        links,
        [storage[i] for i in range(cells)],
        [storage[i] * head[i] + sources[i] for i in range(cells)],
    )
    keep_steps(steps_ref, steps)
    for i, value in enumerate(block):
        five[i] = value
    half = rows // 2
    mine = lax.rem(me, 2)
    own[...] = five[:, pl.ds(pl.multiple_of(mine * half, half), half), :]
    send[...] = five[:, pl.ds(pl.multiple_of((1 - mine) * half, half), half), :]


def make_join(stride, count):
    def join(*refs):
        arrivals, (joined_ref, steps_ref, scratch) = refs[:count], refs[count:]
        place(scratch, arrivals, stride)
        joined, steps = combine(
            [[scratch[i, j] for j in range(5)] for i in range(count)]
        )
        for i, value in enumerate(joined):
            joined_ref[i] = value
        keep_steps(steps_ref, steps)

    return join


def hand_back(edges, middle, own, send):
    near, far = edges
    first = lax.rem(lax.axis_index("gx"), 2) == 0
    own[0] = jnp.where(first, near, middle)
    own[1] = jnp.where(first, middle, far)
    send[0] = jnp.where(first, middle, near)
    send[1] = jnp.where(first, far, middle)


def make_top(stride, count, inner):
    def top(*refs):
        arrivals = refs[:count]
        group_steps, pair_steps, own, send, steps_ref, scratch, edges_top, edges_group = refs[count:]
        position = place(scratch, arrivals, stride)
        nothing = jnp.zeros(own.shape[1:], f32)
        _, steps = combine([[scratch[i, j] for j in range(5)] for i in range(count)])
        keep_steps(steps_ref, steps)
        edges = own_edges(edges_top, position, nothing, expand(steps, nothing, nothing), nothing)
        position = lax.rem(lax.axis_index("gx") // 2, inner)
        edges = own_edges(
            edges_group, position, edges[0], expand(steps_of(group_steps), *edges), edges[1]
        )
        hand_back(edges, expand(steps_of(pair_steps), *edges)[0], own, send)

    return top


def both_halves(own, other, scratch):
    half = own.shape[1]
    mine = lax.rem(lax.axis_index("gx"), 2)
    scratch[:, pl.ds(pl.multiple_of(mine * half, half), half), :] = own[...]
    scratch[:, pl.ds(pl.multiple_of((1 - mine) * half, half), half), :] = other[...]


def y_cells(ref, spot):
    chunks = ref.shape[1] // chunk
    return ref[:, pl.ds(spot, chunks, stride=chunk), :]


def y_links(cond):
    me, count = lax.axis_index("yz"), lax.axis_size("yz")
    cells = [y_cells(cond, spot) for spot in range(chunk)]
    place_of = lax.broadcasted_iota(jnp.int32, cells[0].shape, 1)
    chunks = cells[0].shape[1]
    near = jnp.where((place_of == 0) & (me == 0), 0.0, 2.0 * cells[0])
    far = jnp.where((place_of == chunks - 1) & (me == count - 1), 0.0, 2.0 * cells[-1])
    return cells, near, far


def by_chunk(value, scratch):
    slab, chunks, _ = value.shape
    scratch[...] = value.reshape(slab * chunks, lanes)
    return [scratch[pl.ds(i, slab, stride=chunks), :] for i in range(chunks)]


def from_chunk(values, scratch):
    slab, chunks = values[0].shape[0], len(values)
    for i, value in enumerate(values):
        scratch[pl.ds(i, slab, stride=chunks), :] = value
    return scratch[...].reshape(slab, chunks, lanes)


def y_reduce(own, other, x_steps, cond, storage,
             head_first, x_edges, cell_steps, chunk_steps, message, turned):
    cells = head_first.shape[0]
    both_halves(own, other, x_edges)
    far = x_edges[1]
    for i in reversed(range(cells)):
        far = x_steps[i, 3] + x_steps[i, 1] * x_edges[0] + x_steps[i, 2] * far
        head_first[i] = far
    conds, near, far = y_links(cond)
    links = [harmonic(conds[i], conds[i + 1]) for i in range(chunk - 1)] + [far]
    stores = [y_cells(storage, spot) for spot in range(chunk)]
    loads = [stores[spot] * y_cells(head_first, spot) for spot in range(chunk)]
    block, steps = eliminate(near, links, stores, loads)
    keep_steps(cell_steps, steps)
    parts = [by_chunk(value, turned.at[i]) for i, value in enumerate(block)]
    joined, steps = combine(list(zip(*parts)))
    keep_steps(chunk_steps, steps)
    for i, value in enumerate(joined):
        message[i] = value


def make_z(count, cuts):
    def z_solve(*refs):
        arrivals = refs[:count]
        (cell_steps, chunk_steps, cond, storage, east, north, depth, observed,
         y_factors, head_second, y_edges, head_third, z_terms, message, scaled_cells, scaled_chunks,
         scratch, edges, turned, ahead, behind, inverses, grounds, loads, second, third) = refs[count:]
        me = lax.axis_index("yz")
        for turn, arrival in enumerate(arrivals):
            scratch[me ^ turn] = arrival[...]
        nothing = jnp.zeros(arrivals[0].shape[1:], f32)
        _, steps = combine([[scratch[i, j] for j in range(5)] for i in range(count)])
        keep_steps(y_factors, steps)
        near, far = own_edges(edges, me, nothing, expand(steps, nothing, nothing), nothing)
        faces = [near] + expand(steps_of(chunk_steps), near, far) + [far]
        near = from_chunk(faces[:-1], turned.at[0])
        far = from_chunk(faces[1:], turned.at[1])
        y_edges[0] = near
        y_edges[1] = far
        for spot in reversed(range(chunk)):
            far = cell_steps[spot, 3] + cell_steps[spot, 1] * near + cell_steps[spot, 2] * far
            head_second[spot] = far
            second[:, pl.ds(spot, second.shape[1] // chunk, stride=chunk), :] = far

        slab, rows, _ = cond.shape
        total = slab * rows
        piece = total // cuts
        lane = lax.broadcasted_iota(jnp.int32, (piece, lanes), 1)

        def cut(ref, i):
            per = slab // cuts
            return ref[i * per:(i + 1) * per].reshape(piece, lanes)

        for i in range(cuts):
            here = cut(cond, i)
            ahead[0, i] = jnp.where(
                lane == lanes - 1, 0.0, harmonic(here, pltpu.roll(here, lanes - 1, 1))
            )
            grounds[i] = cut(storage, i)
            loads[i] = cut(storage, i) * cut(second, i)
        levels = lanes.bit_length() - 1
        for level in range(levels):
            shift = 1 << level
            for i in range(cuts):
                link, ground, load = ahead[level, i], grounds[i], loads[i]
                link_back = pltpu.roll(link, shift, 1)
                inverse = 1.0 / (link + link_back + ground)
                behind[level, i] = link_back
                inverses[level, i] = inverse
                held = inverse * ground
                passed = inverse * load
                grounds[i] = (
                    ground
                    + link * pltpu.roll(held, lanes - shift, 1)
                    + link_back * pltpu.roll(held, shift, 1)
                )
                loads[i] = (
                    load
                    + link * pltpu.roll(passed, lanes - shift, 1)
                    + link_back * pltpu.roll(passed, shift, 1)
                )
                if level < levels - 1:
                    ahead[level + 1, i] = link * pltpu.roll(inverse * link, lanes - shift, 1)
        for i in range(cuts):
            grounds[i] = 1.0 / grounds[i]
            third[pl.ds(i * piece, piece), :] = loads[i] * grounds[i]
        head_third[...] = third[...].reshape(slab, rows, lanes)

        local_east = east[...] - lax.axis_index("gx") * slab
        local_north = north[...] - me * rows
        inside = (
            (local_east >= 0) & (local_east < slab) & (local_north >= 0) & (local_north < rows)
        )
        points = inside.shape[1]
        spot = jnp.where(inside, local_east * rows + local_north, -1)
        at_row = jnp.where(
            lax.broadcasted_iota(jnp.int32, (total, points), 0) == spot, 1.0, 0.0
        ).astype(jnp.bfloat16)
        at_depth = lax.broadcasted_iota(jnp.int32, (lanes, points), 0) == depth[...]
        found = sum(
            lax.dot_general(
                part, at_row, (((0,), (0,)), ((), ())), preferred_element_type=f32
            )
            for part in exact_parts(third[...])
        )
        found = jnp.sum(jnp.where(at_depth, found, 0.0), axis=0, keepdims=True)
        misfit = jnp.where(inside, found - observed[...], 0.0)
        for i in range(points // lanes):
            message[2, i:i + 1, :] = misfit[:, i * lanes:(i + 1) * lanes]
        parts = [
            jnp.where(at_depth, part.astype(f32), 0.0).astype(jnp.bfloat16)
            for part in exact_parts(misfit_weight * misfit)
        ]
        source = sum(
            lax.dot_general(
                at_row, part, (((1,), (1,)), ((), ())), preferred_element_type=f32
            )
            for part in parts
        )
        for i in range(cuts):
            loads[i] = source[i * piece:(i + 1) * piece]
        for level in range(levels):
            shift = 1 << level
            for i in range(cuts):
                load = loads[i]
                passed = inverses[level, i] * load
                loads[i] = (
                    load
                    + ahead[level, i] * pltpu.roll(passed, lanes - shift, 1)
                    + behind[level, i] * pltpu.roll(passed, shift, 1)
                )
        per = slab // cuts
        for i in range(cuts):
            adjoint = loads[i] * grounds[i]
            here = cut(cond, i)
            head = third[pl.ds(i * piece, piece), :]
            to_left, to_right = face_gradient(
                here,
                pltpu.roll(here, lanes - 1, 1),
                adjoint - pltpu.roll(adjoint, lanes - 1, 1),
                head - pltpu.roll(head, lanes - 1, 1),
            )
            to_left = jnp.where(lane == lanes - 1, 0.0, to_left)
            to_right = jnp.where(lane == lanes - 1, 0.0, to_right)
            z_terms[i * per:(i + 1) * per] = (
                (to_left + pltpu.roll(to_right, 1, 1)).reshape(per, rows, lanes)
            )
            second[i * per:(i + 1) * per] = (cut(storage, i) * adjoint).reshape(per, rows, lanes)

        near, far, scaled = eliminate_loads(
            factors_of(cell_steps), [y_cells(second, i) for i in range(chunk)]
        )
        for i, value in enumerate(scaled):
            scaled_cells[i] = value
        blocks = list(zip(by_chunk(near, turned.at[0]), by_chunk(far, turned.at[1])))
        joined, scaled = combine_loads(blocks, factors_of(chunk_steps))
        for i, value in enumerate(scaled):
            scaled_chunks[i] = value
        message[0] = joined[0]
        message[1] = joined[1]

    return z_solve


def make_y_back(count):
    def y_back(*refs):
        arrivals = refs[:count]
        (y_factors, cell_steps, chunk_steps, scaled_cells, scaled_chunks, head_second, y_edges,
         cond, storage, z_terms, x_steps,
         terms, scaled_x, own, send, scratch, edges, turned, second, pair) = refs[count:]
        me = lax.axis_index("yz")
        misfit = arrivals[0][2]
        for turn, arrival in enumerate(arrivals):
            scratch[me ^ turn] = arrival[:2]
            if turn:
                misfit = misfit + arrival[2]
        nothing = jnp.zeros(arrivals[0].shape[1:], f32)
        factors = factors_of(y_factors)
        _, scaled = combine_loads([[scratch[i, 0], scratch[i, 1]] for i in range(count)], factors)
        faces = expand(with_scaled(factors, scaled), nothing, nothing)
        near, far = own_edges(edges, me, nothing, faces, nothing)
        factors = factors_of(chunk_steps)
        steps = with_scaled(factors, [scaled_chunks[i] for i in range(len(factors))])
        faces = [near] + expand(steps, near, far) + [far]
        near = from_chunk(faces[:-1], turned.at[0])
        far = from_chunk(faces[1:], turned.at[1])
        conds, near_link, far_link = y_links(cond)
        after = far
        adjoint = [None] * chunk
        for spot in reversed(range(chunk)):
            after = scaled_cells[spot] + cell_steps[spot, 1] * near + cell_steps[spot, 2] * after
            adjoint[spot] = after
            second[:, pl.ds(spot, second.shape[1] // chunk, stride=chunk), :] = after
        from_left = -near_link * (adjoint[0] - near) * (head_second[0] - y_edges[0])
        for spot in range(chunk):
            if spot < chunk - 1:
                to_left, to_right = face_gradient(
                    conds[spot], conds[spot + 1],
                    adjoint[spot] - adjoint[spot + 1],
                    head_second[spot] - head_second[spot + 1],
                )
                value = from_left + to_left
                from_left = to_right
            else:
                value = from_left - far_link * (adjoint[spot] - far) * (head_second[spot] - y_edges[1])
            spots = (slice(None), pl.ds(spot, second.shape[1] // chunk, stride=chunk), slice(None))
            terms[spots] = value + z_terms[spots]

        near, far, scaled = eliminate_loads(
            factors_of(x_steps), [storage[i] * second[i] for i in range(second.shape[0])]
        )
        for i, value in enumerate(scaled):
            scaled_x[i] = value
        pair[0] = near
        pair[1] = far
        half = pair.shape[1] // 2
        mine = lax.rem(lax.axis_index("gx"), 2)
        for ref, side in ((own, mine), (send, 1 - mine)):
            for i in range(2):
                ref[i * half:(i + 1) * half] = pair[i, pl.ds(pl.multiple_of(side * half, half), half), :]
            ref[2 * half:] = misfit

    return y_back


def loads_in(arrivals, scratch, stride):
    rows = scratch.shape[2]
    count = len(arrivals)
    position = lax.rem(lax.axis_index("gx") // stride, count)
    misfit = None
    for turn, arrival in enumerate(arrivals):
        scratch[position ^ turn, 0] = arrival[:rows]
        scratch[position ^ turn, 1] = arrival[rows:2 * rows]
        part = arrival[2 * rows:]
        misfit = part if misfit is None else misfit + part
    return [[scratch[i, 0], scratch[i, 1]] for i in range(count)], misfit, position


def make_join_loads(stride, count):
    def join(*refs):
        arrivals, (steps_ref, message, scaled_ref, scratch) = refs[:count], refs[count:]
        blocks, misfit, _ = loads_in(arrivals, scratch, stride)
        joined, scaled = combine_loads(blocks, factors_of(steps_ref))
        rows = scratch.shape[2]
        message[:rows] = joined[0]
        message[rows:2 * rows] = joined[1]
        message[2 * rows:] = misfit
        for i, value in enumerate(scaled):
            scaled_ref[i] = value

    return join


def make_top_loads(stride, count, inner):
    def top(*refs):
        arrivals = refs[:count]
        (top_steps, group_steps, group_scaled, pair_steps, pair_scaled,
         own, send, misfit_ref, scratch, edges_top, edges_group) = refs[count:]
        blocks, misfit, position = loads_in(arrivals, scratch, stride)
        misfit_ref[...] = misfit
        nothing = jnp.zeros(own.shape[1:], f32)
        factors = factors_of(top_steps)
        _, scaled = combine_loads(blocks, factors)
        faces = expand(with_scaled(factors, scaled), nothing, nothing)
        edges = own_edges(edges_top, position, nothing, faces, nothing)
        position = lax.rem(lax.axis_index("gx") // 2, inner)
        factors = factors_of(group_steps)
        steps = with_scaled(factors, [group_scaled[i] for i in range(len(factors))])
        edges = own_edges(edges_group, position, edges[0], expand(steps, *edges), edges[1])
        steps = with_scaled(factors_of(pair_steps), [pair_scaled[0]])
        hand_back(edges, expand(steps, *edges)[0], own, send)

    return top


def x_back(own, other, x_steps, scaled_x, cond, head, x_edges, terms, gradient, edges):
    cells = cond.shape[0]
    both_halves(own, other, edges)
    near_link, far_link = x_ends(cond)
    adjoint = [None] * cells
    after = edges[1]
    for i in reversed(range(cells)):
        after = scaled_x[i] + x_steps[i, 1] * edges[0] + x_steps[i, 2] * after
        adjoint[i] = after
    from_left = -near_link * (adjoint[0] - edges[0]) * (head[0] - x_edges[0])
    for i in range(cells):
        if i < cells - 1:
            to_left, to_right = face_gradient(
                cond[i], cond[i + 1], adjoint[i] - adjoint[i + 1], head[i] - head[i + 1]
            )
            gradient[i] = terms[i] + from_left + to_left
            from_left = to_right
        else:
            gradient[i] = (
                terms[i] + from_left - far_link * (adjoint[i] - edges[1]) * (head[i] - x_edges[1])
            )


def shards(log_cond, storage, head, well_east, well_north, well_depth, pump_rates,
           probe_east, probe_north, probe_depth, probe_heads):
    slab, rows, _ = log_cond.shape
    devices, columns = lax.axis_size("gx"), lax.axis_size("yz")
    inner = 4 if devices >= 16 else 2
    outer = devices // (2 * inner)
    half, chunks = rows // 2, rows // chunk
    points = probe_heads.shape[0]
    grid = (slab, rows, lanes)
    plane = (half, lanes)
    cell = (chunk, slab, chunks, lanes)
    line = (slab, lanes)

    cond, x_steps, own, send = run(
        x_reduce,
        [grid, (slab, 4, rows, lanes), (5,) + plane, (5,) + plane],
        [log_cond, storage, head]
        + [value.reshape(1, -1) for value in (well_east, well_north, well_depth, pump_rates)],
        [((5, rows, lanes), f32)],
    )
    swap = [(i, i ^ 1) for i in range(devices)]
    joined, pair_steps = run(
        make_join(1, 2),
        [(5,) + plane, (1, 4) + plane],
        [own, lax.ppermute(send, "gx", swap)],
        [((2, 5) + plane, f32)],
    )
    joined, group_steps = run(
        make_join(2, inner),
        [(5,) + plane, (inner - 1, 4) + plane],
        exchange(joined, "gx", 2, inner),
        [((inner, 5) + plane, f32)],
    )
    own, send, top_steps = run(
        make_top(2 * inner, outer, inner),
        [(2,) + plane, (2,) + plane, (outer - 1, 4) + plane],
        exchange(joined, "gx", 2 * inner, outer) + [group_steps, pair_steps],
        [((outer, 5) + plane, f32), ((outer + 1,) + plane, f32), ((inner + 1,) + plane, f32)],
    )
    head_first, x_edges, cell_steps, chunk_steps, message = run(
        y_reduce,
        [grid, (2, rows, lanes), (chunk, 4) + cell[1:], (chunks - 1, 4) + line, (5,) + line],
        [own, lax.ppermute(send, "gx", swap), x_steps, cond, storage],
        [((5, slab * chunks, lanes), f32)],
    )
    cuts = 4
    piece = (cuts, slab * rows // cuts, lanes)
    levels = lanes.bit_length() - 1
    (y_factors, head_second, y_edges, head_third, z_terms, message, scaled_cells, scaled_chunks) = run(
        make_z(columns, cuts),
        [(columns - 1, 4) + line, cell, (2,) + cell[1:], grid, grid,
         (3,) + line, cell, (chunks - 1,) + line],
        exchange(message, "yz", 1, columns)
        + [cell_steps, chunk_steps, cond, storage]
        + [value.reshape(1, -1) for value in (probe_east, probe_north, probe_depth, probe_heads)],
        [((columns, 5) + line, f32), ((columns + 1,) + line, f32), ((2, slab * chunks, lanes), f32)]
        + [((levels,) + piece, f32)] * 3 + [(piece, f32)] * 2
        + [(grid, f32), ((slab * rows, lanes), f32)],
    )
    extra = points // lanes
    note = (2 * half + extra, lanes)
    terms, scaled_x, own, send = run(
        make_y_back(columns),
        [grid, grid, note, note],
        exchange(message, "yz", 1, columns)
        + [y_factors, cell_steps, chunk_steps, scaled_cells, scaled_chunks, head_second, y_edges,
           cond, storage, z_terms, x_steps],
        [((columns, 2) + line, f32), ((columns + 1,) + line, f32), ((2, slab * chunks, lanes), f32),
         (grid, f32), ((2, rows, lanes), f32)],
    )
    message, pair_scaled = run(
        make_join_loads(1, 2),
        [note, (1,) + plane],
        [own, lax.ppermute(send, "gx", swap), pair_steps],
        [((2, 2) + plane, f32)],
    )
    message, group_scaled = run(
        make_join_loads(2, inner),
        [note, (inner - 1,) + plane],
        exchange(message, "gx", 2, inner) + [group_steps],
        [((inner, 2) + plane, f32)],
    )
    own, send, misfits = run(
        make_top_loads(2 * inner, outer, inner),
        [(2,) + plane, (2,) + plane, (extra, lanes)],
        exchange(message, "gx", 2 * inner, outer)
        + [top_steps, group_steps, group_scaled, pair_steps, pair_scaled],
        [((outer, 2) + plane, f32), ((outer + 1,) + plane, f32), ((inner + 1,) + plane, f32)],
    )
    (gradient,) = run(
        x_back,
        [grid],
        [own, lax.ppermute(send, "gx", swap), x_steps, scaled_x, cond, head_first, x_edges, terms],
        [((2, rows, lanes), f32)],
    )
    return head_third, gradient, misfits.reshape(-1)


def solution(mesh):
    cells = P("gx", "yz", None)
    return jax.shard_map(
        shards,
        mesh=mesh,
        in_specs=(cells, cells, cells) + (P(),) * 8,
        out_specs=(cells, cells, P()),
        check_vma=False,
    )
```

profile of v0, /device:TPU:0, one launch (start us, length us, event | category | flops | bytes accessed | tf_op | source)
XLA Modules:
  0.0 55.9 jit_solution(12423362972931136252)
XLA Ops:
  0.7 0.6 %copy-done.11 = f32[32]{0:T(128)S(1)} copy-done((f32[32]{0:T(128)S(1)}, f32[32]{0:T(128)}, u32[]{:S(2)}) %copy-start.11) | copy-done | bytes 152
  1.3 0.9 %copy-done = f32[8,64,128]{2,1,0:T(8,128)S(1)} copy-done((f32[8,64,128]{2,1,0:T(8,128)S(1)}, f32[8,64,128]{2,1,0:T(8,128)}, u32[]{:S(2)}) %copy-start) | copy-done | bytes 262168
  2.3 0.9 %copy-done.2 = f32[8,64,128]{2,1,0:T(8,128)S(1)} copy-done((f32[8,64,128]{2,1,0:T(8,128)S(1)}, f32[8,64,128]{2,1,0:T(8,128)}, u32[]{:S(2)}) %copy-start.2) | copy-done | bytes 262168
  3.2 0.9 %copy-done.3 = f32[8,64,128]{2,1,0:T(8,128)S(1)} copy-done((f32[8,64,128]{2,1,0:T(8,128)S(1)}, f32[8,64,128]{2,1,0:T(8,128)}, u32[]{:S(2)}) %copy-start.3) | copy-done | bytes 262168
  4.6 0.5 collective-permute-start
  5.1 0.9 %collective-permute-done.refs_1_ = f32[5,32,128]{2,1,0:T(8,128)S(1)} collective-permute-done((f32[5,32,128]{2,1,0:T(8,128)S(1)}, f32[5,32,128]{2,1,0:T(8,128)S(1)}, u32[]{:S(2)}, u32[]{:S(2)}) %collective-permute-start) | collective-permute-done | bytes 81952 | tf_op jit(solution)/shard_map/ppermute | solution.py:598
  6.1 3.9 %collective-permute-start.3 = (f32[5,32,128]{2,1,0:T(8,128)S(1)}, f32[5,32,128]{2,1,0:T(8,128)S(1)}, u32[]{:S(2)}, u32[]{:S(2)}) collective-permute-start(f32[5,32,128]{2,1,0:T(8,128)S(1)} %get-tuple-element.40.refs_0_), channel_id=1, source_target_pairs={{0,12},{2,14},{4,8},{6,10},{8,4},{10,6},{12,0},{14,2},{16,28},{18,... | collective-permute-start | bytes 245768 | tf_op jit(solution)/shard_map/ppermute | solution.py:142
  10.0 0.4 collective-permute-start.2
  10.6 2.5 %collective-permute-done.3.refs_3_ = f32[5,32,128]{2,1,0:T(8,128)S(1)} collective-permute-done((f32[5,32,128]{2,1,0:T(8,128)S(1)}, f32[5,32,128]{2,1,0:T(8,128)S(1)}, u32[]{:S(2)}, u32[]{:S(2)}) %collective-permute-start.3) | collective-permute-done | bytes 81952 | tf_op jit(solution)/shard_map/ppermute | solution.py:142
  13.1 1.5 %collective-permute-done.2.refs_2_ = f32[5,32,128]{2,1,0:T(8,128)S(1)} collective-permute-done((f32[5,32,128]{2,1,0:T(8,128)S(1)}, f32[5,32,128]{2,1,0:T(8,128)S(1)}, u32[]{:S(2)}, u32[]{:S(2)}) %collective-permute-start.2) | collective-permute-done | bytes 81952 | tf_op jit(solution)/shard_map/ppermute | solution.py:142
  15.0 2.7 %collective-permute-start.4 = (f32[5,32,128]{2,1,0:T(8,128)S(1)}, f32[5,32,128]{2,1,0:T(8,128)S(1)}, u32[]{:S(2)}, u32[]{:S(2)}) collective-permute-start(f32[5,32,128]{2,1,0:T(8,128)S(1)} %get-tuple-element.41.refs_0_), channel_id=1, source_target_pairs={{0,16},{2,18},{4,20},{6,22},{8,24},{10,26},{12,28},{14,30},{16,0},... | collective-permute-start | bytes 245768 | tf_op jit(solution)/shard_map/ppermute | solution.py:142
  17.6 2.9 %collective-permute-done.4.refs_1_ = f32[5,32,128]{2,1,0:T(8,128)S(1)} collective-permute-done((f32[5,32,128]{2,1,0:T(8,128)S(1)}, f32[5,32,128]{2,1,0:T(8,128)S(1)}, u32[]{:S(2)}, u32[]{:S(2)}) %collective-permute-start.4) | collective-permute-done | bytes 81952 | tf_op jit(solution)/shard_map/ppermute | solution.py:142
  20.7 1.2 %collective-permute-done.5.other = f32[2,32,128]{2,1,0:T(8,128)S(1)} collective-permute-done((f32[2,32,128]{2,1,0:T(8,128)S(1)}, f32[2,32,128]{2,1,0:T(8,128)S(1)}, u32[]{:S(2)}, u32[]{:S(2)}) %collective-permute-start.5) | collective-permute-done | bytes 32800 | tf_op jit(solution)/shard_map/ppermute | solution.py:616
  21.9 0.4 shard_map.134
  22.4 1.6 %collective-permute-start.6 = (f32[5,8,128]{2,1,0:T(8,128)S(1)}, f32[5,8,128]{2,1,0:T(8,128)S(1)}, u32[]{:S(2)}, u32[]{:S(2)}) collective-permute-start(f32[5,8,128]{2,1,0:T(8,128)S(1)} %get-tuple-element.48.refs_0_), channel_id=1, source_target_pairs={{0,1},{1,0},{2,3},{3,2},{4,5},{5,4},{6,7},{7,6},{8,9},{9,8},{10,11... | collective-permute-start | bytes 61448 | tf_op jit(solution)/shard_map/ppermute | solution.py:142
  23.9 2.3 %collective-permute-done.6.refs_1_ = f32[5,8,128]{2,1,0:T(8,128)S(1)} collective-permute-done((f32[5,8,128]{2,1,0:T(8,128)S(1)}, f32[5,8,128]{2,1,0:T(8,128)S(1)}, u32[]{:S(2)}, u32[]{:S(2)}) %collective-permute-start.6) | collective-permute-done | bytes 20512 | tf_op jit(solution)/shard_map/ppermute | solution.py:142
  26.2 0.7 %copy-done.5 = s32[1024]{0:T(1024)S(1)} copy-done((s32[1024]{0:T(1024)S(1)}, s32[1024]{0:T(1024)}, u32[]{:S(2)}) %copy-start.5) | copy-done | bytes 4120
  26.9 7.7 %shard_map.135 = (f32[1,4,8,128]{3,2,1,0:T(8,128)S(1)}, f32[8,8,8,128]{3,2,1,0:T(8,128)S(1)}, f32[2,8,8,128]{3,2,1,0:T(8,128)S(1)}, f32[8,64,128]{2,1,0:T(8,128)...) custom-call(f32[5,8,128]{2,1,0:T(8,128)S(1)} %get-tuple-element.48.r, ...), custom_call_target="tpu_custom_call" | custom-call | flops 1000000 | bytes 2916352 | tf_op jit(solution)/shard_map/pallas_call | solution.py:117
  34.6 1.5 %collective-permute-start.7 = (f32[3,8,128]{2,1,0:T(8,128)S(1)}, f32[3,8,128]{2,1,0:T(8,128)S(1)}, u32[]{:S(2)}, u32[]{:S(2)}) collective-permute-start(f32[3,8,128]{2,1,0:T(8,128)S(1)} %get-tuple-element.52.refs_0_), channel_id=1, source_target_pairs={{0,1},{1,0},{2,3},{3,2},{4,5},{5,4},{6,7},{7,6},{8,9},{9,8},{10,11... | collective-permute-start | bytes 36872 | tf_op jit(solution)/shard_map/ppermute | solution.py:142
  36.1 2.2 %collective-permute-done.7.refs_1_ = f32[3,8,128]{2,1,0:T(8,128)S(1)} collective-permute-done((f32[3,8,128]{2,1,0:T(8,128)S(1)}, f32[3,8,128]{2,1,0:T(8,128)S(1)}, u32[]{:S(2)}, u32[]{:S(2)}) %collective-permute-start.7) | collective-permute-done | bytes 12320 | tf_op jit(solution)/shard_map/ppermute | solution.py:142
  38.3 0.5 shard_map.136
  38.8 1.2 %collective-permute-done.8.refs_1_ = f32[72,128]{1,0:T(8,128)S(1)} collective-permute-done((f32[72,128]{1,0:T(8,128)S(1)}, f32[72,128]{1,0:T(8,128)S(1)}, u32[]{:S(2)}, u32[]{:S(2)}) %collective-permute-start.8) | collective-permute-done | bytes 36896 | tf_op jit(solution)/shard_map/ppermute | solution.py:647
  40.1 2.6 %collective-permute-start.11 = (f32[72,128]{1,0:T(8,128)S(1)}, f32[72,128]{1,0:T(8,128)S(1)}, u32[]{:S(2)}, u32[]{:S(2)}) collective-permute-start(f32[72,128]{1,0:T(8,128)S(1)} %get-tuple-element.61.refs_0_), channel_id=1, source_target_pairs={{0,12},{2,14},{4,8},{6,10},{8,4},{10,6},{12,0},{14,2},{16,28},{18,... | collective-permute-start | bytes 110600 | tf_op jit(solution)/shard_map/ppermute | solution.py:142
  42.7 1.6 %collective-permute-start.10 = (f32[72,128]{1,0:T(8,128)S(1)}, f32[72,128]{1,0:T(8,128)S(1)}, u32[]{:S(2)}, u32[]{:S(2)}) collective-permute-start(f32[72,128]{1,0:T(8,128)S(1)} %get-tuple-element.61.refs_0_), channel_id=1, source_target_pairs={{0,8},{2,10},{4,12},{6,14},{8,0},{10,2},{12,4},{14,6},{16,24},{18,... | collective-permute-start | bytes 110600 | tf_op jit(solution)/shard_map/ppermute | solution.py:142
  44.3 0.7 %collective-permute-done.11.refs_3_ = f32[72,128]{1,0:T(8,128)S(1)} collective-permute-done((f32[72,128]{1,0:T(8,128)S(1)}, f32[72,128]{1,0:T(8,128)S(1)}, u32[]{:S(2)}, u32[]{:S(2)}) %collective-permute-start.11) | collective-permute-done | bytes 36896 | tf_op jit(solution)/shard_map/ppermute | solution.py:142
  45.0 1.7 %collective-permute-done.10.refs_2_ = f32[72,128]{1,0:T(8,128)S(1)} collective-permute-done((f32[72,128]{1,0:T(8,128)S(1)}, f32[72,128]{1,0:T(8,128)S(1)}, u32[]{:S(2)}, u32[]{:S(2)}) %collective-permute-start.10) | collective-permute-done | bytes 36896 | tf_op jit(solution)/shard_map/ppermute | solution.py:142
  46.7 1.6 %collective-permute-done.9.refs_1_ = f32[72,128]{1,0:T(8,128)S(1)} collective-permute-done((f32[72,128]{1,0:T(8,128)S(1)}, f32[72,128]{1,0:T(8,128)S(1)}, u32[]{:S(2)}, u32[]{:S(2)}) %collective-permute-start.9) | collective-permute-done | bytes 36896 | tf_op jit(solution)/shard_map/ppermute | solution.py:142
  48.3 1.9 %collective-permute-start.12 = (f32[72,128]{1,0:T(8,128)S(1)}, f32[72,128]{1,0:T(8,128)S(1)}, u32[]{:S(2)}, u32[]{:S(2)}) collective-permute-start(f32[72,128]{1,0:T(8,128)S(1)} %get-tuple-element.62.refs_0_), channel_id=1, source_target_pairs={{0,16},{2,18},{4,20},{6,22},{8,24},{10,26},{12,28},{14,30},{16,0},... | collective-permute-start | bytes 110600 | tf_op jit(solution)/shard_map/ppermute | solution.py:142
  50.2 3.1 %collective-permute-done.12.refs_1_ = f32[72,128]{1,0:T(8,128)S(1)} collective-permute-done((f32[72,128]{1,0:T(8,128)S(1)}, f32[72,128]{1,0:T(8,128)S(1)}, u32[]{:S(2)}, u32[]{:S(2)}) %collective-permute-start.12) | collective-permute-done | bytes 36896 | tf_op jit(solution)/shard_map/ppermute | solution.py:142
  53.2 0.6 %shard_map.139 = (f32[2,32,128]{2,1,0:T(8,128)S(1)}, f32[2,32,128]{2,1,0:T(8,128)S(1)}, f32[8,128]{1,0:T(8,128)}) custom-call(f32[72,128]{1,0:T(8,128)S(1)} %get-tuple-element.62.refs_0_, f32[72,128]{1,0:T(8,128)S(1)} %collective-permute-done.12.refs_1_, f32[1,4,32,128]{3,2,1,0:T(8,128)S(1)} %get-tuple-element.63.refs_2_, ...), custom_call_target="tpu_custom_call" | custom-call | flops 1000000 | bytes 536576 | tf_op jit(solution)/shard_map/pallas_call | solution.py:117
  53.8 1.2 %collective-permute-done.13.other = f32[2,32,128]{2,1,0:T(8,128)S(1)} collective-permute-done((f32[2,32,128]{2,1,0:T(8,128)S(1)}, f32[2,32,128]{2,1,0:T(8,128)S(1)}, u32[]{:S(2)}, u32[]{:S(2)}) %collective-permute-start.13) | collective-permute-done | bytes 32800 | tf_op jit(solution)/shard_map/ppermute | solution.py:666
  55.0 0.9 %shard_map.140 = f32[8,64,128]{2,1,0:T(8,128)} custom-call(f32[2,32,128]{2,1,0:T(8,128)S(1)} %get-tuple-element.66.own, f32[2,32,128]{2,1,0:T(8,128)S(1)} %collective-permute-done.13.other, f32[8,4,64,128]{3,2,1,0:T(8,128)S(1)} %get-tuple-element.46.x_steps.refs_12_, f32[8,64,128]{2,1,0:T(8,128)S(1)} %get-tuple-element.68.scaled_x, ...), custom_call_target="tpu_custom_call" | custom-call | flops 1000000 | bytes 2490368 | tf_op jit(solution)/shard_map/pallas_call | solution.py:117
  (31 shorter events, 1.3 us)
Async XLA Ops:
  0.6 0.7 %copy-start.11 = (f32[32]{0:T(128)S(1)}, f32[32]{0:T(128)}, u32[]{:S(2)}) copy-start(f32[32]{0:T(128)} %param.17) | copy-start | bytes 388
  0.6 0.7 %copy-start.8 = (s32[32]{0:T(128)S(1)}, s32[32]{0:T(128)}, u32[]{:S(2)}) copy-start(s32[32]{0:T(128)} %param.14) | copy-start | bytes 388
  0.7 0.7 %copy-start.9 = (s32[32]{0:T(128)S(1)}, s32[32]{0:T(128)}, u32[]{:S(2)}) copy-start(s32[32]{0:T(128)} %param.15) | copy-start | bytes 388
  0.7 0.7 %copy-start.10 = (s32[32]{0:T(128)S(1)}, s32[32]{0:T(128)}, u32[]{:S(2)}) copy-start(s32[32]{0:T(128)} %param.16) | copy-start | bytes 388
  1.3 0.9 %copy-start = (f32[8,64,128]{2,1,0:T(8,128)S(1)}, f32[8,64,128]{2,1,0:T(8,128)}, u32[]{:S(2)}) copy-start(f32[8,64,128]{2,1,0:T(8,128)} %refs_10_.1) | copy-start | bytes 786436
  2.3 0.9 %copy-start.2 = (f32[8,64,128]{2,1,0:T(8,128)S(1)}, f32[8,64,128]{2,1,0:T(8,128)}, u32[]{:S(2)}) copy-start(f32[8,64,128]{2,1,0:T(8,128)} %log_cond.1) | copy-start | bytes 786436
  3.2 0.9 %copy-start.3 = (f32[8,64,128]{2,1,0:T(8,128)S(1)}, f32[8,64,128]{2,1,0:T(8,128)}, u32[]{:S(2)}) copy-start(f32[8,64,128]{2,1,0:T(8,128)} %head.1) | copy-start | bytes 786436
  4.6 1.4 %collective-permute-start = (f32[5,32,128]{2,1,0:T(8,128)S(1)}, f32[5,32,128]{2,1,0:T(8,128)S(1)}, u32[]{:S(2)}, u32[]{:S(2)}) collective-permute-start(f32[5,32,128]{2,1,0:T(8,128)S(1)} %get-tuple-element.39), channel_id=1, source_target_pairs={{0,2},{2,0},{4,6},{6,4},{8,10},{10,8},{12,14},{14,12},{16,18},{18,... | collective-permute-start | bytes 245768 | tf_op jit(solution)/shard_map/ppermute | solution.py:598
  6.1 7.1 %collective-permute-start.3 = (f32[5,32,128]{2,1,0:T(8,128)S(1)}, f32[5,32,128]{2,1,0:T(8,128)S(1)}, u32[]{:S(2)}, u32[]{:S(2)}) collective-permute-start(f32[5,32,128]{2,1,0:T(8,128)S(1)} %get-tuple-element.40.refs_0_), channel_id=1, source_target_pairs={{0,12},{2,14},{4,8},{6,10},{8,4},{10,6},{12,0},{14,2},{16,28},{18,... | collective-permute-start | bytes 245768 | tf_op jit(solution)/shard_map/ppermute | solution.py:142
  10.0 4.7 %collective-permute-start.2 = (f32[5,32,128]{2,1,0:T(8,128)S(1)}, f32[5,32,128]{2,1,0:T(8,128)S(1)}, u32[]{:S(2)}, u32[]{:S(2)}) collective-permute-start(f32[5,32,128]{2,1,0:T(8,128)S(1)} %get-tuple-element.40.refs_0_), channel_id=1, source_target_pairs={{0,8},{2,10},{4,12},{6,14},{8,0},{10,2},{12,4},{14,6},{16,24},{18,... | collective-permute-start | bytes 245768 | tf_op jit(solution)/shard_map/ppermute | solution.py:142
  10.4 4.4 %collective-permute-start.1 = (f32[5,32,128]{2,1,0:T(8,128)S(1)}, f32[5,32,128]{2,1,0:T(8,128)S(1)}, u32[]{:S(2)}, u32[]{:S(2)}) collective-permute-start(f32[5,32,128]{2,1,0:T(8,128)S(1)} %get-tuple-element.40.refs_0_), channel_id=1, source_target_pairs={{0,4},{2,6},{4,0},{6,2},{8,12},{10,14},{12,8},{14,10},{16,20},{18,... | collective-permute-start | bytes 245768 | tf_op jit(solution)/shard_map/ppermute | solution.py:142
  15.0 6.9 %copy-start.1 = (f32[8,64,128]{2,1,0:T(8,128)S(1)}, f32[8,64,128]{2,1,0:T(8,128)}, u32[]{:S(2)}) copy-start(f32[8,64,128]{2,1,0:T(8,128)} %refs_10_.1) | copy-start | bytes 786436
  15.0 5.6 %collective-permute-start.4 = (f32[5,32,128]{2,1,0:T(8,128)S(1)}, f32[5,32,128]{2,1,0:T(8,128)S(1)}, u32[]{:S(2)}, u32[]{:S(2)}) collective-permute-start(f32[5,32,128]{2,1,0:T(8,128)S(1)} %get-tuple-element.41.refs_0_), channel_id=1, source_target_pairs={{0,16},{2,18},{4,20},{6,22},{8,24},{10,26},{12,28},{14,30},{16,0},... | collective-permute-start | bytes 245768 | tf_op jit(solution)/shard_map/ppermute | solution.py:142
  20.7 1.3 %collective-permute-start.5 = (f32[2,32,128]{2,1,0:T(8,128)S(1)}, f32[2,32,128]{2,1,0:T(8,128)S(1)}, u32[]{:S(2)}, u32[]{:S(2)}) collective-permute-start(f32[2,32,128]{2,1,0:T(8,128)S(1)} %get-tuple-element.45), channel_id=1, source_target_pairs={{0,2},{2,0},{4,6},{6,4},{8,10},{10,8},{12,14},{14,12},{16,18},{18,... | collective-permute-start | bytes 98312 | tf_op jit(solution)/shard_map/ppermute | solution.py:616
  21.9 4.3 %copy-start.6 = (s32[1024]{0:T(1024)S(1)}, s32[1024]{0:T(1024)}, u32[]{:S(2)}) copy-start(s32[1024]{0:T(1024)} %param.20) | copy-start | bytes 12292
  21.9 4.3 %copy-start.7 = (f32[1024]{0:T(1024)S(1)}, f32[1024]{0:T(1024)}, u32[]{:S(2)}) copy-start(f32[1024]{0:T(1024)} %param.21) | copy-start | bytes 12292
  22.4 3.8 %collective-permute-start.6 = (f32[5,8,128]{2,1,0:T(8,128)S(1)}, f32[5,8,128]{2,1,0:T(8,128)S(1)}, u32[]{:S(2)}, u32[]{:S(2)}) collective-permute-start(f32[5,8,128]{2,1,0:T(8,128)S(1)} %get-tuple-element.48.refs_0_), channel_id=1, source_target_pairs={{0,1},{1,0},{2,3},{3,2},{4,5},{5,4},{6,7},{7,6},{8,9},{9,8},{10,11... | collective-permute-start | bytes 61448 | tf_op jit(solution)/shard_map/ppermute | solution.py:142
  26.2 0.7 %copy-start.5 = (s32[1024]{0:T(1024)S(1)}, s32[1024]{0:T(1024)}, u32[]{:S(2)}) copy-start(s32[1024]{0:T(1024)} %param.19) | copy-start | bytes 12292
  26.2 0.7 %copy-start.4 = (s32[1024]{0:T(1024)S(1)}, s32[1024]{0:T(1024)}, u32[]{:S(2)}) copy-start(s32[1024]{0:T(1024)} %param.18) | copy-start | bytes 12292
  34.6 3.7 %collective-permute-start.7 = (f32[3,8,128]{2,1,0:T(8,128)S(1)}, f32[3,8,128]{2,1,0:T(8,128)S(1)}, u32[]{:S(2)}, u32[]{:S(2)}) collective-permute-start(f32[3,8,128]{2,1,0:T(8,128)S(1)} %get-tuple-element.52.refs_0_), channel_id=1, source_target_pairs={{0,1},{1,0},{2,3},{3,2},{4,5},{5,4},{6,7},{7,6},{8,9},{9,8},{10,11... | collective-permute-start | bytes 36872 | tf_op jit(solution)/shard_map/ppermute | solution.py:142
  38.8 1.3 %collective-permute-start.8 = (f32[72,128]{1,0:T(8,128)S(1)}, f32[72,128]{1,0:T(8,128)S(1)}, u32[]{:S(2)}, u32[]{:S(2)}) collective-permute-start(f32[72,128]{1,0:T(8,128)S(1)} %get-tuple-element.60), channel_id=1, source_target_pairs={{0,2},{2,0},{4,6},{6,4},{8,10},{10,8},{12,14},{14,12},{16,18},{18,... | collective-permute-start | bytes 110600 | tf_op jit(solution)/shard_map/ppermute | solution.py:647
  40.1 4.9 %collective-permute-start.11 = (f32[72,128]{1,0:T(8,128)S(1)}, f32[72,128]{1,0:T(8,128)S(1)}, u32[]{:S(2)}, u32[]{:S(2)}) collective-permute-start(f32[72,128]{1,0:T(8,128)S(1)} %get-tuple-element.61.refs_0_), channel_id=1, source_target_pairs={{0,12},{2,14},{4,8},{6,10},{8,4},{10,6},{12,0},{14,2},{16,28},{18,... | collective-permute-start | bytes 110600 | tf_op jit(solution)/shard_map/ppermute | solution.py:142
  42.7 4.0 %collective-permute-start.10 = (f32[72,128]{1,0:T(8,128)S(1)}, f32[72,128]{1,0:T(8,128)S(1)}, u32[]{:S(2)}, u32[]{:S(2)}) collective-permute-start(f32[72,128]{1,0:T(8,128)S(1)} %get-tuple-element.61.refs_0_), channel_id=1, source_target_pairs={{0,8},{2,10},{4,12},{6,14},{8,0},{10,2},{12,4},{14,6},{16,24},{18,... | collective-permute-start | bytes 110600 | tf_op jit(solution)/shard_map/ppermute | solution.py:142
  44.3 4.0 %collective-permute-start.9 = (f32[72,128]{1,0:T(8,128)S(1)}, f32[72,128]{1,0:T(8,128)S(1)}, u32[]{:S(2)}, u32[]{:S(2)}) collective-permute-start(f32[72,128]{1,0:T(8,128)S(1)} %get-tuple-element.61.refs_0_), channel_id=1, source_target_pairs={{0,4},{2,6},{4,0},{6,2},{8,12},{10,14},{12,8},{14,10},{16,20},{18,... | collective-permute-start | bytes 110600 | tf_op jit(solution)/shard_map/ppermute | solution.py:142
  48.3 4.9 %collective-permute-start.12 = (f32[72,128]{1,0:T(8,128)S(1)}, f32[72,128]{1,0:T(8,128)S(1)}, u32[]{:S(2)}, u32[]{:S(2)}) collective-permute-start(f32[72,128]{1,0:T(8,128)S(1)} %get-tuple-element.62.refs_0_), channel_id=1, source_target_pairs={{0,16},{2,18},{4,20},{6,22},{8,24},{10,26},{12,28},{14,30},{16,0},... | collective-permute-start | bytes 110600 | tf_op jit(solution)/shard_map/ppermute | solution.py:142
  53.8 1.2 %collective-permute-start.13 = (f32[2,32,128]{2,1,0:T(8,128)S(1)}, f32[2,32,128]{2,1,0:T(8,128)S(1)}, u32[]{:S(2)}, u32[]{:S(2)}) collective-permute-start(f32[2,32,128]{2,1,0:T(8,128)S(1)} %get-tuple-element.67), channel_id=1, source_target_pairs={{0,2},{2,0},{4,6},{6,4},{8,10},{10,8},{12,14},{14,12},{16,18},{18,... | collective-permute-start | bytes 98312 | tf_op jit(solution)/shard_map/ppermute | solution.py:666
where the time goes:
time: 56.2 us; the launch traced here: 55.9 us
  waiting for transfers between devices  23.2 us (41%)
  starting transfers between devices  17 us (30%)
  Pallas kernels  10.7 us (19%)
  local copies, waits for them, and re-layouts  4.23 us (8%)
  between operations  0.76 us (1%)
    ppermute x10, waiting for transfers between devices, exchange(): lax.ppermute(value, axis, [(i, i ^ turn * stride) for i in range(size)])  18.7 us
    ppermute x10, starting transfers between devices, exchange(): lax.ppermute(value, axis, [(i, i ^ turn * stride) for i in range(size)])  16.4 us
    pallas_call x11, Pallas kernels, run(): pl.pallas_call(body, out_shape=shapes, in_specs=[pl.BlockSpec(memory_spac...  10.7 us
    ppermute x4, waiting for transfers between devices, shards(): lax.ppermute(send, 'gx', swap)  4.52 us
    unnamed x24, local copies, waits for them, and re-layouts  4.23 us
  transfers between devices with their start and end apart: 14, of which 14 were waited for; matrix products, arithmetic and copies ran while one was open for 0% of the time, Pallas kernels for 0%

commit v1 on v0

v1 whole, which is shorter than its diff:
```python
import jax
import jax.numpy as jnp
from jax import lax
from jax.experimental import pallas as pl
from jax.experimental.pallas import tpu as pltpu
from jax.sharding import PartitionSpec as P


f32 = jnp.float32
misfit_weight = 100.0
lanes = 128
chunk = 8
field = 10
mask = (1 << field) - 1


def harmonic(left_cond, right_cond):
    return 2.0 * left_cond * right_cond / (left_cond + right_cond)


def eliminate(entry, links, grounds, loads):
    near_ground = near_load = far_ground = far_load = None
    steps = []
    for link, ground, load in zip(links, grounds, loads):
        if far_ground is not None:
            ground, load = ground + far_ground, load + far_load
        inverse = 1.0 / (entry + link + ground)
        to_near, to_far = entry * inverse, link * inverse
        far_ground, far_load = to_far * ground, to_far * load
        if near_ground is None:
            near_ground, near_load = to_near * ground, to_near * load
        else:
            near_ground, near_load = near_ground + to_near * ground, near_load + to_near * load
        steps.append((inverse, to_near, to_far, inverse * load))
        entry = to_near * link
    return (entry, near_ground, far_ground, near_load, far_load), steps


def eliminate_loads(factors, loads):
    near_load = far_load = None
    scaled = []
    for (inverse, to_near, to_far), load in zip(factors, loads):
        if far_load is not None:
            load = load + far_load
        far_load = to_far * load
        near_load = to_near * load if near_load is None else near_load + to_near * load
        scaled.append(inverse * load)
    return near_load, far_load, scaled


def expand(steps, near, far):
    values = []
    for _, to_near, to_far, scaled in reversed(steps):
        far = scaled + to_near * near + to_far * far
        values.append(far)
    return values[::-1]


def combine(blocks):
    pairs = list(zip(blocks[:-1], blocks[1:]))
    (entry, near_ground, far_ground, near_load, far_load), steps = eliminate(
        blocks[0][0],
        [after[0] for _, after in pairs],
        [before[2] + after[1] for before, after in pairs],
        [before[4] + after[3] for before, after in pairs],
    )
    joined = (
        entry,
        blocks[0][1] + near_ground,
        blocks[-1][2] + far_ground,
        blocks[0][3] + near_load,
        blocks[-1][4] + far_load,
    )
    return joined, steps


def combine_loads(blocks, factors):
    near_load, far_load, scaled = eliminate_loads(
        factors, [before[1] + after[0] for before, after in zip(blocks[:-1], blocks[1:])]
    )
    return (blocks[0][0] + near_load, blocks[-1][1] + far_load), scaled


def with_scaled(factors, scaled):
    return [factor + (value,) for factor, value in zip(factors, scaled)]


def factors_of(ref):
    return [(ref[i, 0], ref[i, 1], ref[i, 2]) for i in range(ref.shape[0])]


def steps_of(ref):
    return [(None, ref[i, 1], ref[i, 2], ref[i, 3]) for i in range(ref.shape[0])]


def keep_steps(ref, steps):
    for i, step in enumerate(steps):
        for j, value in enumerate(step):
            ref[i, j] = value


def face_gradient(left_cond, right_cond, adjoint_drop, head_drop):
    total = 1.0 / (left_cond + right_cond)
    flow = -(adjoint_drop * head_drop) * (2.0 * left_cond * right_cond * total) * total
    return flow * right_cond, flow * left_cond


def bf16_parts(values, count):
    parts = []
    for _ in range(count):
        part = values.astype(jnp.bfloat16)
        parts.append(part)
        values = values - part.astype(jnp.float32)
    return parts


def run(body, outs, ins, scratch=(), raw=0, after=(), flops=1000000, limit=24):
    shapes = [
        jax.ShapeDtypeStruct(*((out, f32) if isinstance(out[0], int) else out)) for out in outs
    ]
    size = 4 * (sum(x.size for x in ins) + sum(x.size for x in shapes))
    places = [pltpu.HBM] * raw + [pltpu.VMEM] * (len(ins) - raw) + [pl.ANY] * len(after)
    count = len(ins)

    def ordered(*refs):
        return body(*refs[:count], *refs[count + len(after):])

    return pl.pallas_call(
        ordered,
        out_shape=shapes,
        in_specs=[pl.BlockSpec(memory_space=place) for place in places],
        out_specs=[pl.BlockSpec(memory_space=pltpu.VMEM)] * len(outs),
        scratch_shapes=[
            item if not isinstance(item, tuple) else pltpu.VMEM(*item) for item in scratch
        ],
        compiler_params=pltpu.CompilerParams(vmem_limit_bytes=int(limit * 1024 * 1024)),
        cost_estimate=pl.CostEstimate(flops=flops, bytes_accessed=size, transcendentals=0),
    )(*ins, *after)


def spot_in(stride, count):
    return lax.rem(lax.axis_index("gx") // stride, count)


def place(scratch, arrivals, stride):
    position = spot_in(stride, len(arrivals))
    for turn, arrival in enumerate(arrivals):
        scratch[position ^ turn] = arrival[...]


def exchange(value, axis, stride, count):
    size = lax.axis_size(axis)
    return [value] + [
        lax.ppermute(value, axis, [(i, i ^ (turn * stride)) for i in range(size)])
        for turn in range(1, count)
    ]


def swap(value):
    return lax.ppermute(value, "gx", [(i, i ^ 1) for i in range(lax.axis_size("gx"))])


def own_edges(scratch, position, near, faces, far):
    for i, value in enumerate([near] + faces + [far]):
        scratch[i] = value
    return scratch[position], scratch[position + 1]


def x_ends(cond):
    me, count = lax.axis_index("gx"), lax.axis_size("gx")
    depth = cond.shape[0]
    near = jnp.where(me == 0, 0.0, 2.0) * cond[0]
    far = jnp.where(me == count - 1, 0.0, 2.0) * cond[depth - 1]
    return near, far


def x_eliminate(cond, storage, loads):
    cells = cond.shape[0]
    near, far = x_ends(cond)
    links = [harmonic(cond[i], cond[i + 1]) for i in range(cells - 1)] + [far]
    return eliminate(
        near, links, [storage[i] for i in range(cells)], [loads[i] for i in range(cells)]
    )


def x_factor(cond, storage, loads, steps_ref):
    keep_steps(steps_ref, x_eliminate(cond, storage, loads)[1])


def x_load(log_cond_in, storage_in, head_in, cond, storage, loads, log_cond, head, done):
    moves = [
        pltpu.make_async_copy(source, target, done.at[i])
        for i, (source, target) in enumerate(
            ((log_cond_in, log_cond), (storage_in, storage), (head_in, head))
        )
    ]
    for move in moves:
        move.start()
    moves[0].wait()
    cond[...] = jnp.exp(log_cond[...])
    moves[1].wait()
    moves[2].wait()
    loads[...] = storage[...] * head[...]


def x_reduce(cond, storage, stored, places, rates, loads, own, send, five):
    cells, rows, _ = cond.shape
    me, group = lax.axis_index("gx"), lax.axis_index("yz")
    wells = rates.shape[1]
    local_east = lax.shift_right_logical(places[...], 2 * field) - me * cells
    local_north = (lax.shift_right_logical(places[...], field) & mask) - group * rows
    depth = places[...] & mask
    inside = (
        (local_east >= 0) & (local_east < cells) & (local_north >= 0) & (local_north < rows)
    )
    spot = jnp.where(inside, local_east * rows + local_north, -1)
    at_row = jnp.where(
        lax.broadcasted_iota(jnp.int32, (cells * rows, wells), 0) == spot, 1.0, 0.0
    ).astype(jnp.bfloat16)
    at_depth = lax.broadcasted_iota(jnp.int32, (lanes, wells), 0) == depth
    sources = sum(
        lax.dot_general(
            at_row, part, (((1,), (1,)), ((), ())), preferred_element_type=f32
        )
        for part in bf16_parts(jnp.where(at_depth, rates[...], 0.0), 3)
    ).reshape(cells, rows, lanes)
    for i in range(cells):
        loads[i] = stored[i] + sources[i]
    block, _ = x_eliminate(cond, storage, loads)
    for i, value in enumerate(block):
        five[i] = value
    half = rows // 2
    mine = lax.rem(me, 2)
    own[...] = five[:, pl.ds(pl.multiple_of(mine * half, half), half), :]
    send[...] = five[:, pl.ds(pl.multiple_of((1 - mine) * half, half), half), :]


def make_join(stride, count):
    def join(*refs):
        arrivals, (joined_ref, steps_ref, scratch) = refs[:count], refs[count:]
        place(scratch, arrivals, stride)
        joined, steps = combine([[scratch[i, j] for j in range(5)] for i in range(count)])
        for i, value in enumerate(joined):
            joined_ref[i] = value
        keep_steps(steps_ref, steps)

    return join


def descend(levels, edges, scratch):
    for stride, steps in levels[:-1]:
        faces = expand(steps, *edges)
        edges = own_edges(scratch, spot_in(stride, len(steps) + 1), edges[0], faces, edges[1])
    return edges[0], expand(levels[-1][1], *edges)[0], edges[1]


def hand_back(near, middle, far, own, send):
    first = spot_in(1, 2) == 0
    own[0] = jnp.where(first, near, middle)
    own[1] = jnp.where(first, middle, far)
    send[0] = jnp.where(first, middle, near)
    send[1] = jnp.where(first, far, middle)


def make_top(strides, counts):
    below = len(strides) - 1

    def top(*refs):
        arrivals = refs[:counts[-1]]
        lower, (own, send, steps_ref, scratch, edges) = (
            refs[counts[-1]:counts[-1] + below], refs[counts[-1] + below:]
        )
        place(scratch, arrivals, strides[-1])
        nothing = jnp.zeros(own.shape[1:], f32)
        _, steps = combine([[scratch[i, j] for j in range(5)] for i in range(counts[-1])])
        keep_steps(steps_ref, steps)
        levels = [(strides[-1], steps)] + [
            (strides[i], steps_of(lower[i])) for i in reversed(range(below))
        ]
        hand_back(*descend(levels, (nothing, nothing), edges), own, send)

    return top


def both_halves(own, other, scratch):
    half = own.shape[1]
    mine = lax.rem(lax.axis_index("gx"), 2)
    scratch[:, pl.ds(pl.multiple_of(mine * half, half), half), :] = own[...]
    scratch[:, pl.ds(pl.multiple_of((1 - mine) * half, half), half), :] = other[...]


def y_cells(ref, spot):
    chunks = ref.shape[1] // chunk
    return ref[:, pl.ds(spot, chunks, stride=chunk), :]


def y_links(cond):
    me, count = lax.axis_index("yz"), lax.axis_size("yz")
    cells = [y_cells(cond, spot) for spot in range(chunk)]
    place_of = lax.broadcasted_iota(jnp.int32, cells[0].shape, 1)
    chunks = cells[0].shape[1]
    near = jnp.where((place_of == 0) & (me == 0), 0.0, 2.0 * cells[0])
    far = jnp.where((place_of == chunks - 1) & (me == count - 1), 0.0, 2.0 * cells[-1])
    return cells, near, far


def by_chunk(value, scratch):
    slab, chunks, _ = value.shape
    scratch[...] = value.reshape(slab * chunks, lanes)
    return [scratch[pl.ds(i, slab, stride=chunks), :] for i in range(chunks)]


def from_chunk(values, scratch):
    slab, chunks = values[0].shape[0], len(values)
    for i, value in enumerate(values):
        scratch[pl.ds(i, slab, stride=chunks), :] = value
    return scratch[...].reshape(slab, chunks, lanes)


def y_factor(cond, storage, cell_factors, chunk_factors, ends, turned):
    conds, near, far = y_links(cond)
    links = [harmonic(conds[i], conds[i + 1]) for i in range(chunk - 1)] + [far]
    nothing = [jnp.zeros_like(near)] * chunk
    block, steps = eliminate(near, links, [y_cells(storage, i) for i in range(chunk)], nothing)
    keep_steps(cell_factors, [step[:3] for step in steps])
    parts = [by_chunk(value, turned.at[i]) for i, value in enumerate(block[:3])]
    nothing = [jnp.zeros_like(parts[0][0])] * len(parts[0])
    joined, steps = combine(list(zip(*parts, nothing, nothing)))
    keep_steps(chunk_factors, [step[:3] for step in steps])
    for i in range(3):
        ends[i] = joined[i]


def z_links(cond):
    lane = lax.broadcasted_iota(jnp.int32, cond.shape, 1)
    after = pltpu.roll(cond, lanes - 1, 1)
    return lane == lanes - 1, after


def piece_of(ref, i, cuts):
    per = ref.shape[0] // cuts
    return ref[i * per:(i + 1) * per].reshape(per * ref.shape[1], lanes)


def make_z_factor(cuts, first, last, total):
    def z_factor(*refs):
        if first == 0:
            cond, storage, from_back, from_ahead, links, grounds = refs
            for i in range(cuts):
                here = piece_of(cond, i, cuts)
                ending, after = z_links(here)
                links[i] = jnp.where(ending, 0.0, harmonic(here, after))
                grounds[i] = piece_of(storage, i, cuts)
            links_in, grounds_in = links, grounds
        else:
            links_in, grounds_in, from_back, from_ahead, links, grounds = refs
        for level in range(first, last):
            shift = 1 << level
            for i in range(cuts):
                link, ground = links_in[i], grounds_in[i]
                link_back = pltpu.roll(link, shift, 1)
                inverse = 1.0 / (link + link_back + ground)
                passed = inverse * link
                from_back[level - first, i] = pltpu.roll(passed, shift, 1)
                from_ahead[level - first, i] = link * pltpu.roll(inverse, lanes - shift, 1)
                held = inverse * ground
                grounds[i] = (
                    ground
                    + link * pltpu.roll(held, lanes - shift, 1)
                    + link_back * pltpu.roll(held, shift, 1)
                )
                links[i] = link * pltpu.roll(passed, lanes - shift, 1)
            links_in, grounds_in = links, grounds
        if last == total:
            for i in range(cuts):
                grounds[i] = 1.0 / grounds[i]

    return z_factor


def make_points(slab, rows):
    def points(east, north, depth, at_row, at_depth, here):
        local_east = east[...] - lax.axis_index("gx") * slab
        local_north = north[...] - lax.axis_index("yz") * rows
        inside = (
            (local_east >= 0) & (local_east < slab) & (local_north >= 0) & (local_north < rows)
        )
        spot = jnp.where(inside, local_east * rows + local_north, -1)
        at_row[...] = jnp.where(
            lax.broadcasted_iota(jnp.int32, at_row.shape, 0) == spot, 1.0, 0.0
        ).astype(jnp.bfloat16)
        at_depth[...] = jnp.where(
            lax.broadcasted_iota(jnp.int32, at_depth.shape, 0) == depth[...], 1.0, 0.0
        )
        here[...] = jnp.where(inside, 1.0, 0.0)

    return points


def y_forward(own, other, x_steps, storage, cell_factors, chunk_factors, ends,
              head_first, x_edges, scaled_cells, scaled_chunks, message, loads, turned):
    cells = head_first.shape[0]
    both_halves(own, other, x_edges)
    near, far = x_edges[0], x_edges[1]
    for i in reversed(range(cells)):
        far = x_steps[i, 3] + x_steps[i, 1] * near + x_steps[i, 2] * far
        head_first[i] = far
        loads[i] = storage[i] * far
    for i in range(3):
        message[i] = ends[i]
    y_loads(loads, cell_factors, chunk_factors, scaled_cells, scaled_chunks, turned, message.at[3:5])


def y_loads(loads, cell_factors, chunk_factors, scaled_cells, scaled_chunks, turned, message):
    near, far, scaled = eliminate_loads(
        factors_of(cell_factors), [y_cells(loads, i) for i in range(chunk)]
    )
    for i, value in enumerate(scaled):
        scaled_cells[i] = value
    blocks = list(zip(by_chunk(near, turned.at[0]), by_chunk(far, turned.at[1])))
    joined, scaled = combine_loads(blocks, factors_of(chunk_factors))
    for i, value in enumerate(scaled):
        scaled_chunks[i] = value
    message[0] = joined[0]
    message[1] = joined[1]


def y_expand(near, far, cell_factors, chunk_factors, scaled_cells, scaled_chunks,
             turned, solved, edges, natural):
    factors = factors_of(chunk_factors)
    steps = with_scaled(factors, [scaled_chunks[i] for i in range(len(factors))])
    faces = [near] + expand(steps, near, far) + [far]
    near = from_chunk(faces[:-1], turned.at[0])
    far = from_chunk(faces[1:], turned.at[1])
    edges[0] = near
    edges[1] = far
    for spot in reversed(range(chunk)):
        far = scaled_cells[spot] + cell_factors[spot, 1] * near + cell_factors[spot, 2] * far
        solved[spot] = far
        natural[:, pl.ds(spot, natural.shape[1] // chunk, stride=chunk), :] = far


def z_sweep(loads, parts):
    level = 0
    for from_back, from_ahead in parts:
        for part in range(from_back.shape[0]):
            shift = 1 << level
            level = level + 1
            for i in range(from_back.shape[1]):
                load = loads[i]
                loads[i] = (
                    load
                    + from_ahead[part, i] * pltpu.roll(load, lanes - shift, 1)
                    + from_back[part, i] * pltpu.roll(load, shift, 1)
                )


def make_z(count, cuts, split):
    def z_solve(*refs):
        arrivals, tables = refs[:count], refs[count:count + 2 * split]
        sweeps = [(tables[2 * i], tables[2 * i + 1]) for i in range(split)]
        (cell_factors, chunk_factors, scaled_cells, scaled_chunks, storage,
         inverse, at_row, at_depth, here, observed,
         y_factors, head_second, y_edges, head_third, adjoint_third, message,
         next_cells, next_chunks,
         scratch, edges, turned, loads, second, third) = refs[count + 2 * split:]
        me = lax.axis_index("yz")
        for turn, arrival in enumerate(arrivals):
            scratch[me ^ turn] = arrival[...]
        nothing = jnp.zeros(arrivals[0].shape[1:], f32)
        _, steps = combine([[scratch[i, j] for j in range(5)] for i in range(count)])
        keep_steps(y_factors, [step[:3] for step in steps])
        near, far = own_edges(edges, me, nothing, expand(steps, nothing, nothing), nothing)
        y_expand(near, far, cell_factors, chunk_factors, scaled_cells, scaled_chunks,
                 turned, head_second, y_edges, second)

        slab, rows, _ = storage.shape
        per = slab // cuts
        piece = per * rows
        for i in range(cuts):
            loads[i] = piece_of(storage, i, cuts) * piece_of(second, i, cuts)
        z_sweep(loads, sweeps)
        for i in range(cuts):
            head = loads[i] * inverse[i]
            head_third[i * per:(i + 1) * per] = head.reshape(per, rows, lanes)
            for j, part in enumerate(bf16_parts(head, 2)):
                third[pl.ds(i * piece, piece), j * lanes:(j + 1) * lanes] = part
        found = lax.dot_general(
            third[...], at_row[...], (((0,), (0,)), ((), ())), preferred_element_type=f32
        )
        found = jnp.sum(
            at_depth[...] * (found[:lanes] + found[lanes:]), axis=0, keepdims=True
        )
        misfit = here[...] * (found - observed[...])
        for i in range(misfit.shape[1] // lanes):
            message[2, i:i + 1, :] = misfit[:, i * lanes:(i + 1) * lanes]
        parts = [
            (at_depth[...] * part.astype(f32)).astype(jnp.bfloat16)
            for part in bf16_parts(misfit_weight * misfit, 2)
        ]
        source = lax.dot_general(
            at_row[...], jnp.concatenate(parts, axis=0),
            (((1,), (1,)), ((), ())), preferred_element_type=f32,
        )
        for i in range(cuts):
            part = source[i * piece:(i + 1) * piece]
            loads[i] = part[:, :lanes] + part[:, lanes:]
        z_sweep(loads, sweeps)
        for i in range(cuts):
            adjoint = (loads[i] * inverse[i]).reshape(per, rows, lanes)
            adjoint_third[i * per:(i + 1) * per] = adjoint
            second[i * per:(i + 1) * per] = storage[i * per:(i + 1) * per] * adjoint
        y_loads(second, cell_factors, chunk_factors, next_cells, next_chunks, turned,
                message.at[0:2])

    return z_solve


def make_y_back(count):
    def y_back(*refs):
        arrivals = refs[:count]
        (y_factors, cell_factors, chunk_factors, scaled_cells, scaled_chunks, storage, x_steps,
         adjoint_second, y_edges, scaled_x, own, send, scratch, edges, turned, second, pair
         ) = refs[count:]
        me = lax.axis_index("yz")
        misfit = arrivals[0][2]
        for turn, arrival in enumerate(arrivals):
            scratch[me ^ turn] = arrival[:2]
            if turn:
                misfit = misfit + arrival[2]
        nothing = jnp.zeros(arrivals[0].shape[1:], f32)
        factors = factors_of(y_factors)
        _, scaled = combine_loads([[scratch[i, 0], scratch[i, 1]] for i in range(count)], factors)
        faces = expand(with_scaled(factors, scaled), nothing, nothing)
        near, far = own_edges(edges, me, nothing, faces, nothing)
        y_expand(near, far, cell_factors, chunk_factors, scaled_cells, scaled_chunks,
                 turned, adjoint_second, y_edges, second)
        near, far, scaled = eliminate_loads(
            factors_of(x_steps), [storage[i] * second[i] for i in range(second.shape[0])]
        )
        for i, value in enumerate(scaled):
            scaled_x[i] = value
        pair[0] = near
        pair[1] = far
        half = pair.shape[1] // 2
        mine = lax.rem(lax.axis_index("gx"), 2)
        for ref, side in ((own, mine), (send, 1 - mine)):
            for i in range(2):
                ref[i * half:(i + 1) * half] = pair[i, pl.ds(pl.multiple_of(side * half, half), half), :]
            ref[2 * half:] = misfit

    return y_back


def make_terms(cuts):
    def gather_terms(cond, head_third, adjoint_third, head_second, adjoint_second,
                     head_edges, adjoint_edges, terms, natural):
        conds, near_link, far_link = y_links(cond)
        from_left = (
            -near_link * (adjoint_second[0] - adjoint_edges[0]) * (head_second[0] - head_edges[0])
        )
        for spot in range(chunk):
            if spot < chunk - 1:
                to_left, to_right = face_gradient(
                    conds[spot], conds[spot + 1],
                    adjoint_second[spot] - adjoint_second[spot + 1],
                    head_second[spot] - head_second[spot + 1],
                )
            else:
                to_left = (
                    -far_link * (adjoint_second[spot] - adjoint_edges[1])
                    * (head_second[spot] - head_edges[1])
                )
            natural[:, pl.ds(spot, natural.shape[1] // chunk, stride=chunk), :] = from_left + to_left
            from_left = to_right
        slab, rows, _ = cond.shape
        per = slab // cuts
        for i in range(cuts):
            here, head, adjoint = [
                piece_of(ref, i, cuts) for ref in (cond, head_third, adjoint_third)
            ]
            last, after = z_links(here)
            to_left, to_right = face_gradient(
                here, after,
                adjoint - pltpu.roll(adjoint, lanes - 1, 1),
                head - pltpu.roll(head, lanes - 1, 1),
            )
            to_left = jnp.where(last, 0.0, to_left)
            to_right = jnp.where(last, 0.0, to_right)
            value = (to_left + pltpu.roll(to_right, 1, 1)).reshape(per, rows, lanes)
            terms[i * per:(i + 1) * per] = value + natural[i * per:(i + 1) * per]

    return gather_terms


def loads_in(arrivals, scratch, stride):
    rows, count = scratch.shape[2], len(arrivals)
    misfit = None
    for turn, arrival in enumerate(arrivals):
        position = spot_in(stride, count) ^ turn
        scratch[position, 0] = arrival[:rows]
        scratch[position, 1] = arrival[rows:2 * rows]
        part = arrival[2 * rows:]
        misfit = part if misfit is None else misfit + part
    return [[scratch[i, 0], scratch[i, 1]] for i in range(count)], misfit


def make_join_loads(stride, count):
    def join(*refs):
        arrivals, (steps_ref, message, scaled_ref, scratch) = refs[:count], refs[count:]
        blocks, misfit = loads_in(arrivals, scratch, stride)
        joined, scaled = combine_loads(blocks, factors_of(steps_ref))
        rows = scratch.shape[2]
        message[:rows] = joined[0]
        message[rows:2 * rows] = joined[1]
        message[2 * rows:] = misfit
        for i, value in enumerate(scaled):
            scaled_ref[i] = value

    return join


def make_top_loads(strides, counts):
    below = len(strides) - 1

    def top(*refs):
        arrivals, refs = refs[:counts[-1]], refs[counts[-1]:]
        top_steps, lower, lower_scaled = refs[0], refs[1:1 + below], refs[1 + below:1 + 2 * below]
        own, send, misfit_ref, scratch, edges = refs[1 + 2 * below:]
        blocks, misfit = loads_in(arrivals, scratch, strides[-1])
        nothing = jnp.zeros(scratch.shape[2:], f32)
        factors = factors_of(top_steps)
        levels = [(strides[-1], with_scaled(factors, combine_loads(blocks, factors)[1]))]
        for i in reversed(range(below)):
            factors = factors_of(lower[i])
            scaled = [lower_scaled[i][j] for j in range(len(factors))]
            levels.append((strides[i], with_scaled(factors, scaled)))
        misfit_ref[...] = misfit
        hand_back(*descend(levels, (nothing, nothing), edges), own, send)

    return top


def x_back(own, other, x_steps, scaled_x, cond, head, x_edges, terms, gradient, edges):
    cells = cond.shape[0]
    both_halves(own, other, edges)
    near_link, far_link = x_ends(cond)
    adjoint = [None] * cells
    after = edges[1]
    for i in reversed(range(cells)):
        after = scaled_x[i] + x_steps[i, 1] * edges[0] + x_steps[i, 2] * after
        adjoint[i] = after
    from_left = -near_link * (adjoint[0] - edges[0]) * (head[0] - x_edges[0])
    for i in range(cells):
        if i < cells - 1:
            to_left, to_right = face_gradient(
                cond[i], cond[i + 1], adjoint[i] - adjoint[i + 1], head[i] - head[i + 1]
            )
            gradient[i] = terms[i] + from_left + to_left
            from_left = to_right
        else:
            gradient[i] = (
                terms[i] + from_left - far_link * (adjoint[i] - edges[1]) * (head[i] - x_edges[1])
            )


def shards(log_cond, storage, head, well_east, well_north, well_depth, pump_rates,
           probe_east, probe_north, probe_depth, probe_heads):
    slab, rows, _ = log_cond.shape
    devices, columns = lax.axis_size("gx"), lax.axis_size("yz")
    inner = 4 if devices >= 16 else 2
    strides, counts = [1, 2, 2 * inner], [2, inner, devices // (2 * inner)]
    half = rows // 2
    chunks = rows // chunk
    points = probe_heads.shape[0]
    grid = (slab, rows, lanes)
    plane = (half, lanes)
    cell = (chunk, slab, chunks, lanes)
    line = (slab, lanes)

    places = ((well_east << (2 * field)) + (well_north << field) + well_depth).reshape(1, -1)
    probes = [value.reshape(1, -1) for value in (probe_east, probe_north, probe_depth, probe_heads)]
    cond, storage, stored = run(
        x_load,
        [grid, grid, grid],
        [log_cond, storage, head],
        [(grid, f32), (grid, f32), pltpu.SemaphoreType.DMA((3,))],
        raw=3,
        limit=53,
    )
    loads, own, send = run(
        x_reduce,
        [grid, (5,) + plane, (5,) + plane],
        [cond, storage, stored, places, pump_rates.reshape(1, -1)],
        [((5, rows, lanes), f32)],
    )
    (x_steps,) = run(x_factor, [(slab, 4, rows, lanes)], [cond, storage, loads], after=[send])
    cell_factors, chunk_factors, ends = run(
        y_factor,
        [(chunk, 3) + cell[1:], (chunks - 1, 3) + line, (3,) + line],
        [cond, storage],
        [((3, slab * chunks, lanes), f32)],
        after=[send],
    )
    joined, steps = run(
        make_join(1, 2),
        [(5,) + plane, (1, 4) + plane],
        [own, swap(send)],
        [((2, 5) + plane, f32)],
        after=[x_steps, ends],
    )
    x_levels = [steps]

    cuts = 4
    piece = (cuts, slab * rows // cuts, lanes)
    levels = lanes.bit_length() - 1
    bounds = [0, 4, levels]
    split = len(bounds) - 1
    carried, z_parts, waits = [cond, storage], [], []
    for i, (stride, count) in enumerate(zip(strides[1:], counts[1:])):
        arrivals = exchange(joined, "gx", stride, count)
        waits = []
        if i < split:
            first, last = bounds[i:i + 2]
            from_back, from_ahead, *carried = run(
                make_z_factor(cuts, first, last, levels),
                [(last - first,) + piece] * 2 + [piece] * 2,
                carried,
                after=[joined],
            )
            z_parts += [from_back, from_ahead]
            waits = [carried[1]]
        if i == split - 1:
            at_row, at_depth, here = run(
                make_points(slab, rows),
                [((slab * rows, points), jnp.bfloat16), (lanes, points), (1, points)],
                probes[:3],
                after=[joined],
            )
            waits.append(here)
        if i < len(strides) - 2:
            joined, steps = run(
                make_join(stride, count),
                [(5,) + plane, (count - 1, 4) + plane],
                arrivals,
                [((count, 5) + plane, f32)],
                after=waits,
            )
            x_levels.append(steps)
    own, send, steps = run(
        make_top(strides, counts),
        [(2,) + plane, (2,) + plane, (counts[-1] - 1, 4) + plane],
        arrivals + x_levels,
        [((counts[-1], 5) + plane, f32), ((max(counts) + 1,) + plane, f32)],
        after=waits,
    )
    x_levels.append(steps)
    inverse = carried[1]
    head_first, x_edges, scaled_cells, scaled_chunks, message = run(
        y_forward,
        [grid, (2, rows, lanes), cell, (chunks - 1,) + line, (5,) + line],
        [own, swap(send), x_steps, storage, cell_factors, chunk_factors, ends],
        [(grid, f32), ((2, slab * chunks, lanes), f32)],
    )
    (y_factors, head_second, head_edges, head_third, adjoint_third, message,
     scaled_cells, scaled_chunks) = run(
        make_z(columns, cuts, split),
        [(columns - 1, 3) + line, cell, (2,) + cell[1:], grid, grid,
         (3,) + line, cell, (chunks - 1,) + line],
        exchange(message, "yz", 1, columns)
        + z_parts
        + [cell_factors, chunk_factors, scaled_cells, scaled_chunks, storage,
           inverse, at_row, at_depth, here, probes[3]],
        [((columns, 5) + line, f32), ((columns + 1,) + line, f32), ((2, slab * chunks, lanes), f32),
         (piece, f32), (grid, f32), ((slab * rows, 2 * lanes), jnp.bfloat16)],
    )
    extra = points // lanes
    note = (2 * half + extra, lanes)
    adjoint_second, adjoint_edges, scaled_x, own, send = run(
        make_y_back(columns),
        [cell, (2,) + cell[1:], grid, note, note],
        exchange(message, "yz", 1, columns)
        + [y_factors, cell_factors, chunk_factors, scaled_cells, scaled_chunks, storage, x_steps],
        [((columns, 2) + line, f32), ((columns + 1,) + line, f32), ((2, slab * chunks, lanes), f32),
         (grid, f32), ((2, rows, lanes), f32)],
    )
    (terms,) = run(
        make_terms(cuts),
        [grid],
        [cond, head_third, adjoint_third, head_second, adjoint_second, head_edges, adjoint_edges],
        [(grid, f32)],
    )
    arrivals, x_scaled = [own, swap(send)], []
    for i, (stride, count) in enumerate(zip(strides[:-1], counts[:-1])):
        message, scaled = run(
            make_join_loads(stride, count),
            [note, (count - 1,) + plane],
            arrivals + [x_levels[i]],
            [((count, 2) + plane, f32)],
        )
        x_scaled.append(scaled)
        arrivals = exchange(message, "gx", strides[i + 1], counts[i + 1])
    own, send, misfits = run(
        make_top_loads(strides, counts),
        [(2,) + plane, (2,) + plane, (extra, lanes)],
        arrivals + x_levels[-1:] + x_levels[:-1] + x_scaled,
        [((counts[-1], 2) + plane, f32), ((max(counts) + 1,) + plane, f32)],
    )
    (gradient,) = run(
        x_back,
        [grid],
        [own, swap(send), x_steps, scaled_x, cond, head_first, x_edges, terms],
        [((2, rows, lanes), f32)],
    )
    return head_third, gradient, misfits.reshape(-1)


def solution(mesh):
    cells = P("gx", "yz", None)
    return jax.shard_map(
        shards,
        mesh=mesh,
        in_specs=(cells, cells, cells) + (P(),) * 8,
        out_specs=(cells, cells, P()),
        check_vma=False,
    )
```

time: 56.2 us -> 50.7 us (0.902)
  waiting for transfers between devices: 23.2 us -> 16.5 us
  Pallas kernels: 10.7 us -> 13.9 us
  local copies, waits for them, and re-layouts: 4.23 us -> 2.03 us
  other arithmetic: 0 us -> 0.69 us
    ppermute x10, waiting for transfers between devices: 18.7 us -> 13 us  [exchange(): lax.ppermute(value, axis, [(i, i ^ turn * stride) for i in range(size)])]
    pallas_call x11 -> x18, Pallas kernels: 10.7 us -> 13.9 us  [run(): pl.pallas_call(ordered, out_shape=shapes, in_specs=[pl.BlockSpec(memory_s...]
    unnamed x24 -> x12, local copies, waits for them, and re-layouts: 4.23 us -> 2.03 us
    ppermute x4, waiting for transfers between devices: 4.52 us -> 3.51 us  [swap(): lax.ppermute(value, 'gx', [(i, i ^ 1) for i in range(lax.axis_size('gx'))])]
    reshape x0 -> x1, other arithmetic: none -> 0.69 us  [shards(): ((well_east << 2 * field) + (well_north << field) + well_depth).reshape(1...]
  transfers between devices with their start and end apart: 14 -> 14, of which waited for: 14 -> 12; matrix products, arithmetic and copies ran while one was open for 0% -> 0% of each run, Pallas kernels for 0% -> 13%
where the time goes in v1:
time: 50.7 us; the launch traced here: 50.4 us
  starting transfers between devices  16.5 us (33%)
  waiting for transfers between devices  16.5 us (33%)
  Pallas kernels  13.9 us (27%)
  local copies, waits for them, and re-layouts  2.03 us (4%)
  between operations  0.78 us (2%)
  other arithmetic  0.69 us (1%)
    ppermute x10, starting transfers between devices, exchange(): lax.ppermute(value, axis, [(i, i ^ turn * stride) for i in range(size)])  15.8 us
    pallas_call x18, Pallas kernels, run(): pl.pallas_call(ordered, out_shape=shapes, in_specs=[pl.BlockSpec(memory_s...  13.9 us
    ppermute x10, waiting for transfers between devices, exchange(): lax.ppermute(value, axis, [(i, i ^ turn * stride) for i in range(size)])  13 us
    ppermute x4, waiting for transfers between devices, swap(): lax.ppermute(value, 'gx', [(i, i ^ 1) for i in range(lax.axis_size('gx'))])  3.51 us
    unnamed x12, local copies, waits for them, and re-layouts  2.03 us
  transfers between devices with their start and end apart: 14, of which 12 were waited for; matrix products, arithmetic and copies ran while one was open for 0% of the time, Pallas kernels for 13%

profile of v1, /device:TPU:0, one launch (start us, length us, event | category | flops | bytes accessed | tf_op | source)
XLA Modules:
  0.0 50.4 jit_solution(6006575258840476125)
XLA Ops:
  0.6 0.7 %add_bitcast_fusion.refs_3_ = s32[1,32]{1,0:T(1,128)S(1)} fusion(s32[32]{0:T(128)} %param.16, s32[32]{0:T(128)} %param.15, s32[32]{0:T(128)} %param.14), kind=kLoop, calls=%fused_computation | loop fusion | flops 128 | bytes 512 | tf_op jit(solution)/shard_map/reshape | solution.py:681
  1.3 1.2 %shard_map.130 = (f32[8,64,128]{2,1,0:T(8,128)S(1)}, f32[8,64,128]{2,1,0:T(8,128)S(1)}, f32[8,64,128]{2,1,0:T(8,128)S(1)}) custom-call(f32[8,64,128]{2,1,0:T(8,128)} %refs_0_.1, f32[8,64,128]{2,1,0:T(8,128)} %refs_1_.1, f32[8,64,128]{2,1,0:T(8,128)} %refs_2_.1), custom_call_target="tpu_custom_call" | custom-call | flops 1000000 | bytes 1572864 | tf_op jit(solution)/shard_map/pallas_call | solution.py:128
  2.5 0.6 %copy-done.5 = f32[32]{0:T(128)S(1)} copy-done((f32[32]{0:T(128)S(1)}, f32[32]{0:T(128)}, u32[]{:S(2)}) %copy-start.5) | copy-done | bytes 152
  3.2 0.3 shard_map.131
  3.5 0.5 %collective-permute-start = (f32[5,32,128]{2,1,0:T(8,128)S(1)}, f32[5,32,128]{2,1,0:T(8,128)S(1)}, u32[]{:S(2)}, u32[]{:S(2)}) collective-permute-start(f32[5,32,128]{2,1,0:T(8,128)S(1)} %get-tuple-element.58.refs_3_.refs_2_), channel_id=1, source_target_pairs={{0,2},{2,0},{4,6},{6,4},{8,10},{10,8},{12,14},{14,12},{16,18},{18,... | collective-permute-start | bytes 245768 | tf_op jit(solution)/shard_map/ppermute | solution.py:160
  4.5 0.5 collective-permute-done.refs_1_
  5.0 3.9 %collective-permute-start.3 = (f32[5,32,128]{2,1,0:T(8,128)S(1)}, f32[5,32,128]{2,1,0:T(8,128)S(1)}, u32[]{:S(2)}, u32[]{:S(2)}) collective-permute-start(f32[5,32,128]{2,1,0:T(8,128)S(1)} %get-tuple-element.61.refs_2_.refs_0_), channel_id=1, source_target_pairs={{0,12},{2,14},{4,8},{6,10},{8,4},{10,6},{12,0},{14,2},{16,28},{18,... | collective-permute-start | bytes 245768 | tf_op jit(solution)/shard_map/ppermute | solution.py:154
  8.9 0.4 collective-permute-start.2
  9.6 2.7 %shard_map.135 = (f32[4,4,128,128]{3,2,1,0:T(8,128)S(1)}, f32[4,4,128,128]{3,2,1,0:T(8,128)S(1)}, f32[4,128,128]{2,1,0:T(8,128)S(1)}, f32[4,128,128]{2,1,0:T(8,128)S(1)}) custom-call(f32[8,64,128]{2,1,0:T(8,128)S(1)} %get-tuple-element.54.refs_0_.refs_4_, f32[8,64,128]{2,1,0:T(8,128)S(1)} %get-tuple-element.55.refs_1_.refs_3_.refs_10_.refs_7_, ...), custom_call_target="tpu_custom_call" | custom-call | flops 1000000 | bytes 3145728 | tf_op jit(solution)/shard_map/pallas_call | solution.py:128
  12.3 1.3 %collective-permute-done.2.refs_2_ = f32[5,32,128]{2,1,0:T(8,128)S(1)} collective-permute-done((f32[5,32,128]{2,1,0:T(8,128)S(1)}, f32[5,32,128]{2,1,0:T(8,128)S(1)}, u32[]{:S(2)}, u32[]{:S(2)}) %collective-permute-start.2) | collective-permute-done | bytes 81952 | tf_op jit(solution)/shard_map/ppermute | solution.py:154
  13.9 2.7 %collective-permute-start.4 = (f32[5,32,128]{2,1,0:T(8,128)S(1)}, f32[5,32,128]{2,1,0:T(8,128)S(1)}, u32[]{:S(2)}, u32[]{:S(2)}) collective-permute-start(f32[5,32,128]{2,1,0:T(8,128)S(1)} %get-tuple-element.63.refs_2_.refs_3_.refs_0_), channel_id=1, source_target_pairs={{0,16},{2,18},{4,20},{6,22},{8,24},{10,26},{12,28},{14,30},{16,0},... | collective-permute-start | bytes 245768 | tf_op jit(solution)/shard_map/ppermute | solution.py:154
  16.6 2.5 %shard_map.137 = (f32[3,4,128,128]{3,2,1,0:T(8,128)S(1)}, f32[3,4,128,128]{3,2,1,0:T(8,128)S(1)}, f32[4,128,128]{2,1,0:T(8,128)}, f32[4,128,128]{2,1,0:T(8,128)S(1)}) custom-call(f32[4,128,128]{2,1,0:T(8,128)S(1)} %get-tuple-element.66.refs_0_, f32[4,128,128]{2,1,0:T(8,128)S(1)} %get-tuple-element.62.refs_4_.refs_1_, ...), custom_call_target="tpu_custom_call" | custom-call | flops 1000000 | bytes 2621440 | tf_op jit(solution)/shard_map/pallas_call | solution.py:128
  19.1 0.7 %copy-done.1 = s32[1024]{0:T(1024)S(1)} copy-done((s32[1024]{0:T(1024)S(1)}, s32[1024]{0:T(1024)}, u32[]{:S(2)}) %copy-start.1) | copy-done | bytes 4120
  20.2 1.2 %collective-permute-done.5.refs_1_ = f32[2,32,128]{2,1,0:T(8,128)S(1)} collective-permute-done((f32[2,32,128]{2,1,0:T(8,128)S(1)}, f32[2,32,128]{2,1,0:T(8,128)S(1)}, u32[]{:S(2)}, u32[]{:S(2)}) %collective-permute-start.5) | collective-permute-done | bytes 32800 | tf_op jit(solution)/shard_map/ppermute | solution.py:160
  21.5 1.6 %collective-permute-start.6 = (f32[5,8,128]{2,1,0:T(8,128)S(1)}, f32[5,8,128]{2,1,0:T(8,128)S(1)}, u32[]{:S(2)}, u32[]{:S(2)}) collective-permute-start(f32[5,8,128]{2,1,0:T(8,128)S(1)} %get-tuple-element.73.refs_0_), channel_id=1, source_target_pairs={{0,1},{1,0},{2,3},{3,2},{4,5},{5,4},{6,7},{7,6},{8,9},{9,8},{10,11... | collective-permute-start | bytes 61448 | tf_op jit(solution)/shard_map/ppermute | solution.py:154
  23.1 2.3 %collective-permute-done.6.refs_1_ = f32[5,8,128]{2,1,0:T(8,128)S(1)} collective-permute-done((f32[5,8,128]{2,1,0:T(8,128)S(1)}, f32[5,8,128]{2,1,0:T(8,128)S(1)}, u32[]{:S(2)}, u32[]{:S(2)}) %collective-permute-start.6) | collective-permute-done | bytes 20512 | tf_op jit(solution)/shard_map/ppermute | solution.py:154
  25.4 0.7 %copy-done.4 = f32[1024]{0:T(1024)S(1)} copy-done((f32[1024]{0:T(1024)S(1)}, f32[1024]{0:T(1024)}, u32[]{:S(2)}) %copy-start.4) | copy-done | bytes 4120
  26.1 3.7 %shard_map.141 = (f32[1,3,8,128]{3,2,1,0:T(8,128)S(1)}, f32[8,8,8,128]{3,2,1,0:T(8,128)S(1)}, f32[2,8,8,128]{3,2,1,0:T(8,128)S(1)}, f32[8,64,128]{2,1,0:T(8,128)...) custom-call(f32[5,8,128]{2,1,0:T(8,128)S(1)} %get-tuple-element.73.r, ...), custom_call_target="tpu_custom_call" | custom-call | flops 1000000 | bytes 9195520 | tf_op jit(solution)/shard_map/pallas_call | solution.py:128
  29.8 1.5 %collective-permute-start.7 = (f32[3,8,128]{2,1,0:T(8,128)S(1)}, f32[3,8,128]{2,1,0:T(8,128)S(1)}, u32[]{:S(2)}, u32[]{:S(2)}) collective-permute-start(f32[3,8,128]{2,1,0:T(8,128)S(1)} %get-tuple-element.83.refs_0_), channel_id=1, source_target_pairs={{0,1},{1,0},{2,3},{3,2},{4,5},{5,4},{6,7},{7,6},{8,9},{9,8},{10,11... | collective-permute-start | bytes 36872 | tf_op jit(solution)/shard_map/ppermute | solution.py:154
  31.3 2.2 %collective-permute-done.7.refs_1_ = f32[3,8,128]{2,1,0:T(8,128)S(1)} collective-permute-done((f32[3,8,128]{2,1,0:T(8,128)S(1)}, f32[3,8,128]{2,1,0:T(8,128)S(1)}, u32[]{:S(2)}, u32[]{:S(2)}) %collective-permute-start.7) | collective-permute-done | bytes 12320 | tf_op jit(solution)/shard_map/ppermute | solution.py:154
  33.8 1.2 %collective-permute-done.8.refs_1_ = f32[72,128]{1,0:T(8,128)S(1)} collective-permute-done((f32[72,128]{1,0:T(8,128)S(1)}, f32[72,128]{1,0:T(8,128)S(1)}, u32[]{:S(2)}, u32[]{:S(2)}) %collective-permute-start.8) | collective-permute-done | bytes 36896 | tf_op jit(solution)/shard_map/ppermute | solution.py:160
  35.1 2.3 %collective-permute-start.11 = (f32[72,128]{1,0:T(8,128)S(1)}, f32[72,128]{1,0:T(8,128)S(1)}, u32[]{:S(2)}, u32[]{:S(2)}) collective-permute-start(f32[72,128]{1,0:T(8,128)S(1)} %get-tuple-element.89.refs_0_), channel_id=1, source_target_pairs={{0,12},{2,14},{4,8},{6,10},{8,4},{10,6},{12,0},{14,2},{16,28},{18,... | collective-permute-start | bytes 110600 | tf_op jit(solution)/shard_map/ppermute | solution.py:154
  37.4 1.3 %collective-permute-start.10 = (f32[72,128]{1,0:T(8,128)S(1)}, f32[72,128]{1,0:T(8,128)S(1)}, u32[]{:S(2)}, u32[]{:S(2)}) collective-permute-start(f32[72,128]{1,0:T(8,128)S(1)} %get-tuple-element.89.refs_0_), channel_id=1, source_target_pairs={{0,8},{2,10},{4,12},{6,14},{8,0},{10,2},{12,4},{14,6},{16,24},{18,... | collective-permute-start | bytes 110600 | tf_op jit(solution)/shard_map/ppermute | solution.py:154
  38.7 1.2 %collective-permute-done.11.refs_3_ = f32[72,128]{1,0:T(8,128)S(1)} collective-permute-done((f32[72,128]{1,0:T(8,128)S(1)}, f32[72,128]{1,0:T(8,128)S(1)}, u32[]{:S(2)}, u32[]{:S(2)}) %collective-permute-start.11) | collective-permute-done | bytes 36896 | tf_op jit(solution)/shard_map/ppermute | solution.py:154
  40.0 1.4 %collective-permute-done.10.refs_2_ = f32[72,128]{1,0:T(8,128)S(1)} collective-permute-done((f32[72,128]{1,0:T(8,128)S(1)}, f32[72,128]{1,0:T(8,128)S(1)}, u32[]{:S(2)}, u32[]{:S(2)}) %collective-permute-start.10) | collective-permute-done | bytes 36896 | tf_op jit(solution)/shard_map/ppermute | solution.py:154
  41.4 1.3 %collective-permute-done.9.refs_1_ = f32[72,128]{1,0:T(8,128)S(1)} collective-permute-done((f32[72,128]{1,0:T(8,128)S(1)}, f32[72,128]{1,0:T(8,128)S(1)}, u32[]{:S(2)}, u32[]{:S(2)}) %collective-permute-start.9) | collective-permute-done | bytes 36896 | tf_op jit(solution)/shard_map/ppermute | solution.py:154
  42.8 1.9 %collective-permute-start.12 = (f32[72,128]{1,0:T(8,128)S(1)}, f32[72,128]{1,0:T(8,128)S(1)}, u32[]{:S(2)}, u32[]{:S(2)}) collective-permute-start(f32[72,128]{1,0:T(8,128)S(1)} %get-tuple-element.90.refs_0_), channel_id=1, source_target_pairs={{0,16},{2,18},{4,20},{6,22},{8,24},{10,26},{12,28},{14,30},{16,0},... | collective-permute-start | bytes 110600 | tf_op jit(solution)/shard_map/ppermute | solution.py:154
  44.6 3.1 %collective-permute-done.12.refs_1_ = f32[72,128]{1,0:T(8,128)S(1)} collective-permute-done((f32[72,128]{1,0:T(8,128)S(1)}, f32[72,128]{1,0:T(8,128)S(1)}, u32[]{:S(2)}, u32[]{:S(2)}) %collective-permute-start.12) | collective-permute-done | bytes 36896 | tf_op jit(solution)/shard_map/ppermute | solution.py:154
  47.7 0.6 %shard_map.145 = (f32[2,32,128]{2,1,0:T(8,128)S(1)}, f32[2,32,128]{2,1,0:T(8,128)S(1)}, f32[8,128]{1,0:T(8,128)}) custom-call(f32[72,128]{1,0:T(8,128)S(1)} %get-tuple-element.90.refs_0_, f32[72,128]{1,0:T(8,128)S(1)} %collective-permute-done.12.refs_1_, f32[1,4,32,128]{3,2,1,0:T(8,128)S(1)} %get-tuple-element.91.refs_2_, ...), custom_call_target="tpu_custom_call" | custom-call | flops 1000000 | bytes 536576 | tf_op jit(solution)/shard_map/pallas_call | solution.py:128
  48.3 0.6 %shard_map.146.refs_7_ = f32[8,64,128]{2,1,0:T(8,128)S(1)} custom-call(f32[8,64,128]{2,1,0:T(8,128)S(1)} %get-tuple-element.54.refs_0_.refs_4_, f32[8,64,128]{2,1,0:T(8,128)S(1)} %copy-done, f32[8,64,128]{2,1,0:T(8,128)S(1)} %get-tuple-element.99.refs_2_, f32[8,8,8,128]{3,2,1,0:T(8,128)S(1)} %get-tuple-element.100.refs_3_, ...), custom_call_target="tpu_custom_call" | custom-call | flops 1000000 | bytes 1703936 | tf_op jit(solution)/shard_map/pallas_call | solution.py:128
  48.9 0.6 %collective-permute-done.13.refs_1_ = f32[2,32,128]{2,1,0:T(8,128)S(1)} collective-permute-done((f32[2,32,128]{2,1,0:T(8,128)S(1)}, f32[2,32,128]{2,1,0:T(8,128)S(1)}, u32[]{:S(2)}, u32[]{:S(2)}) %collective-permute-start.13) | collective-permute-done | bytes 32800 | tf_op jit(solution)/shard_map/ppermute | solution.py:160
  49.5 0.9 %shard_map.147 = f32[8,64,128]{2,1,0:T(8,128)} custom-call(f32[2,32,128]{2,1,0:T(8,128)S(1)} %get-tuple-element.94.refs_0_, f32[2,32,128]{2,1,0:T(8,128)S(1)} %collective-permute-done.13.refs_1_, f32[8,4,64,128]{3,2,1,0:T(8,128)S(1)} %shard_map.132.refs_2_.refs_8_, f32[8,64,128]{2,1,0:T(8,128)S(1)} %get-tuple-element.96.refs_3_, ...), custom_call_target="tpu_custom_call" | custom-call | flops 1000000 | bytes 2490368 | tf_op jit(solution)/shard_map/pallas_call | solution.py:128
  (27 shorter events, 1.9 us)
Async XLA Ops:
  2.5 0.7 %copy-start.5 = (f32[32]{0:T(128)S(1)}, f32[32]{0:T(128)}, u32[]{:S(2)}) copy-start(f32[32]{0:T(128)} %param.17) | copy-start | bytes 388
  3.5 1.4 %collective-permute-start = (f32[5,32,128]{2,1,0:T(8,128)S(1)}, f32[5,32,128]{2,1,0:T(8,128)S(1)}, u32[]{:S(2)}, u32[]{:S(2)}) collective-permute-start(f32[5,32,128]{2,1,0:T(8,128)S(1)} %get-tuple-element.58.refs_3_.refs_2_), channel_id=1, source_target_pairs={{0,2},{2,0},{4,6},{6,4},{8,10},{10,8},{12,14},{14,12},{16,18},{18,... | collective-permute-start | bytes 245768 | tf_op jit(solution)/shard_map/ppermute | solution.py:160
  5.0 7.3 %collective-permute-start.3 = (f32[5,32,128]{2,1,0:T(8,128)S(1)}, f32[5,32,128]{2,1,0:T(8,128)S(1)}, u32[]{:S(2)}, u32[]{:S(2)}) collective-permute-start(f32[5,32,128]{2,1,0:T(8,128)S(1)} %get-tuple-element.61.refs_2_.refs_0_), channel_id=1, source_target_pairs={{0,12},{2,14},{4,8},{6,10},{8,4},{10,6},{12,0},{14,2},{16,28},{18,... | collective-permute-start | bytes 245768 | tf_op jit(solution)/shard_map/ppermute | solution.py:154
  8.9 4.7 %collective-permute-start.2 = (f32[5,32,128]{2,1,0:T(8,128)S(1)}, f32[5,32,128]{2,1,0:T(8,128)S(1)}, u32[]{:S(2)}, u32[]{:S(2)}) collective-permute-start(f32[5,32,128]{2,1,0:T(8,128)S(1)} %get-tuple-element.61.refs_2_.refs_0_), channel_id=1, source_target_pairs={{0,8},{2,10},{4,12},{6,14},{8,0},{10,2},{12,4},{14,6},{16,24},{18,... | collective-permute-start | bytes 245768 | tf_op jit(solution)/shard_map/ppermute | solution.py:154
  9.4 4.4 %collective-permute-start.1 = (f32[5,32,128]{2,1,0:T(8,128)S(1)}, f32[5,32,128]{2,1,0:T(8,128)S(1)}, u32[]{:S(2)}, u32[]{:S(2)}) collective-permute-start(f32[5,32,128]{2,1,0:T(8,128)S(1)} %get-tuple-element.61.refs_2_.refs_0_), channel_id=1, source_target_pairs={{0,4},{2,6},{4,0},{6,2},{8,12},{10,14},{12,8},{14,10},{16,20},{18,... | collective-permute-start | bytes 245768 | tf_op jit(solution)/shard_map/ppermute | solution.py:154
  13.9 6.1 %collective-permute-start.4 = (f32[5,32,128]{2,1,0:T(8,128)S(1)}, f32[5,32,128]{2,1,0:T(8,128)S(1)}, u32[]{:S(2)}, u32[]{:S(2)}) collective-permute-start(f32[5,32,128]{2,1,0:T(8,128)S(1)} %get-tuple-element.63.refs_2_.refs_3_.refs_0_), channel_id=1, source_target_pairs={{0,16},{2,18},{4,20},{6,22},{8,24},{10,26},{12,28},{14,30},{16,0},... | collective-permute-start | bytes 245768 | tf_op jit(solution)/shard_map/ppermute | solution.py:154
  16.6 2.5 %copy-start.2 = (s32[1024]{0:T(1024)S(1)}, s32[1024]{0:T(1024)}, u32[]{:S(2)}) copy-start(s32[1024]{0:T(1024)} %param.19) | copy-start | bytes 12292
  16.6 2.5 %copy-start.3 = (s32[1024]{0:T(1024)S(1)}, s32[1024]{0:T(1024)}, u32[]{:S(2)}) copy-start(s32[1024]{0:T(1024)} %param.20) | copy-start | bytes 12292
  19.1 0.7 %copy-start.1 = (s32[1024]{0:T(1024)S(1)}, s32[1024]{0:T(1024)}, u32[]{:S(2)}) copy-start(s32[1024]{0:T(1024)} %param.18) | copy-start | bytes 12292
  20.1 1.3 %collective-permute-start.5 = (f32[2,32,128]{2,1,0:T(8,128)S(1)}, f32[2,32,128]{2,1,0:T(8,128)S(1)}, u32[]{:S(2)}, u32[]{:S(2)}) collective-permute-start(f32[2,32,128]{2,1,0:T(8,128)S(1)} %get-tuple-element.70), channel_id=1, source_target_pairs={{0,2},{2,0},{4,6},{6,4},{8,10},{10,8},{12,14},{14,12},{16,18},{18,... | collective-permute-start | bytes 98312 | tf_op jit(solution)/shard_map/ppermute | solution.py:160
  21.5 3.8 %collective-permute-start.6 = (f32[5,8,128]{2,1,0:T(8,128)S(1)}, f32[5,8,128]{2,1,0:T(8,128)S(1)}, u32[]{:S(2)}, u32[]{:S(2)}) collective-permute-start(f32[5,8,128]{2,1,0:T(8,128)S(1)} %get-tuple-element.73.refs_0_), channel_id=1, source_target_pairs={{0,1},{1,0},{2,3},{3,2},{4,5},{5,4},{6,7},{7,6},{8,9},{9,8},{10,11... | collective-permute-start | bytes 61448 | tf_op jit(solution)/shard_map/ppermute | solution.py:154
  25.4 0.7 %copy-start.4 = (f32[1024]{0:T(1024)S(1)}, f32[1024]{0:T(1024)}, u32[]{:S(2)}) copy-start(f32[1024]{0:T(1024)} %param.21) | copy-start | bytes 12292
  29.8 3.7 %collective-permute-start.7 = (f32[3,8,128]{2,1,0:T(8,128)S(1)}, f32[3,8,128]{2,1,0:T(8,128)S(1)}, u32[]{:S(2)}, u32[]{:S(2)}) collective-permute-start(f32[3,8,128]{2,1,0:T(8,128)S(1)} %get-tuple-element.83.refs_0_), channel_id=1, source_target_pairs={{0,1},{1,0},{2,3},{3,2},{4,5},{5,4},{6,7},{7,6},{8,9},{9,8},{10,11... | collective-permute-start | bytes 36872 | tf_op jit(solution)/shard_map/ppermute | solution.py:154
  33.8 1.3 %collective-permute-start.8 = (f32[72,128]{1,0:T(8,128)S(1)}, f32[72,128]{1,0:T(8,128)S(1)}, u32[]{:S(2)}, u32[]{:S(2)}) collective-permute-start(f32[72,128]{1,0:T(8,128)S(1)} %get-tuple-element.88), channel_id=1, source_target_pairs={{0,2},{2,0},{4,6},{6,4},{8,10},{10,8},{12,14},{14,12},{16,18},{18,... | collective-permute-start | bytes 110600 | tf_op jit(solution)/shard_map/ppermute | solution.py:160
  35.1 4.9 %collective-permute-start.11 = (f32[72,128]{1,0:T(8,128)S(1)}, f32[72,128]{1,0:T(8,128)S(1)}, u32[]{:S(2)}, u32[]{:S(2)}) collective-permute-start(f32[72,128]{1,0:T(8,128)S(1)} %get-tuple-element.89.refs_0_), channel_id=1, source_target_pairs={{0,12},{2,14},{4,8},{6,10},{8,4},{10,6},{12,0},{14,2},{16,28},{18,... | collective-permute-start | bytes 110600 | tf_op jit(solution)/shard_map/ppermute | solution.py:154
  37.4 4.0 %collective-permute-start.10 = (f32[72,128]{1,0:T(8,128)S(1)}, f32[72,128]{1,0:T(8,128)S(1)}, u32[]{:S(2)}, u32[]{:S(2)}) collective-permute-start(f32[72,128]{1,0:T(8,128)S(1)} %get-tuple-element.89.refs_0_), channel_id=1, source_target_pairs={{0,8},{2,10},{4,12},{6,14},{8,0},{10,2},{12,4},{14,6},{16,24},{18,... | collective-permute-start | bytes 110600 | tf_op jit(solution)/shard_map/ppermute | solution.py:154
  38.7 4.0 %collective-permute-start.9 = (f32[72,128]{1,0:T(8,128)S(1)}, f32[72,128]{1,0:T(8,128)S(1)}, u32[]{:S(2)}, u32[]{:S(2)}) collective-permute-start(f32[72,128]{1,0:T(8,128)S(1)} %get-tuple-element.89.refs_0_), channel_id=1, source_target_pairs={{0,4},{2,6},{4,0},{6,2},{8,12},{10,14},{12,8},{14,10},{16,20},{18,... | collective-permute-start | bytes 110600 | tf_op jit(solution)/shard_map/ppermute | solution.py:154
  42.7 5.6 %copy-start = (f32[8,64,128]{2,1,0:T(8,128)S(1)}, f32[8,64,128]{2,1,0:T(8,128)}, u32[]{:S(2)}) copy-start(f32[8,64,128]{2,1,0:T(8,128)} %get-tuple-element.51.refs_1_) | copy-start | bytes 786436
  42.8 4.9 %collective-permute-start.12 = (f32[72,128]{1,0:T(8,128)S(1)}, f32[72,128]{1,0:T(8,128)S(1)}, u32[]{:S(2)}, u32[]{:S(2)}) collective-permute-start(f32[72,128]{1,0:T(8,128)S(1)} %get-tuple-element.90.refs_0_), channel_id=1, source_target_pairs={{0,16},{2,18},{4,20},{6,22},{8,24},{10,26},{12,28},{14,30},{16,0},... | collective-permute-start | bytes 110600 | tf_op jit(solution)/shard_map/ppermute | solution.py:154
  48.3 1.2 %collective-permute-start.13 = (f32[2,32,128]{2,1,0:T(8,128)S(1)}, f32[2,32,128]{2,1,0:T(8,128)S(1)}, u32[]{:S(2)}, u32[]{:S(2)}) collective-permute-start(f32[2,32,128]{2,1,0:T(8,128)S(1)} %get-tuple-element.95), channel_id=1, source_target_pairs={{0,2},{2,0},{4,6},{6,4},{8,10},{10,8},{12,14},{14,12},{16,18},{18,... | collective-permute-start | bytes 98312 | tf_op jit(solution)/shard_map/ppermute | solution.py:160

commit v2 on v1

--- a/solution.py
+++ b/solution.py
@@ -9,7 +9,7 @@
 f32 = jnp.float32
 misfit_weight = 100.0
 lanes = 128
-chunk = 8
+chunks = 8
 field = 10
 mask = (1 << field) - 1
 
@@ -148,16 +148,49 @@
         scratch[position ^ turn] = arrival[...]
 
 
-def exchange(value, axis, stride, count):
-    size = lax.axis_size(axis)
+def exchange(value, stride, count):
+    size = lax.axis_size("gx")
     return [value] + [
-        lax.ppermute(value, axis, [(i, i ^ (turn * stride)) for i in range(size)])
+        lax.ppermute(value, "gx", [(i, i ^ (turn * stride)) for i in range(size)])
         for turn in range(1, count)
     ]
 
 
 def swap(value):
-    return lax.ppermute(value, "gx", [(i, i ^ 1) for i in range(lax.axis_size("gx"))])
+    return exchange(value, 1, 2)[1]
+
+
+def exchange_rows(value):
+    size, columns = lax.axis_size("gx"), lax.axis_size("yz")
+    return [value] + [
+        lax.ppermute(
+            value,
+            ("gx", "yz"),
+            [
+                (i * columns + j, (i ^ (turn % 2)) * columns + (j ^ (turn // 2)))
+                for i in range(size)
+                for j in range(columns)
+            ],
+        )
+        for turn in range(1, 2 * columns)
+    ]
+
+
+def side():
+    return lax.rem(lax.axis_index("gx"), 2)
+
+
+def row_block():
+    return lax.axis_index("yz") * 2 + side()
+
+
+def local_spot(east, north, slab, rows):
+    local_east = east - lax.axis_index("gx") // 2 * slab
+    local_north = north - row_block() * rows
+    inside = (
+        (local_east >= 0) & (local_east < slab) & (local_north >= 0) & (local_north < rows)
+    )
+    return inside, jnp.where(inside, local_east * rows + local_north, -1)
 
 
 def own_edges(scratch, position, near, faces, far):
@@ -166,73 +199,87 @@
     return scratch[position], scratch[position + 1]
 
 
+def pair_cells(ref, i):
+    cells = ref.shape[0] // 2
+    return jnp.stack([ref[i], ref[cells + i]])
+
+
 def x_ends(cond):
-    me, count = lax.axis_index("gx"), lax.axis_size("gx")
-    depth = cond.shape[0]
-    near = jnp.where(me == 0, 0.0, 2.0) * cond[0]
-    far = jnp.where(me == count - 1, 0.0, 2.0) * cond[depth - 1]
-    return near, far
-
-
-def x_eliminate(cond, storage, loads):
+    pair, count = lax.axis_index("gx") // 2, lax.axis_size("gx") // 2
     cells = cond.shape[0]
-    near, far = x_ends(cond)
-    links = [harmonic(cond[i], cond[i + 1]) for i in range(cells - 1)] + [far]
-    return eliminate(
-        near, links, [storage[i] for i in range(cells)], [loads[i] for i in range(cells)]
-    )
-
-
-def x_factor(cond, storage, loads, steps_ref):
-    keep_steps(steps_ref, x_eliminate(cond, storage, loads)[1])
-
-
-def x_load(log_cond_in, storage_in, head_in, cond, storage, loads, log_cond, head, done):
-    moves = [
-        pltpu.make_async_copy(source, target, done.at[i])
-        for i, (source, target) in enumerate(
-            ((log_cond_in, log_cond), (storage_in, storage), (head_in, head))
-        )
-    ]
+    near = [jnp.where(pair == 0, 0.0, 2.0) * cond[0], 2.0 * cond[cells // 2]]
+    far = [2.0 * cond[cells // 2 - 1], jnp.where(pair == count - 1, 0.0, 2.0) * cond[cells - 1]]
+    return jnp.stack(near), jnp.stack(far)
+
+
+def x_load(log_cond, storage, head, *refs):
+    targets, done = refs[:6], refs[6]
+    half = targets[0].shape[1]
+    moves = []
+    for part, some in ((1 - side(), targets[3:]), (side(), targets[:3])):
+        rows = pl.ds(pl.multiple_of(part * half, half), half)
+        for source, target in zip((log_cond, storage, head), some):
+            moves.append(
+                pltpu.make_async_copy(source.at[:, rows, :], target, done.at[len(moves)])
+            )
     for move in moves:
         move.start()
-    moves[0].wait()
-    cond[...] = jnp.exp(log_cond[...])
-    moves[1].wait()
-    moves[2].wait()
-    loads[...] = storage[...] * head[...]
-
-
-def x_reduce(cond, storage, stored, places, rates, loads, own, send, five):
-    cells, rows, _ = cond.shape
-    me, group = lax.axis_index("gx"), lax.axis_index("yz")
-    wells = rates.shape[1]
-    local_east = lax.shift_right_logical(places[...], 2 * field) - me * cells
-    local_north = (lax.shift_right_logical(places[...], field) & mask) - group * rows
-    depth = places[...] & mask
-    inside = (
-        (local_east >= 0) & (local_east < cells) & (local_north >= 0) & (local_north < rows)
-    )
-    spot = jnp.where(inside, local_east * rows + local_north, -1)
-    at_row = jnp.where(
-        lax.broadcasted_iota(jnp.int32, (cells * rows, wells), 0) == spot, 1.0, 0.0
-    ).astype(jnp.bfloat16)
-    at_depth = lax.broadcasted_iota(jnp.int32, (lanes, wells), 0) == depth
-    sources = sum(
-        lax.dot_general(
-            at_row, part, (((1,), (1,)), ((), ())), preferred_element_type=f32
-        )
-        for part in bf16_parts(jnp.where(at_depth, rates[...], 0.0), 3)
-    ).reshape(cells, rows, lanes)
-    for i in range(cells):
-        loads[i] = stored[i] + sources[i]
-    block, _ = x_eliminate(cond, storage, loads)
-    for i, value in enumerate(block):
-        five[i] = value
-    half = rows // 2
-    mine = lax.rem(me, 2)
-    own[...] = five[:, pl.ds(pl.multiple_of(mine * half, half), half), :]
-    send[...] = five[:, pl.ds(pl.multiple_of((1 - mine) * half, half), half), :]
+    for move in moves:
+        move.wait()
+
+
+def make_wells(slab, rows):
+    def wells(places, rates, sources):
+        _, spot = local_spot(
+            lax.shift_right_logical(places[...], 2 * field),
+            lax.shift_right_logical(places[...], field) & mask,
+            slab,
+            rows,
+        )
+        count = rates.shape[1]
+        at_row = jnp.where(
+            lax.broadcasted_iota(jnp.int32, (slab * rows, count), 0) == spot, 1.0, 0.0
+        ).astype(jnp.bfloat16)
+        at_depth = (
+            lax.broadcasted_iota(jnp.int32, (lanes, count), 0) == (places[...] & mask)
+        )
+        sources[...] = sum(
+            lax.dot_general(
+                at_row, part, (((1,), (1,)), ((), ())), preferred_element_type=f32
+            )
+            for part in bf16_parts(jnp.where(at_depth, rates[...], 0.0), 3)
+        ).reshape(slab, rows, lanes)
+
+    return wells
+
+
+def x_reduce(*refs):
+    parts, (sources, cond, storage, steps_ref, pair_steps, block_ref, raw, loads) = (
+        refs[:6], refs[6:]
+    )
+    cells = cond.shape[0] // 2
+    for i in range(3):
+        raw[side(), i] = parts[i][...]
+        raw[1 - side(), i] = parts[3 + i][...]
+    for i in range(2):
+        part = slice(i * cells, (i + 1) * cells)
+        cond[part] = jnp.exp(raw[i, 0])
+        storage[part] = raw[i, 1]
+        loads[part] = raw[i, 1] * raw[i, 2] + sources[part]
+    near, far = x_ends(cond)
+    conds = [pair_cells(cond, i) for i in range(cells)]
+    links = [harmonic(conds[i], conds[i + 1]) for i in range(cells - 1)] + [far]
+    block, steps = eliminate(
+        near,
+        links,
+        [pair_cells(storage, i) for i in range(cells)],
+        [pair_cells(loads, i) for i in range(cells)],
+    )
+    keep_steps(steps_ref, steps)
+    joined, steps = combine([[value[i] for value in block] for i in range(2)])
+    keep_steps(pair_steps, steps)
+    for i, value in enumerate(joined):
+        block_ref[i] = value
 
 
 def make_join(stride, count):
@@ -254,64 +301,60 @@
     return edges[0], expand(levels[-1][1], *edges)[0], edges[1]
 
 
-def hand_back(near, middle, far, own, send):
-    first = spot_in(1, 2) == 0
-    own[0] = jnp.where(first, near, middle)
-    own[1] = jnp.where(first, middle, far)
-    send[0] = jnp.where(first, middle, near)
-    send[1] = jnp.where(first, far, middle)
-
-
 def make_top(strides, counts):
     below = len(strides) - 1
 
     def top(*refs):
         arrivals = refs[:counts[-1]]
-        lower, (own, send, steps_ref, scratch, edges) = (
+        lower, (faces_ref, steps_ref, scratch, edges) = (
             refs[counts[-1]:counts[-1] + below], refs[counts[-1] + below:]
         )
         place(scratch, arrivals, strides[-1])
-        nothing = jnp.zeros(own.shape[1:], f32)
+        nothing = jnp.zeros(faces_ref.shape[1:], f32)
         _, steps = combine([[scratch[i, j] for j in range(5)] for i in range(counts[-1])])
         keep_steps(steps_ref, steps)
         levels = [(strides[-1], steps)] + [
             (strides[i], steps_of(lower[i])) for i in reversed(range(below))
         ]
-        hand_back(*descend(levels, (nothing, nothing), edges), own, send)
+        for i, value in enumerate(descend(levels, (nothing, nothing), edges)):
+            faces_ref[i] = value
 
     return top
 
 
-def both_halves(own, other, scratch):
-    half = own.shape[1]
-    mine = lax.rem(lax.axis_index("gx"), 2)
-    scratch[:, pl.ds(pl.multiple_of(mine * half, half), half), :] = own[...]
-    scratch[:, pl.ds(pl.multiple_of((1 - mine) * half, half), half), :] = other[...]
-
-
-def y_cells(ref, spot):
-    chunks = ref.shape[1] // chunk
-    return ref[:, pl.ds(spot, chunks, stride=chunk), :]
+def both_edges(faces):
+    return jnp.stack([faces[0], faces[1]]), jnp.stack([faces[1], faces[2]])
+
+
+def y_spots(ref):
+    return ref.shape[1] // chunks
+
+
+def y_rows(ref, spot):
+    return (slice(None), pl.ds(spot, chunks, stride=y_spots(ref)), slice(None))
+
+
+def y_cells(ref):
+    return [ref[y_rows(ref, spot)] for spot in range(y_spots(ref))]
 
 
 def y_links(cond):
-    me, count = lax.axis_index("yz"), lax.axis_size("yz")
-    cells = [y_cells(cond, spot) for spot in range(chunk)]
+    me, count = row_block(), 2 * lax.axis_size("yz")
+    cells = y_cells(cond)
     place_of = lax.broadcasted_iota(jnp.int32, cells[0].shape, 1)
-    chunks = cells[0].shape[1]
     near = jnp.where((place_of == 0) & (me == 0), 0.0, 2.0 * cells[0])
     far = jnp.where((place_of == chunks - 1) & (me == count - 1), 0.0, 2.0 * cells[-1])
     return cells, near, far
 
 
 def by_chunk(value, scratch):
-    slab, chunks, _ = value.shape
+    slab = value.shape[0]
     scratch[...] = value.reshape(slab * chunks, lanes)
     return [scratch[pl.ds(i, slab, stride=chunks), :] for i in range(chunks)]
 
 
 def from_chunk(values, scratch):
-    slab, chunks = values[0].shape[0], len(values)
+    slab = values[0].shape[0]
     for i, value in enumerate(values):
         scratch[pl.ds(i, slab, stride=chunks), :] = value
     return scratch[...].reshape(slab, chunks, lanes)
@@ -319,9 +362,9 @@
 
 def y_factor(cond, storage, cell_factors, chunk_factors, ends, turned):
     conds, near, far = y_links(cond)
-    links = [harmonic(conds[i], conds[i + 1]) for i in range(chunk - 1)] + [far]
-    nothing = [jnp.zeros_like(near)] * chunk
-    block, steps = eliminate(near, links, [y_cells(storage, i) for i in range(chunk)], nothing)
+    links = [harmonic(before, after) for before, after in zip(conds[:-1], conds[1:])] + [far]
+    nothing = [jnp.zeros_like(near)] * len(conds)
+    block, steps = eliminate(near, links, y_cells(storage), nothing)
     keep_steps(cell_factors, [step[:3] for step in steps])
     parts = [by_chunk(value, turned.at[i]) for i, value in enumerate(block[:3])]
     nothing = [jnp.zeros_like(parts[0][0])] * len(parts[0])
@@ -379,13 +422,8 @@
 
 
 def make_points(slab, rows):
-    def points(east, north, depth, at_row, at_depth, here):
-        local_east = east[...] - lax.axis_index("gx") * slab
-        local_north = north[...] - lax.axis_index("yz") * rows
-        inside = (
-            (local_east >= 0) & (local_east < slab) & (local_north >= 0) & (local_north < rows)
-        )
-        spot = jnp.where(inside, local_east * rows + local_north, -1)
+    def points(east, north, depth, heads, at_row, at_depth, here, observed):
+        inside, spot = local_spot(east[...], north[...], slab, rows)
         at_row[...] = jnp.where(
             lax.broadcasted_iota(jnp.int32, at_row.shape, 0) == spot, 1.0, 0.0
         ).astype(jnp.bfloat16)
@@ -393,27 +431,30 @@
             lax.broadcasted_iota(jnp.int32, at_depth.shape, 0) == depth[...], 1.0, 0.0
         )
         here[...] = jnp.where(inside, 1.0, 0.0)
+        observed[...] = heads[...]
 
     return points
 
 
-def y_forward(own, other, x_steps, storage, cell_factors, chunk_factors, ends,
-              head_first, x_edges, scaled_cells, scaled_chunks, message, loads, turned):
-    cells = head_first.shape[0]
-    both_halves(own, other, x_edges)
-    near, far = x_edges[0], x_edges[1]
+def y_forward(x_faces, x_steps, storage, cell_factors, chunk_factors, ends,
+              head_first, scaled_cells, scaled_chunks, message, loads, turned):
+    cells = head_first.shape[0] // 2
+    near, far = both_edges(x_faces)
     for i in reversed(range(cells)):
         far = x_steps[i, 3] + x_steps[i, 1] * near + x_steps[i, 2] * far
-        head_first[i] = far
-        loads[i] = storage[i] * far
+        for j in range(2):
+            head_first[j * cells + i] = far[j]
+            loads[j * cells + i] = storage[j * cells + i] * far[j]
     for i in range(3):
         message[i] = ends[i]
-    y_loads(loads, cell_factors, chunk_factors, scaled_cells, scaled_chunks, turned, message.at[3:5])
-
-
-def y_loads(loads, cell_factors, chunk_factors, scaled_cells, scaled_chunks, turned, message):
+    near, far = y_loads(loads, cell_factors, chunk_factors, scaled_cells, scaled_chunks, turned)
+    message[3] = near
+    message[4] = far
+
+
+def y_loads(loads, cell_factors, chunk_factors, scaled_cells, scaled_chunks, turned):
     near, far, scaled = eliminate_loads(
-        factors_of(cell_factors), [y_cells(loads, i) for i in range(chunk)]
+        factors_of(cell_factors), y_cells(loads)
     )
     for i, value in enumerate(scaled):
         scaled_cells[i] = value
@@ -421,8 +462,7 @@
     joined, scaled = combine_loads(blocks, factors_of(chunk_factors))
     for i, value in enumerate(scaled):
         scaled_chunks[i] = value
-    message[0] = joined[0]
-    message[1] = joined[1]
+    return joined
 
 
 def y_expand(near, far, cell_factors, chunk_factors, scaled_cells, scaled_chunks,
@@ -434,10 +474,10 @@
     far = from_chunk(faces[1:], turned.at[1])
     edges[0] = near
     edges[1] = far
-    for spot in reversed(range(chunk)):
+    for spot in reversed(range(y_spots(natural))):
         far = scaled_cells[spot] + cell_factors[spot, 1] * near + cell_factors[spot, 2] * far
         solved[spot] = far
-        natural[:, pl.ds(spot, natural.shape[1] // chunk, stride=chunk), :] = far
+        natural[y_rows(natural, spot)] = far
 
 
 def z_sweep(loads, parts):
@@ -461,10 +501,10 @@
         sweeps = [(tables[2 * i], tables[2 * i + 1]) for i in range(split)]
         (cell_factors, chunk_factors, scaled_cells, scaled_chunks, storage,
          inverse, at_row, at_depth, here, observed,
-         y_factors, head_second, y_edges, head_third, adjoint_third, message,
+         y_factors, head_second, y_edges, head_third, head_send, adjoint_third, message,
          next_cells, next_chunks,
          scratch, edges, turned, loads, second, third) = refs[count + 2 * split:]
-        me = lax.axis_index("yz")
+        me = row_block()
         for turn, arrival in enumerate(arrivals):
             scratch[me ^ turn] = arrival[...]
         nothing = jnp.zeros(arrivals[0].shape[1:], f32)
@@ -493,7 +533,10 @@
         )
         misfit = here[...] * (found - observed[...])
         for i in range(misfit.shape[1] // lanes):
-            message[2, i:i + 1, :] = misfit[:, i * lanes:(i + 1) * lanes]
+            row = 2 * slab + i
+            message[row:row + 1, :] = misfit[:, i * lanes:(i + 1) * lanes]
+        cells = slab // 2
+        head_send[...] = head_third[pl.ds((1 - side()) * cells, cells)]
         parts = [
             (at_depth[...] * part.astype(f32)).astype(jnp.bfloat16)
             for part in bf16_parts(misfit_weight * misfit, 2)
@@ -510,8 +553,9 @@
             adjoint = (loads[i] * inverse[i]).reshape(per, rows, lanes)
             adjoint_third[i * per:(i + 1) * per] = adjoint
             second[i * per:(i + 1) * per] = storage[i * per:(i + 1) * per] * adjoint
-        y_loads(second, cell_factors, chunk_factors, next_cells, next_chunks, turned,
-                message.at[0:2])
+        near, far = y_loads(second, cell_factors, chunk_factors, next_cells, next_chunks, turned)
+        message[:slab] = near
+        message[slab:2 * slab] = far
 
     return z_solve
 
@@ -520,34 +564,37 @@
     def y_back(*refs):
         arrivals = refs[:count]
         (y_factors, cell_factors, chunk_factors, scaled_cells, scaled_chunks, storage, x_steps,
-         adjoint_second, y_edges, scaled_x, own, send, scratch, edges, turned, second, pair
-         ) = refs[count:]
-        me = lax.axis_index("yz")
-        misfit = arrivals[0][2]
+         pair_steps, adjoint_second, y_edges, scaled_x, pair_scaled, note,
+         scratch, edges, turned, second) = refs[count:]
+        me, slab = row_block(), storage.shape[0]
+        misfit = None
         for turn, arrival in enumerate(arrivals):
-            scratch[me ^ turn] = arrival[:2]
-            if turn:
-                misfit = misfit + arrival[2]
-        nothing = jnp.zeros(arrivals[0].shape[1:], f32)
+            scratch[me ^ turn, 0] = arrival[:slab]
+            scratch[me ^ turn, 1] = arrival[slab:2 * slab]
+            part = arrival[2 * slab:]
+            misfit = part if misfit is None else misfit + part
+        nothing = jnp.zeros(scratch.shape[2:], f32)
         factors = factors_of(y_factors)
         _, scaled = combine_loads([[scratch[i, 0], scratch[i, 1]] for i in range(count)], factors)
         faces = expand(with_scaled(factors, scaled), nothing, nothing)
         near, far = own_edges(edges, me, nothing, faces, nothing)
         y_expand(near, far, cell_factors, chunk_factors, scaled_cells, scaled_chunks,
                  turned, adjoint_second, y_edges, second)
+        for i in range(slab):
+            second[i] = storage[i] * second[i]
         near, far, scaled = eliminate_loads(
-            factors_of(x_steps), [storage[i] * second[i] for i in range(second.shape[0])]
+            factors_of(x_steps), [pair_cells(second, i) for i in range(slab // 2)]
         )
         for i, value in enumerate(scaled):
             scaled_x[i] = value
-        pair[0] = near
-        pair[1] = far
-        half = pair.shape[1] // 2
-        mine = lax.rem(lax.axis_index("gx"), 2)
-        for ref, side in ((own, mine), (send, 1 - mine)):
-            for i in range(2):
-                ref[i * half:(i + 1) * half] = pair[i, pl.ds(pl.multiple_of(side * half, half), half), :]
-            ref[2 * half:] = misfit
+        (near, far), scaled = combine_loads(
+            [[near[i], far[i]] for i in range(2)], factors_of(pair_steps)
+        )
+        pair_scaled[0] = scaled[0]
+        rows = near.shape[0]
+        note[:rows] = near
+        note[rows:2 * rows] = far
+        note[2 * rows:] = misfit
 
     return y_back
 
@@ -559,8 +606,9 @@
         from_left = (
             -near_link * (adjoint_second[0] - adjoint_edges[0]) * (head_second[0] - head_edges[0])
         )
-        for spot in range(chunk):
-            if spot < chunk - 1:
+        spots = len(conds)
+        for spot in range(spots):
+            if spot < spots - 1:
                 to_left, to_right = face_gradient(
                     conds[spot], conds[spot + 1],
                     adjoint_second[spot] - adjoint_second[spot + 1],
@@ -571,7 +619,7 @@
                     -far_link * (adjoint_second[spot] - adjoint_edges[1])
                     * (head_second[spot] - head_edges[1])
                 )
-            natural[:, pl.ds(spot, natural.shape[1] // chunk, stride=chunk), :] = from_left + to_left
+            natural[y_rows(natural, spot)] = from_left + to_left
             from_left = to_right
         slab, rows, _ = cond.shape
         per = slab // cuts
@@ -626,7 +674,7 @@
     def top(*refs):
         arrivals, refs = refs[:counts[-1]], refs[counts[-1]:]
         top_steps, lower, lower_scaled = refs[0], refs[1:1 + below], refs[1 + below:1 + 2 * below]
-        own, send, misfit_ref, scratch, edges = refs[1 + 2 * below:]
+        faces_ref, misfit_ref, scratch, edges = refs[1 + 2 * below:]
         blocks, misfit = loads_in(arrivals, scratch, strides[-1])
         nothing = jnp.zeros(scratch.shape[2:], f32)
         factors = factors_of(top_steps)
@@ -636,90 +684,105 @@
             scaled = [lower_scaled[i][j] for j in range(len(factors))]
             levels.append((strides[i], with_scaled(factors, scaled)))
         misfit_ref[...] = misfit
-        hand_back(*descend(levels, (nothing, nothing), edges), own, send)
+        for i, value in enumerate(descend(levels, (nothing, nothing), edges)):
+            faces_ref[i] = value
 
     return top
 
 
-def x_back(own, other, x_steps, scaled_x, cond, head, x_edges, terms, gradient, edges):
-    cells = cond.shape[0]
-    both_halves(own, other, edges)
+def x_back(faces, head_faces, x_steps, scaled_x, cond, head, terms, own, send, gradient):
+    cells = cond.shape[0] // 2
+    near, far = both_edges(faces)
+    head_near, head_far = both_edges(head_faces)
     near_link, far_link = x_ends(cond)
+    conds = [pair_cells(cond, i) for i in range(cells)]
+    heads = [pair_cells(head, i) for i in range(cells)]
     adjoint = [None] * cells
-    after = edges[1]
+    after = far
     for i in reversed(range(cells)):
-        after = scaled_x[i] + x_steps[i, 1] * edges[0] + x_steps[i, 2] * after
+        after = scaled_x[i] + x_steps[i, 1] * near + x_steps[i, 2] * after
         adjoint[i] = after
-    from_left = -near_link * (adjoint[0] - edges[0]) * (head[0] - x_edges[0])
+    from_left = -near_link * (adjoint[0] - near) * (heads[0] - head_near)
     for i in range(cells):
         if i < cells - 1:
             to_left, to_right = face_gradient(
-                cond[i], cond[i + 1], adjoint[i] - adjoint[i + 1], head[i] - head[i + 1]
+                conds[i], conds[i + 1], adjoint[i] - adjoint[i + 1], heads[i] - heads[i + 1]
             )
-            gradient[i] = terms[i] + from_left + to_left
-            from_left = to_right
         else:
-            gradient[i] = (
-                terms[i] + from_left - far_link * (adjoint[i] - edges[1]) * (head[i] - x_edges[1])
-            )
+            to_left = -far_link * (adjoint[i] - far) * (heads[i] - head_far)
+        value = from_left + to_left
+        for j in range(2):
+            gradient[j * cells + i] = terms[j * cells + i] + value[j]
+        from_left = to_right
+    own[...] = gradient[pl.ds(side() * cells, cells)]
+    send[...] = gradient[pl.ds((1 - side()) * cells, cells)]
+
+
+def settle(own, other, whole, full):
+    cells, half, _ = other.shape
+    start = (own.shape[0] - cells) // cells * side() * cells
+    full[:, pl.ds(pl.multiple_of(side() * half, half), half), :] = own[pl.ds(start, cells)]
+    full[:, pl.ds(pl.multiple_of((1 - side()) * half, half), half), :] = other[...]
+    whole[...] = full[...]
+
+
+def settle_last(own, other, misfits, whole, misfits_out, full):
+    misfits_out[...] = misfits[...]
+    settle(own, other, whole, full)
 
 
 def shards(log_cond, storage, head, well_east, well_north, well_depth, pump_rates,
            probe_east, probe_north, probe_depth, probe_heads):
-    slab, rows, _ = log_cond.shape
+    cells, rows, _ = log_cond.shape
     devices, columns = lax.axis_size("gx"), lax.axis_size("yz")
     inner = 4 if devices >= 16 else 2
     strides, counts = [1, 2, 2 * inner], [2, inner, devices // (2 * inner)]
-    half = rows // 2
-    chunks = rows // chunk
+    slab, half = 2 * cells, rows // 2
     points = probe_heads.shape[0]
-    grid = (slab, rows, lanes)
+    grid = (slab, half, lanes)
     plane = (half, lanes)
-    cell = (chunk, slab, chunks, lanes)
+    spots = half // chunks
+    cell = (spots, slab, chunks, lanes)
     line = (slab, lanes)
+    turned = (slab * chunks, lanes)
 
     places = ((well_east << (2 * field)) + (well_north << field) + well_depth).reshape(1, -1)
     probes = [value.reshape(1, -1) for value in (probe_east, probe_north, probe_depth, probe_heads)]
-    cond, storage, stored = run(
+    parts = run(
         x_load,
-        [grid, grid, grid],
+        [(cells,) + plane] * 6,
         [log_cond, storage, head],
-        [(grid, f32), (grid, f32), pltpu.SemaphoreType.DMA((3,))],
+        [pltpu.SemaphoreType.DMA((6,))],
         raw=3,
         limit=53,
     )
-    loads, own, send = run(
+    (sources,) = run(
+        make_wells(slab, half), [grid], [places, jnp.where(places >= 0, pump_rates.reshape(1, -1), 0.0)], after=[parts[3]]
+    )
+    cond, storage, x_steps, pair_steps, joined = run(
         x_reduce,
-        [grid, (5,) + plane, (5,) + plane],
-        [cond, storage, stored, places, pump_rates.reshape(1, -1)],
-        [((5, rows, lanes), f32)],
-    )
-    (x_steps,) = run(x_factor, [(slab, 4, rows, lanes)], [cond, storage, loads], after=[send])
+        [grid, grid, (cells, 4, 2) + plane, (1, 4) + plane, (5,) + plane],
+        list(parts[:3]) + [swap(part) for part in parts[3:]] + [sources],
+        [((2, 3, cells) + plane, f32), (grid, f32)],
+    )
+    x_levels = [pair_steps]
     cell_factors, chunk_factors, ends = run(
         y_factor,
-        [(chunk, 3) + cell[1:], (chunks - 1, 3) + line, (3,) + line],
+        [(spots, 3) + cell[1:], (chunks - 1, 3) + line, (3,) + line],
         [cond, storage],
-        [((3, slab * chunks, lanes), f32)],
-        after=[send],
-    )
-    joined, steps = run(
-        make_join(1, 2),
-        [(5,) + plane, (1, 4) + plane],
-        [own, swap(send)],
-        [((2, 5) + plane, f32)],
-        after=[x_steps, ends],
-    )
-    x_levels = [steps]
+        [((3,) + turned, f32)],
+        after=[joined],
+    )
 
     cuts = 4
-    piece = (cuts, slab * rows // cuts, lanes)
+    piece = (cuts, slab * half // cuts, lanes)
     levels = lanes.bit_length() - 1
     bounds = [0, 4, levels]
     split = len(bounds) - 1
     carried, z_parts, waits = [cond, storage], [], []
     for i, (stride, count) in enumerate(zip(strides[1:], counts[1:])):
-        arrivals = exchange(joined, "gx", stride, count)
-        waits = []
+        arrivals = exchange(joined, stride, count)
+        waits = [ends]
         if i < split:
             first, last = bounds[i:i + 2]
             from_back, from_ahead, *carried = run(
@@ -729,15 +792,7 @@
                 after=[joined],
             )
             z_parts += [from_back, from_ahead]
-            waits = [carried[1]]
-        if i == split - 1:
-            at_row, at_depth, here = run(
-                make_points(slab, rows),
-                [((slab * rows, points), jnp.bfloat16), (lanes, points), (1, points)],
-                probes[:3],
-                after=[joined],
-            )
-            waits.append(here)
+            waits.append(carried[1])
         if i < len(strides) - 2:
             joined, steps = run(
                 make_join(stride, count),
@@ -747,72 +802,85 @@
                 after=waits,
             )
             x_levels.append(steps)
-    own, send, steps = run(
+    x_faces, steps = run(
         make_top(strides, counts),
-        [(2,) + plane, (2,) + plane, (counts[-1] - 1, 4) + plane],
+        [(3,) + plane, (counts[-1] - 1, 4) + plane],
         arrivals + x_levels,
         [((counts[-1], 5) + plane, f32), ((max(counts) + 1,) + plane, f32)],
         after=waits,
     )
     x_levels.append(steps)
     inverse = carried[1]
-    head_first, x_edges, scaled_cells, scaled_chunks, message = run(
+    head_first, scaled_cells, scaled_chunks, message = run(
         y_forward,
-        [grid, (2, rows, lanes), cell, (chunks - 1,) + line, (5,) + line],
-        [own, swap(send), x_steps, storage, cell_factors, chunk_factors, ends],
-        [(grid, f32), ((2, slab * chunks, lanes), f32)],
-    )
-    (y_factors, head_second, head_edges, head_third, adjoint_third, message,
+        [grid, cell, (chunks - 1,) + line, (5,) + line],
+        [x_faces, x_steps, storage, cell_factors, chunk_factors, ends],
+        [(grid, f32), ((2,) + turned, f32)],
+    )
+    at_row, at_depth, here, observed = run(
+        make_points(slab, half),
+        [((slab * half, points), jnp.bfloat16), (lanes, points), (1, points), (1, points)],
+        probes,
+        after=[message],
+    )
+    extra, blocks = points // lanes, 2 * columns
+    (y_factors, head_second, head_edges, head_third, head_send, adjoint_third, message,
      scaled_cells, scaled_chunks) = run(
-        make_z(columns, cuts, split),
-        [(columns - 1, 3) + line, cell, (2,) + cell[1:], grid, grid,
-         (3,) + line, cell, (chunks - 1,) + line],
-        exchange(message, "yz", 1, columns)
+        make_z(blocks, cuts, split),
+        [(blocks - 1, 3) + line, cell, (2,) + cell[1:], grid, (cells,) + plane, grid,
+         (2 * slab + extra, lanes), cell, (chunks - 1,) + line],
+        exchange_rows(message)
         + z_parts
         + [cell_factors, chunk_factors, scaled_cells, scaled_chunks, storage,
-           inverse, at_row, at_depth, here, probes[3]],
-        [((columns, 5) + line, f32), ((columns + 1,) + line, f32), ((2, slab * chunks, lanes), f32),
-         (piece, f32), (grid, f32), ((slab * rows, 2 * lanes), jnp.bfloat16)],
-    )
-    extra = points // lanes
+           inverse, at_row, at_depth, here, observed],
+        [((blocks, 5) + line, f32), ((blocks + 1,) + line, f32), ((2,) + turned, f32),
+         (piece, f32), (grid, f32), ((slab * half, 2 * lanes), jnp.bfloat16)],
+    )
     note = (2 * half + extra, lanes)
-    adjoint_second, adjoint_edges, scaled_x, own, send = run(
-        make_y_back(columns),
-        [cell, (2,) + cell[1:], grid, note, note],
-        exchange(message, "yz", 1, columns)
-        + [y_factors, cell_factors, chunk_factors, scaled_cells, scaled_chunks, storage, x_steps],
-        [((columns, 2) + line, f32), ((columns + 1,) + line, f32), ((2, slab * chunks, lanes), f32),
-         (grid, f32), ((2, rows, lanes), f32)],
-    )
+    adjoint_second, adjoint_edges, scaled_x, scaled, message = run(
+        make_y_back(blocks),
+        [cell, (2,) + cell[1:], (cells, 2) + plane, (1,) + plane, note],
+        exchange_rows(message)
+        + [y_factors, cell_factors, chunk_factors, scaled_cells, scaled_chunks, storage, x_steps,
+           pair_steps],
+        [((blocks, 2) + line, f32), ((blocks + 1,) + line, f32), ((2,) + turned, f32),
+         (grid, f32)],
+    )
+    x_scaled = [scaled]
     (terms,) = run(
         make_terms(cuts),
         [grid],
         [cond, head_third, adjoint_third, head_second, adjoint_second, head_edges, adjoint_edges],
         [(grid, f32)],
     )
-    arrivals, x_scaled = [own, swap(send)], []
-    for i, (stride, count) in enumerate(zip(strides[:-1], counts[:-1])):
+    for i in range(1, len(strides) - 1):
+        arrivals = exchange(message, strides[i], counts[i])
         message, scaled = run(
-            make_join_loads(stride, count),
-            [note, (count - 1,) + plane],
+            make_join_loads(strides[i], counts[i]),
+            [note, (counts[i] - 1,) + plane],
             arrivals + [x_levels[i]],
-            [((count, 2) + plane, f32)],
+            [((counts[i], 2) + plane, f32)],
         )
         x_scaled.append(scaled)
-        arrivals = exchange(message, "gx", strides[i + 1], counts[i + 1])
-    own, send, misfits = run(
+    faces, misfits = run(
         make_top_loads(strides, counts),
-        [(2,) + plane, (2,) + plane, (extra, lanes)],
-        arrivals + x_levels[-1:] + x_levels[:-1] + x_scaled,
+        [(3,) + plane, (extra, lanes)],
+        exchange(message, strides[-1], counts[-1]) + x_levels[-1:] + x_levels[:-1] + x_scaled,
         [((counts[-1], 2) + plane, f32), ((max(counts) + 1,) + plane, f32)],
-    )
-    (gradient,) = run(
+        after=[terms],
+    )
+    whole = (cells, rows, lanes)
+    (head_next,) = run(settle, [whole], [head_third, swap(head_send)], [(whole, f32)])
+    own, send = run(
         x_back,
-        [grid],
-        [own, swap(send), x_steps, scaled_x, cond, head_first, x_edges, terms],
-        [((2, rows, lanes), f32)],
-    )
-    return head_third, gradient, misfits.reshape(-1)
+        [(cells,) + plane, (cells,) + plane],
+        [faces, x_faces, x_steps, scaled_x, cond, head_first, terms],
+        [(grid, f32)],
+    )
+    gradient, misfits = run(
+        settle_last, [whole, (extra, lanes)], [own, swap(send), misfits], [(whole, f32)]
+    )
+    return head_next, gradient, misfits.reshape(-1)
 
 
 def solution(mesh):

time: 50.7 us -> 47.6 us (0.939)
  waiting for transfers between devices: 16.5 us -> 13.7 us
  starting transfers between devices: 16.5 us -> 18.9 us
  local copies, waits for them, and re-layouts: 2.03 us -> 0.15 us
  other arithmetic: 0.69 us -> 0.01 us
    ppermute x14 -> x19, waiting for transfers between devices: 16.5 us -> 13.7 us  [the longest x13 8.56 us: exchange(): lax.ppermute(value, 'gx', [(i, i ^ turn * stride) for i in range(size)])]
    ppermute x14 -> x19, starting transfers between devices: 16.5 us -> 18.9 us  [the longest x13 15.1 us: exchange(): lax.ppermute(value, 'gx', [(i, i ^ turn * stride) for i in range(size)])]
    unnamed x12 -> x16, local copies, waits for them, and re-layouts: 2.03 us -> 0.15 us
    reshape x1 -> x0, other arithmetic: 0.69 us -> none  [shards(): ((well_east << 2 * field) + (well_north << field) + well_depth).reshape(1...]
  transfers between devices with their start and end apart: 14 -> 19, of which waited for: 12 -> 14; matrix products, arithmetic and copies ran while one was open for 0% -> 0% of each run, Pallas kernels for 13% -> 16%
where the time goes in v2:
time: 47.6 us; the launch traced here: 47.4 us
  starting transfers between devices  18.9 us (40%)
  Pallas kernels  13.9 us (29%)
  waiting for transfers between devices  13.7 us (29%)
  between operations  0.82 us (2%)
    ppermute x13, starting transfers between devices, exchange(): lax.ppermute(value, 'gx', [(i, i ^ turn * stride) for i in range(size)])  15.1 us
    pallas_call x18, Pallas kernels, run(): pl.pallas_call(ordered, out_shape=shapes, in_specs=[pl.BlockSpec(memory_s...  13.9 us
    ppermute x13, waiting for transfers between devices, exchange(): lax.ppermute(value, 'gx', [(i, i ^ turn * stride) for i in range(size)])  8.56 us
    ppermute x6, waiting for transfers between devices, exchange_rows(): lax.ppermute(value, ('gx', 'yz'), [(i * columns + j, (i ^ turn % 2) * col...  5.12 us
    ppermute x6, starting transfers between devices, exchange_rows(): lax.ppermute(value, ('gx', 'yz'), [(i * columns + j, (i ^ turn % 2) * col...  3.85 us
  transfers between devices with their start and end apart: 19, of which 14 were waited for; matrix products, arithmetic and copies ran while one was open for 0% of the time, Pallas kernels for 16%

profile of v2, /device:TPU:0, one launch (start us, length us, event | category | flops | bytes accessed | tf_op | source)
XLA Modules:
  0.0 47.4 jit_solution(5059380036995964504)
XLA Ops:
  0.6 1.3 %shard_map.130 = (f32[8,32,128]{2,1,0:T(8,128)S(1)}, f32[8,32,128]{2,1,0:T(8,128)S(1)}, f32[8,32,128]{2,1,0:T(8,128)S(1)}, f32[8,32,128]{2,1,0:T(8,128)S(1)}, f3...) custom-call(f32[8,64,128]{2,1,0:T(8,128)} %refs_0_.1, f32[8,64,128]{2,1,0:T(8,128)} %refs_1_.1, f32[8,64,128]{2,1,0:T(8,128)} %refs_2_.1), custom_call_target="tpu_custom_call" | custom-call | flops 1000000 | bytes 1572864 | tf_op jit(solution)/shard_map/pallas_call | solution.py:128
  1.9 0.5 %collective-permute-start.1 = (f32[8,32,128]{2,1,0:T(8,128)S(1)}, f32[8,32,128]{2,1,0:T(8,128)S(1)}, u32[]{:S(2)}, u32[]{:S(2)}) collective-permute-start(f32[8,32,128]{2,1,0:T(8,128)S(1)} %get-tuple-element.62), channel_id=1, source_target_pairs={{0,2},{2,0},{4,6},{6,4},{8,10},{10,8},{12,14},{14,12},{16,18},{18,... | collective-permute-start | bytes 393224 | tf_op jit(solution)/shard_map/ppermute | solution.py:154
  2.6 0.5 collective-permute-start
  3.4 0.4 collective-permute-done.2.refs_5_
  4.0 0.4 shard_map.132
  4.4 3.9 %collective-permute-start.5 = (f32[5,32,128]{2,1,0:T(8,128)S(1)}, f32[5,32,128]{2,1,0:T(8,128)S(1)}, u32[]{:S(2)}, u32[]{:S(2)}) collective-permute-start(f32[5,32,128]{2,1,0:T(8,128)S(1)} %get-tuple-element.64.refs_2_.refs_0_), channel_id=1, source_target_pairs={{0,12},{2,14},{4,8},{6,10},{8,4},{10,6},{12,0},{14,2},{16,28},{18,... | collective-permute-start | bytes 245768 | tf_op jit(solution)/shard_map/ppermute | solution.py:154
  8.3 0.4 collective-permute-start.4
  9.3 2.7 %shard_map.134 = (f32[4,4,128,128]{3,2,1,0:T(8,128)S(1)}, f32[4,4,128,128]{3,2,1,0:T(8,128)S(1)}, f32[4,128,128]{2,1,0:T(8,128)S(1)}, f32[4,128,128]{2,1,0:T(8,128)S(1)}) custom-call(f32[16,32,128]{2,1,0:T(8,128)S(1)} %get-tuple-element.65.refs_0_.refs_4_, f32[16,32,128]{2,1,0:T(8,128)S(1)} %get-tuple-element.66.refs_1_.refs_2_.refs_12_.refs_9_, ...), custom_call_target="tpu_custom_call" | custom-call | flops 1000000 | bytes 3145728 | tf_op jit(solution)/shard_map/pallas_call | solution.py:128
  12.0 1.1 %collective-permute-done.4.refs_2_ = f32[5,32,128]{2,1,0:T(8,128)S(1)} collective-permute-done((f32[5,32,128]{2,1,0:T(8,128)S(1)}, f32[5,32,128]{2,1,0:T(8,128)S(1)}, u32[]{:S(2)}, u32[]{:S(2)}) %collective-permute-start.4) | collective-permute-done | bytes 81952 | tf_op jit(solution)/shard_map/ppermute | solution.py:154
  13.3 2.7 %collective-permute-start.6 = (f32[5,32,128]{2,1,0:T(8,128)S(1)}, f32[5,32,128]{2,1,0:T(8,128)S(1)}, u32[]{:S(2)}, u32[]{:S(2)}) collective-permute-start(f32[5,32,128]{2,1,0:T(8,128)S(1)} %get-tuple-element.69.refs_2_.refs_0_), channel_id=1, source_target_pairs={{0,16},{2,18},{4,20},{6,22},{8,24},{10,26},{12,28},{14,30},{16,0},... | collective-permute-start | bytes 245768 | tf_op jit(solution)/shard_map/ppermute | solution.py:154
  16.0 2.5 %shard_map.136 = (f32[3,4,128,128]{3,2,1,0:T(8,128)S(1)}, f32[3,4,128,128]{3,2,1,0:T(8,128)S(1)}, f32[4,128,128]{2,1,0:T(8,128)}, f32[4,128,128]{2,1,0:T(8,128)S(1)}) custom-call(f32[4,128,128]{2,1,0:T(8,128)S(1)} %get-tuple-element.72.refs_0_, f32[4,128,128]{2,1,0:T(8,128)S(1)} %get-tuple-element.68.refs_5_.refs_1_, ...), custom_call_target="tpu_custom_call" | custom-call | flops 1000000 | bytes 2621440 | tf_op jit(solution)/shard_map/pallas_call | solution.py:128
  18.5 0.4 collective-permute-done.6.refs_1_
  19.3 1.6 %collective-permute-start.8 = (f32[5,16,128]{2,1,0:T(8,128)S(1)}, f32[5,16,128]{2,1,0:T(8,128)S(1)}, u32[]{:S(2)}, u32[]{:S(2)}) collective-permute-start(f32[5,16,128]{2,1,0:T(8,128)S(1)} %get-tuple-element.78.refs_4_.refs_0_), channel_id=1, source_target_pairs={{0,1},{1,0},{2,3},{3,2},{4,5},{5,4},{6,7},{7,6},{8,9},{9,8},{10,11... | collective-permute-start | bytes 122888 | tf_op jit(solution)/shard_map/ppermute | solution.py:166
  20.9 0.3 collective-permute-start.7
  21.4 1.7 %collective-permute-done.9.refs_3_ = f32[5,16,128]{2,1,0:T(8,128)S(1)} collective-permute-done((f32[5,16,128]{2,1,0:T(8,128)S(1)}, f32[5,16,128]{2,1,0:T(8,128)S(1)}, u32[]{:S(2)}, u32[]{:S(2)}) %collective-permute-start.9) | collective-permute-done | bytes 40992 | tf_op jit(solution)/shard_map/ppermute | solution.py:166
  23.1 0.6 %collective-permute-done.8.refs_2_ = f32[5,16,128]{2,1,0:T(8,128)S(1)} collective-permute-done((f32[5,16,128]{2,1,0:T(8,128)S(1)}, f32[5,16,128]{2,1,0:T(8,128)S(1)}, u32[]{:S(2)}, u32[]{:S(2)}) %collective-permute-start.8) | collective-permute-done | bytes 40992 | tf_op jit(solution)/shard_map/ppermute | solution.py:166
  23.7 3.3 %shard_map.140 = (f32[3,3,16,128]{3,2,1,0:T(8,128)S(1)}, f32[4,16,8,128]{3,2,1,0:T(8,128)S(1)}, f32[2,16,8,128]{3,2,1,0:T(8,128)S(1)}, f32[16,32,128]{2,1,0:T(8,...) custom-call(f32[5,16,128]{2,1,0:T(8,128)S(1)} %get-tuple-element.78., ...), custom_call_target="tpu_custom_call" | custom-call | flops 1000000 | bytes 9728000 | tf_op jit(solution)/shard_map/pallas_call | solution.py:128
  27.0 1.0 %collective-permute-start.13 = (f32[40,128]{1,0:T(8,128)S(1)}, f32[40,128]{1,0:T(8,128)S(1)}, u32[]{:S(2)}, u32[]{:S(2)}) collective-permute-start(f32[40,128]{1,0:T(8,128)S(1)} %get-tuple-element.91.refs_0_), channel_id=1, source_target_pairs={{0,3},{1,2},{2,1},{3,0},{4,7},{5,6},{6,5},{7,4},{8,11},{9,10},{10,... | collective-permute-start | bytes 61448 | tf_op jit(solution)/shard_map/ppermute | solution.py:166
  28.0 0.9 %collective-permute-start.12 = (f32[40,128]{1,0:T(8,128)S(1)}, f32[40,128]{1,0:T(8,128)S(1)}, u32[]{:S(2)}, u32[]{:S(2)}) collective-permute-start(f32[40,128]{1,0:T(8,128)S(1)} %get-tuple-element.91.refs_0_), channel_id=1, source_target_pairs={{0,1},{1,0},{2,3},{3,2},{4,5},{5,4},{6,7},{7,6},{8,9},{9,8},{10,11... | collective-permute-start | bytes 61448 | tf_op jit(solution)/shard_map/ppermute | solution.py:166
  28.9 1.3 %collective-permute-done.13.refs_3_ = f32[40,128]{1,0:T(8,128)S(1)} collective-permute-done((f32[40,128]{1,0:T(8,128)S(1)}, f32[40,128]{1,0:T(8,128)S(1)}, u32[]{:S(2)}, u32[]{:S(2)}) %collective-permute-start.13) | collective-permute-done | bytes 20512 | tf_op jit(solution)/shard_map/ppermute | solution.py:166
  30.2 1.5 %collective-permute-done.12.refs_2_ = f32[40,128]{1,0:T(8,128)S(1)} collective-permute-done((f32[40,128]{1,0:T(8,128)S(1)}, f32[40,128]{1,0:T(8,128)S(1)}, u32[]{:S(2)}, u32[]{:S(2)}) %collective-permute-start.12) | collective-permute-done | bytes 20512 | tf_op jit(solution)/shard_map/ppermute | solution.py:166
  32.0 3.2 %collective-permute-start.16 = (f32[72,128]{1,0:T(8,128)S(1)}, f32[72,128]{1,0:T(8,128)S(1)}, u32[]{:S(2)}, u32[]{:S(2)}) collective-permute-start(f32[72,128]{1,0:T(8,128)S(1)} %get-tuple-element.95.refs_0_), channel_id=1, source_target_pairs={{0,12},{2,14},{4,8},{6,10},{8,4},{10,6},{12,0},{14,2},{16,28},{18,... | collective-permute-start | bytes 110600 | tf_op jit(solution)/shard_map/ppermute | solution.py:154
  35.2 0.8 %collective-permute-start.15 = (f32[72,128]{1,0:T(8,128)S(1)}, f32[72,128]{1,0:T(8,128)S(1)}, u32[]{:S(2)}, u32[]{:S(2)}) collective-permute-start(f32[72,128]{1,0:T(8,128)S(1)} %get-tuple-element.95.refs_0_), channel_id=1, source_target_pairs={{0,8},{2,10},{4,12},{6,14},{8,0},{10,2},{12,4},{14,6},{16,24},{18,... | collective-permute-start | bytes 110600 | tf_op jit(solution)/shard_map/ppermute | solution.py:154
  36.1 1.1 %collective-permute-done.16.refs_3_ = f32[72,128]{1,0:T(8,128)S(1)} collective-permute-done((f32[72,128]{1,0:T(8,128)S(1)}, f32[72,128]{1,0:T(8,128)S(1)}, u32[]{:S(2)}, u32[]{:S(2)}) %collective-permute-start.16) | collective-permute-done | bytes 36896 | tf_op jit(solution)/shard_map/ppermute | solution.py:154
  37.1 2.0 %collective-permute-done.15.refs_2_ = f32[72,128]{1,0:T(8,128)S(1)} collective-permute-done((f32[72,128]{1,0:T(8,128)S(1)}, f32[72,128]{1,0:T(8,128)S(1)}, u32[]{:S(2)}, u32[]{:S(2)}) %collective-permute-start.15) | collective-permute-done | bytes 36896 | tf_op jit(solution)/shard_map/ppermute | solution.py:154
  39.2 0.8 %collective-permute-done.14.refs_1_ = f32[72,128]{1,0:T(8,128)S(1)} collective-permute-done((f32[72,128]{1,0:T(8,128)S(1)}, f32[72,128]{1,0:T(8,128)S(1)}, u32[]{:S(2)}, u32[]{:S(2)}) %collective-permute-start.14) | collective-permute-done | bytes 36896 | tf_op jit(solution)/shard_map/ppermute | solution.py:154
  40.1 2.6 %collective-permute-start.17 = (f32[72,128]{1,0:T(8,128)S(1)}, f32[72,128]{1,0:T(8,128)S(1)}, u32[]{:S(2)}, u32[]{:S(2)}) collective-permute-start(f32[72,128]{1,0:T(8,128)S(1)} %get-tuple-element.96.refs_0_), channel_id=1, source_target_pairs={{0,16},{2,18},{4,20},{6,22},{8,24},{10,26},{12,28},{14,30},{16,0},... | collective-permute-start | bytes 110600 | tf_op jit(solution)/shard_map/ppermute | solution.py:154
  42.7 0.5 %shard_map.144.refs_7_.refs_6_ = f32[16,32,128]{2,1,0:T(8,128)S(1)} custom-call(f32[16,32,128]{2,1,0:T(8,128)S(1)} %get-tuple-element.65.refs_0_.refs_4_, f32[16,32,128]{2,1,0:T(8,128)S(1)} %get-tuple-element.89.refs_0_.refs_1_, f32[16,32,128]{2,1,0:T(8,128)S(1)} %get-tuple-element.100.refs_2_, f32[4,16,8,128]{3,2,1,0:T(8,128)S(1)} %get-tuple-element.101.refs_3_, ...), custom_call_target="tpu_custom_call" | custom-call | flops 1000000 | bytes 1835008 | tf_op jit(solution)/shard_map/pallas_call | solution.py:128
  43.2 1.8 %collective-permute-done.17.refs_1_ = f32[72,128]{1,0:T(8,128)S(1)} collective-permute-done((f32[72,128]{1,0:T(8,128)S(1)}, f32[72,128]{1,0:T(8,128)S(1)}, u32[]{:S(2)}, u32[]{:S(2)}) %collective-permute-start.17) | collective-permute-done | bytes 36896 | tf_op jit(solution)/shard_map/ppermute | solution.py:154
  45.3 0.8 %shard_map.141 = f32[8,64,128]{2,1,0:T(8,128)} custom-call(f32[16,32,128]{2,1,0:T(8,128)S(1)} %get-tuple-element.89.refs_0_.refs_1_, f32[8,32,128]{2,1,0:T(8,128)S(1)} %collective-permute-done.10.refs_1_), custom_call_target="tpu_custom_call" | custom-call | flops 1000000 | bytes 655360 | tf_op jit(solution)/shard_map/pallas_call | solution.py:128
  46.1 0.6 %collective-permute-done.18.refs_1_ = f32[8,32,128]{2,1,0:T(8,128)S(1)} collective-permute-done((f32[8,32,128]{2,1,0:T(8,128)S(1)}, f32[8,32,128]{2,1,0:T(8,128)S(1)}, u32[]{:S(2)}, u32[]{:S(2)}) %collective-permute-start.18) | collective-permute-done | bytes 131104 | tf_op jit(solution)/shard_map/ppermute | solution.py:154
  46.7 0.8 %shard_map.147 = (f32[8,64,128]{2,1,0:T(8,128)}, f32[8,128]{1,0:T(8,128)}) custom-call(f32[8,32,128]{2,1,0:T(8,128)S(1)} %get-tuple-element.108.refs_0_, f32[8,32,128]{2,1,0:T(8,128)S(1)} %collective-permute-done.18.refs_1_, f32[8,128]{1,0:T(8,128)S(1)} %get-tuple-element.110.refs_2_), custom_call_target="tpu_custom_call" | custom-call | flops 1000000 | bytes 532480 | tf_op jit(solution)/shard_map/pallas_call | solution.py:128
  (41 shorter events, 2.7 us)
Async XLA Ops:
  1.9 1.5 %collective-permute-start.1 = (f32[8,32,128]{2,1,0:T(8,128)S(1)}, f32[8,32,128]{2,1,0:T(8,128)S(1)}, u32[]{:S(2)}, u32[]{:S(2)}) collective-permute-start(f32[8,32,128]{2,1,0:T(8,128)S(1)} %get-tuple-element.62), channel_id=1, source_target_pairs={{0,2},{2,0},{4,6},{6,4},{8,10},{10,8},{12,14},{14,12},{16,18},{18,... | collective-permute-start | bytes 393224 | tf_op jit(solution)/shard_map/ppermute | solution.py:154
  2.4 0.7 %copy-start.7 = (s32[32]{0:T(128)S(1)}, s32[32]{0:T(128)}, u32[]{:S(2)}) copy-start(s32[32]{0:T(128)} %param.14) | copy-start | bytes 388
  2.4 0.7 %copy-start.4 = (f32[32]{0:T(128)S(1)}, f32[32]{0:T(128)}, u32[]{:S(2)}) copy-start(f32[32]{0:T(128)} %param.17) | copy-start | bytes 388
  2.4 0.7 %copy-start.5 = (s32[32]{0:T(128)S(1)}, s32[32]{0:T(128)}, u32[]{:S(2)}) copy-start(s32[32]{0:T(128)} %param.16) | copy-start | bytes 388
  2.4 0.7 %copy-start.6 = (s32[32]{0:T(128)S(1)}, s32[32]{0:T(128)}, u32[]{:S(2)}) copy-start(s32[32]{0:T(128)} %param.15) | copy-start | bytes 388
  2.4 1.4 %collective-permute-start.2 = (f32[8,32,128]{2,1,0:T(8,128)S(1)}, f32[8,32,128]{2,1,0:T(8,128)S(1)}, u32[]{:S(2)}, u32[]{:S(2)}) collective-permute-start(f32[8,32,128]{2,1,0:T(8,128)S(1)} %get-tuple-element.63), channel_id=1, source_target_pairs={{0,2},{2,0},{4,6},{6,4},{8,10},{10,8},{12,14},{14,12},{16,18},{18,... | collective-permute-start | bytes 393224 | tf_op jit(solution)/shard_map/ppermute | solution.py:154
  2.6 1.5 %collective-permute-start = (f32[8,32,128]{2,1,0:T(8,128)S(1)}, f32[8,32,128]{2,1,0:T(8,128)S(1)}, u32[]{:S(2)}, u32[]{:S(2)}) collective-permute-start(f32[8,32,128]{2,1,0:T(8,128)S(1)} %get-tuple-element.61.refs_2_), channel_id=1, source_target_pairs={{0,2},{2,0},{4,6},{6,4},{8,10},{10,8},{12,14},{14,12},{16,18},{18,... | collective-permute-start | bytes 393224 | tf_op jit(solution)/shard_map/ppermute | solution.py:154
  4.4 7.6 %collective-permute-start.5 = (f32[5,32,128]{2,1,0:T(8,128)S(1)}, f32[5,32,128]{2,1,0:T(8,128)S(1)}, u32[]{:S(2)}, u32[]{:S(2)}) collective-permute-start(f32[5,32,128]{2,1,0:T(8,128)S(1)} %get-tuple-element.64.refs_2_.refs_0_), channel_id=1, source_target_pairs={{0,12},{2,14},{4,8},{6,10},{8,4},{10,6},{12,0},{14,2},{16,28},{18,... | collective-permute-start | bytes 245768 | tf_op jit(solution)/shard_map/ppermute | solution.py:154
  8.3 4.7 %collective-permute-start.4 = (f32[5,32,128]{2,1,0:T(8,128)S(1)}, f32[5,32,128]{2,1,0:T(8,128)S(1)}, u32[]{:S(2)}, u32[]{:S(2)}) collective-permute-start(f32[5,32,128]{2,1,0:T(8,128)S(1)} %get-tuple-element.64.refs_2_.refs_0_), channel_id=1, source_target_pairs={{0,8},{2,10},{4,12},{6,14},{8,0},{10,2},{12,4},{14,6},{16,24},{18,... | collective-permute-start | bytes 245768 | tf_op jit(solution)/shard_map/ppermute | solution.py:154
  8.8 4.4 %collective-permute-start.3 = (f32[5,32,128]{2,1,0:T(8,128)S(1)}, f32[5,32,128]{2,1,0:T(8,128)S(1)}, u32[]{:S(2)}, u32[]{:S(2)}) collective-permute-start(f32[5,32,128]{2,1,0:T(8,128)S(1)} %get-tuple-element.64.refs_2_.refs_0_), channel_id=1, source_target_pairs={{0,4},{2,6},{4,0},{6,2},{8,12},{10,14},{12,8},{14,10},{16,20},{18,... | collective-permute-start | bytes 245768 | tf_op jit(solution)/shard_map/ppermute | solution.py:154
  13.3 5.6 %collective-permute-start.6 = (f32[5,32,128]{2,1,0:T(8,128)S(1)}, f32[5,32,128]{2,1,0:T(8,128)S(1)}, u32[]{:S(2)}, u32[]{:S(2)}) collective-permute-start(f32[5,32,128]{2,1,0:T(8,128)S(1)} %get-tuple-element.69.refs_2_.refs_0_), channel_id=1, source_target_pairs={{0,16},{2,18},{4,20},{6,22},{8,24},{10,26},{12,28},{14,30},{16,0},... | collective-permute-start | bytes 245768 | tf_op jit(solution)/shard_map/ppermute | solution.py:154
  19.0 2.2 %copy-start.2 = (s32[1024]{0:T(1024)S(1)}, s32[1024]{0:T(1024)}, u32[]{:S(2)}) copy-start(s32[1024]{0:T(1024)} %param.20) | copy-start | bytes 12292
  19.0 2.2 %copy-start.3 = (f32[1024]{0:T(1024)S(1)}, f32[1024]{0:T(1024)}, u32[]{:S(2)}) copy-start(f32[1024]{0:T(1024)} %param.21) | copy-start | bytes 12292
  19.2 2.0 %copy-start.1 = (s32[1024]{0:T(1024)S(1)}, s32[1024]{0:T(1024)}, u32[]{:S(2)}) copy-start(s32[1024]{0:T(1024)} %param.19) | copy-start | bytes 12292
  19.2 1.9 %copy-start = (s32[1024]{0:T(1024)S(1)}, s32[1024]{0:T(1024)}, u32[]{:S(2)}) copy-start(s32[1024]{0:T(1024)} %param.18) | copy-start | bytes 12292
  19.2 3.9 %collective-permute-start.9 = (f32[5,16,128]{2,1,0:T(8,128)S(1)}, f32[5,16,128]{2,1,0:T(8,128)S(1)}, u32[]{:S(2)}, u32[]{:S(2)}) collective-permute-start(f32[5,16,128]{2,1,0:T(8,128)S(1)} %get-tuple-element.78.refs_4_.refs_0_), channel_id=1, source_target_pairs={{0,3},{1,2},{2,1},{3,0},{4,7},{5,6},{6,5},{7,4},{8,11},{9,10},{10,... | collective-permute-start | bytes 122888 | tf_op jit(solution)/shard_map/ppermute | solution.py:166
  19.3 4.4 %collective-permute-start.8 = (f32[5,16,128]{2,1,0:T(8,128)S(1)}, f32[5,16,128]{2,1,0:T(8,128)S(1)}, u32[]{:S(2)}, u32[]{:S(2)}) collective-permute-start(f32[5,16,128]{2,1,0:T(8,128)S(1)} %get-tuple-element.78.refs_4_.refs_0_), channel_id=1, source_target_pairs={{0,1},{1,0},{2,3},{3,2},{4,5},{5,4},{6,7},{7,6},{8,9},{9,8},{10,11... | collective-permute-start | bytes 122888 | tf_op jit(solution)/shard_map/ppermute | solution.py:166
  20.9 2.8 %collective-permute-start.7 = (f32[5,16,128]{2,1,0:T(8,128)S(1)}, f32[5,16,128]{2,1,0:T(8,128)S(1)}, u32[]{:S(2)}, u32[]{:S(2)}) collective-permute-start(f32[5,16,128]{2,1,0:T(8,128)S(1)} %get-tuple-element.78.refs_4_.refs_0_), channel_id=1, source_target_pairs={{0,2},{1,3},{2,0},{3,1},{4,6},{5,7},{6,4},{7,5},{8,10},{9,11},{10,... | collective-permute-start | bytes 122888 | tf_op jit(solution)/shard_map/ppermute | solution.py:166
  27.0 3.3 %collective-permute-start.13 = (f32[40,128]{1,0:T(8,128)S(1)}, f32[40,128]{1,0:T(8,128)S(1)}, u32[]{:S(2)}, u32[]{:S(2)}) collective-permute-start(f32[40,128]{1,0:T(8,128)S(1)} %get-tuple-element.91.refs_0_), channel_id=1, source_target_pairs={{0,3},{1,2},{2,1},{3,0},{4,7},{5,6},{6,5},{7,4},{8,11},{9,10},{10,... | collective-permute-start | bytes 61448 | tf_op jit(solution)/shard_map/ppermute | solution.py:166
  28.0 3.8 %collective-permute-start.12 = (f32[40,128]{1,0:T(8,128)S(1)}, f32[40,128]{1,0:T(8,128)S(1)}, u32[]{:S(2)}, u32[]{:S(2)}) collective-permute-start(f32[40,128]{1,0:T(8,128)S(1)} %get-tuple-element.91.refs_0_), channel_id=1, source_target_pairs={{0,1},{1,0},{2,3},{3,2},{4,5},{5,4},{6,7},{7,6},{8,9},{9,8},{10,11... | collective-permute-start | bytes 61448 | tf_op jit(solution)/shard_map/ppermute | solution.py:166
  28.8 2.9 %collective-permute-start.11 = (f32[40,128]{1,0:T(8,128)S(1)}, f32[40,128]{1,0:T(8,128)S(1)}, u32[]{:S(2)}, u32[]{:S(2)}) collective-permute-start(f32[40,128]{1,0:T(8,128)S(1)} %get-tuple-element.91.refs_0_), channel_id=1, source_target_pairs={{0,2},{1,3},{2,0},{3,1},{4,6},{5,7},{6,4},{7,5},{8,10},{9,11},{10,... | collective-permute-start | bytes 61448 | tf_op jit(solution)/shard_map/ppermute | solution.py:166
  32.0 5.2 %collective-permute-start.16 = (f32[72,128]{1,0:T(8,128)S(1)}, f32[72,128]{1,0:T(8,128)S(1)}, u32[]{:S(2)}, u32[]{:S(2)}) collective-permute-start(f32[72,128]{1,0:T(8,128)S(1)} %get-tuple-element.95.refs_0_), channel_id=1, source_target_pairs={{0,12},{2,14},{4,8},{6,10},{8,4},{10,6},{12,0},{14,2},{16,28},{18,... | collective-permute-start | bytes 110600 | tf_op jit(solution)/shard_map/ppermute | solution.py:154
  35.2 4.0 %collective-permute-start.15 = (f32[72,128]{1,0:T(8,128)S(1)}, f32[72,128]{1,0:T(8,128)S(1)}, u32[]{:S(2)}, u32[]{:S(2)}) collective-permute-start(f32[72,128]{1,0:T(8,128)S(1)} %get-tuple-element.95.refs_0_), channel_id=1, source_target_pairs={{0,8},{2,10},{4,12},{6,14},{8,0},{10,2},{12,4},{14,6},{16,24},{18,... | collective-permute-start | bytes 110600 | tf_op jit(solution)/shard_map/ppermute | solution.py:154
  36.1 4.0 %collective-permute-start.14 = (f32[72,128]{1,0:T(8,128)S(1)}, f32[72,128]{1,0:T(8,128)S(1)}, u32[]{:S(2)}, u32[]{:S(2)}) collective-permute-start(f32[72,128]{1,0:T(8,128)S(1)} %get-tuple-element.95.refs_0_), channel_id=1, source_target_pairs={{0,4},{2,6},{4,0},{6,2},{8,12},{10,14},{12,8},{14,10},{16,20},{18,... | collective-permute-start | bytes 110600 | tf_op jit(solution)/shard_map/ppermute | solution.py:154
  40.1 4.9 %collective-permute-start.17 = (f32[72,128]{1,0:T(8,128)S(1)}, f32[72,128]{1,0:T(8,128)S(1)}, u32[]{:S(2)}, u32[]{:S(2)}) collective-permute-start(f32[72,128]{1,0:T(8,128)S(1)} %get-tuple-element.96.refs_0_), channel_id=1, source_target_pairs={{0,16},{2,18},{4,20},{6,22},{8,24},{10,26},{12,28},{14,30},{16,0},... | collective-permute-start | bytes 110600 | tf_op jit(solution)/shard_map/ppermute | solution.py:154
  42.7 2.7 %collective-permute-start.10 = (f32[8,32,128]{2,1,0:T(8,128)S(1)}, f32[8,32,128]{2,1,0:T(8,128)S(1)}, u32[]{:S(2)}, u32[]{:S(2)}) collective-permute-start(f32[8,32,128]{2,1,0:T(8,128)S(1)} %get-tuple-element.90), channel_id=1, source_target_pairs={{0,2},{2,0},{4,6},{6,4},{8,10},{10,8},{12,14},{14,12},{16,18},{18,... | collective-permute-start | bytes 393224 | tf_op jit(solution)/shard_map/ppermute | solution.py:154
  45.2 1.4 %collective-permute-start.18 = (f32[8,32,128]{2,1,0:T(8,128)S(1)}, f32[8,32,128]{2,1,0:T(8,128)S(1)}, u32[]{:S(2)}, u32[]{:S(2)}) collective-permute-start(f32[8,32,128]{2,1,0:T(8,128)S(1)} %get-tuple-element.109), channel_id=1, source_target_pairs={{0,2},{2,0},{4,6},{6,4},{8,10},{10,8},{12,14},{14,12},{16,18},{18,... | collective-permute-start | bytes 393224 | tf_op jit(solution)/shard_map/ppermute | solution.py:154

commit v3 on v2

--- a/solution.py
+++ b/solution.py
@@ -282,11 +282,21 @@
         block_ref[i] = value
 
 
-def make_join(stride, count):
+def facing(near, far, stride):
+    return jnp.where(spot_in(stride, 2) == 0, far, near)
+
+
+def make_join(stride, count, two_left):
     def join(*refs):
         arrivals, (joined_ref, steps_ref, scratch) = refs[:count], refs[count:]
         place(scratch, arrivals, stride)
         joined, steps = combine([[scratch[i, j] for j in range(5)] for i in range(count)])
+        if two_left:
+            _, near_ground, far_ground, near_load, far_load = joined
+            joined = [
+                facing(near_ground, far_ground, stride * count),
+                facing(near_load, far_load, stride * count),
+            ]
         for i, value in enumerate(joined):
             joined_ref[i] = value
         keep_steps(steps_ref, steps)
@@ -309,9 +319,14 @@
         lower, (faces_ref, steps_ref, scratch, edges) = (
             refs[counts[-1]:counts[-1] + below], refs[counts[-1] + below:]
         )
-        place(scratch, arrivals, strides[-1])
         nothing = jnp.zeros(faces_ref.shape[1:], f32)
-        _, steps = combine([[scratch[i, j] for j in range(5)] for i in range(counts[-1])])
+        if counts[-1] == 2:
+            ground, load = [arrivals[0][i] + arrivals[1][i] for i in range(2)]
+            inverse = 1.0 / ground
+            steps = [(inverse, nothing, nothing, inverse * load)]
+        else:
+            place(scratch, arrivals, strides[-1])
+            _, steps = combine([[scratch[i, j] for j in range(5)] for i in range(counts[-1])])
         keep_steps(steps_ref, steps)
         levels = [(strides[-1], steps)] + [
             (strides[i], steps_of(lower[i])) for i in reversed(range(below))
@@ -385,40 +400,57 @@
     return ref[i * per:(i + 1) * per].reshape(per * ref.shape[1], lanes)
 
 
-def make_z_factor(cuts, first, last, total):
-    def z_factor(*refs):
-        if first == 0:
-            cond, storage, from_back, from_ahead, links, grounds = refs
-            for i in range(cuts):
-                here = piece_of(cond, i, cuts)
-                ending, after = z_links(here)
-                links[i] = jnp.where(ending, 0.0, harmonic(here, after))
-                grounds[i] = piece_of(storage, i, cuts)
-            links_in, grounds_in = links, grounds
-        else:
-            links_in, grounds_in, from_back, from_ahead, links, grounds = refs
-        for level in range(first, last):
-            shift = 1 << level
-            for i in range(cuts):
-                link, ground = links_in[i], grounds_in[i]
-                link_back = pltpu.roll(link, shift, 1)
-                inverse = 1.0 / (link + link_back + ground)
-                passed = inverse * link
-                from_back[level - first, i] = pltpu.roll(passed, shift, 1)
-                from_ahead[level - first, i] = link * pltpu.roll(inverse, lanes - shift, 1)
-                held = inverse * ground
-                grounds[i] = (
-                    ground
-                    + link * pltpu.roll(held, lanes - shift, 1)
-                    + link_back * pltpu.roll(held, shift, 1)
-                )
-                links[i] = link * pltpu.roll(passed, lanes - shift, 1)
-            links_in, grounds_in = links, grounds
-        if last == total:
-            for i in range(cuts):
-                grounds[i] = 1.0 / grounds[i]
-
-    return z_factor
+def turn_tiles(values, target):
+    values = values.reshape(target.shape)
+    for i in range(target.shape[0]):
+        target[i] = values[i].T
+
+
+def z_factor(cond, storage, cell_factors, joints, inverse_ref, cond_up, storage_up):
+    turn_tiles(cond[...], cond_up)
+    turn_tiles(storage[...], storage_up)
+    conds = y_cells(cond_up)
+    place_of = lax.broadcasted_iota(jnp.int32, conds[0].shape, 1)
+    near = jnp.where(place_of == 0, 0.0, 2.0 * conds[0])
+    far = jnp.where(place_of == chunks - 1, 0.0, 2.0 * conds[-1])
+    links = [harmonic(before, after) for before, after in zip(conds[:-1], conds[1:])] + [far]
+    nothing = [jnp.zeros_like(near)] * len(conds)
+    block, steps = eliminate(near, links, y_cells(storage_up), nothing)
+    keep_steps(cell_factors, [step[:3] for step in steps])
+    link = pltpu.roll(block[0], chunks - 1, 1)
+    ground = block[2] + pltpu.roll(block[1], chunks - 1, 1)
+    ground = jnp.where(place_of == chunks - 1, 1.0, ground)
+    for level in range(chunks.bit_length() - 1):
+        shift = 1 << level
+        link_back = pltpu.roll(link, shift, 1)
+        inverse = 1.0 / (link + link_back + ground)
+        passed, held = inverse * link, inverse * ground
+        joints[level, 0] = pltpu.roll(passed, shift, 1)
+        joints[level, 1] = link * pltpu.roll(inverse, chunks - shift, 1)
+        ground = (
+            ground
+            + link * pltpu.roll(held, chunks - shift, 1)
+            + link_back * pltpu.roll(held, shift, 1)
+        )
+        link = link * pltpu.roll(passed, chunks - shift, 1)
+    inverse_ref[...] = 1.0 / ground
+
+
+def z_sweep(loads, cell_factors, joints, inverse, solved):
+    factors = factors_of(cell_factors)
+    near, far, scaled = eliminate_loads(factors, y_cells(loads))
+    load = far + pltpu.roll(near, chunks - 1, 1)
+    for level in range(joints.shape[0]):
+        shift = 1 << level
+        load = (
+            load
+            + joints[level, 1] * pltpu.roll(load, chunks - shift, 1)
+            + joints[level, 0] * pltpu.roll(load, shift, 1)
+        )
+    far = load * inverse[...]
+    near = pltpu.roll(far, 1, 1)
+    for spot, value in enumerate(expand(with_scaled(factors, scaled), near, far)):
+        solved[y_rows(solved, spot)] = value
 
 
 def make_points(slab, rows):
@@ -480,30 +512,14 @@
         natural[y_rows(natural, spot)] = far
 
 
-def z_sweep(loads, parts):
-    level = 0
-    for from_back, from_ahead in parts:
-        for part in range(from_back.shape[0]):
-            shift = 1 << level
-            level = level + 1
-            for i in range(from_back.shape[1]):
-                load = loads[i]
-                loads[i] = (
-                    load
-                    + from_ahead[part, i] * pltpu.roll(load, lanes - shift, 1)
-                    + from_back[part, i] * pltpu.roll(load, shift, 1)
-                )
-
-
-def make_z(count, cuts, split):
+def make_z(count):
     def z_solve(*refs):
-        arrivals, tables = refs[:count], refs[count:count + 2 * split]
-        sweeps = [(tables[2 * i], tables[2 * i + 1]) for i in range(split)]
+        arrivals = refs[:count]
         (cell_factors, chunk_factors, scaled_cells, scaled_chunks, storage,
-         inverse, at_row, at_depth, here, observed,
-         y_factors, head_second, y_edges, head_third, head_send, adjoint_third, message,
+         z_factors, joints, inverse, at_row, at_depth, here, observed,
+         y_factors, head_second, y_edges, head_up, adjoint_third, message,
          next_cells, next_chunks,
-         scratch, edges, turned, loads, second, third) = refs[count + 2 * split:]
+         scratch, edges, turned, loads, second) = refs[count:]
         me = row_block()
         for turn, arrival in enumerate(arrivals):
             scratch[me ^ turn] = arrival[...]
@@ -514,19 +530,16 @@
         y_expand(near, far, cell_factors, chunk_factors, scaled_cells, scaled_chunks,
                  turned, head_second, y_edges, second)
 
-        slab, rows, _ = storage.shape
-        per = slab // cuts
-        piece = per * rows
-        for i in range(cuts):
-            loads[i] = piece_of(storage, i, cuts) * piece_of(second, i, cuts)
-        z_sweep(loads, sweeps)
-        for i in range(cuts):
-            head = loads[i] * inverse[i]
-            head_third[i * per:(i + 1) * per] = head.reshape(per, rows, lanes)
-            for j, part in enumerate(bf16_parts(head, 2)):
-                third[pl.ds(i * piece, piece), j * lanes:(j + 1) * lanes] = part
-        found = lax.dot_general(
-            third[...], at_row[...], (((0,), (0,)), ((), ())), preferred_element_type=f32
+        slab = storage.shape[0]
+        turn_tiles(storage[...] * second[...], loads)
+        tiles = loads.shape[0]
+        z_sweep(loads, z_factors, joints, inverse, head_up)
+        found = jnp.dot(
+            jnp.concatenate(
+                bf16_parts(jnp.concatenate([head_up[i] for i in range(tiles)], axis=1), 2), axis=0
+            ),
+            at_row[...],
+            preferred_element_type=f32,
         )
         found = jnp.sum(
             at_depth[...] * (found[:lanes] + found[lanes:]), axis=0, keepdims=True
@@ -535,29 +548,32 @@
         for i in range(misfit.shape[1] // lanes):
             row = 2 * slab + i
             message[row:row + 1, :] = misfit[:, i * lanes:(i + 1) * lanes]
-        cells = slab // 2
-        head_send[...] = head_third[pl.ds((1 - side()) * cells, cells)]
         parts = [
             (at_depth[...] * part.astype(f32)).astype(jnp.bfloat16)
             for part in bf16_parts(misfit_weight * misfit, 2)
         ]
         source = lax.dot_general(
-            at_row[...], jnp.concatenate(parts, axis=0),
+            jnp.concatenate(parts, axis=0), at_row[...],
             (((1,), (1,)), ((), ())), preferred_element_type=f32,
         )
-        for i in range(cuts):
-            part = source[i * piece:(i + 1) * piece]
-            loads[i] = part[:, :lanes] + part[:, lanes:]
-        z_sweep(loads, sweeps)
-        for i in range(cuts):
-            adjoint = (loads[i] * inverse[i]).reshape(per, rows, lanes)
-            adjoint_third[i * per:(i + 1) * per] = adjoint
-            second[i * per:(i + 1) * per] = storage[i * per:(i + 1) * per] * adjoint
+        for i in range(tiles):
+            tile = slice(i * lanes, (i + 1) * lanes)
+            loads[i] = source[:lanes, tile] + source[lanes:, tile]
+        z_sweep(loads, z_factors, joints, inverse, loads)
+        adjoint_third[...] = jnp.stack([loads[i].T for i in range(tiles)]).reshape(second.shape)
+        second[...] = storage[...] * adjoint_third[...]
         near, far = y_loads(second, cell_factors, chunk_factors, next_cells, next_chunks, turned)
         message[:slab] = near
         message[slab:2 * slab] = far
 
     return z_solve
+
+
+def lay_head(head_up, head_third, head_send):
+    cells = head_send.shape[0]
+    tiles = head_up.shape[0]
+    head_third[...] = jnp.stack([head_up[i].T for i in range(tiles)]).reshape(head_third.shape)
+    head_send[...] = head_third[pl.ds((1 - side()) * cells, cells)]
 
 
 def make_y_back(count):
@@ -653,15 +669,19 @@
     return [[scratch[i, 0], scratch[i, 1]] for i in range(count)], misfit
 
 
-def make_join_loads(stride, count):
+def make_join_loads(stride, count, two_left):
     def join(*refs):
         arrivals, (steps_ref, message, scaled_ref, scratch) = refs[:count], refs[count:]
         blocks, misfit = loads_in(arrivals, scratch, stride)
         joined, scaled = combine_loads(blocks, factors_of(steps_ref))
         rows = scratch.shape[2]
-        message[:rows] = joined[0]
-        message[rows:2 * rows] = joined[1]
-        message[2 * rows:] = misfit
+        if two_left:
+            message[:rows] = facing(*joined, stride * count)
+            message[rows:] = misfit
+        else:
+            message[:rows] = joined[0]
+            message[rows:2 * rows] = joined[1]
+            message[2 * rows:] = misfit
         for i, value in enumerate(scaled):
             scaled_ref[i] = value
 
@@ -675,10 +695,16 @@
         arrivals, refs = refs[:counts[-1]], refs[counts[-1]:]
         top_steps, lower, lower_scaled = refs[0], refs[1:1 + below], refs[1 + below:1 + 2 * below]
         faces_ref, misfit_ref, scratch, edges = refs[1 + 2 * below:]
-        blocks, misfit = loads_in(arrivals, scratch, strides[-1])
         nothing = jnp.zeros(scratch.shape[2:], f32)
         factors = factors_of(top_steps)
-        levels = [(strides[-1], with_scaled(factors, combine_loads(blocks, factors)[1]))]
+        if counts[-1] == 2:
+            rows = nothing.shape[0]
+            total = arrivals[0][...] + arrivals[1][...]
+            scaled, misfit = [factors[0][0] * total[:rows]], total[rows:]
+        else:
+            blocks, misfit = loads_in(arrivals, scratch, strides[-1])
+            scaled = combine_loads(blocks, factors)[1]
+        levels = [(strides[-1], with_scaled(factors, scaled))]
         for i in reversed(range(below)):
             factors = factors_of(lower[i])
             scaled = [lower_scaled[i][j] for j in range(len(factors))]
@@ -737,6 +763,7 @@
     devices, columns = lax.axis_size("gx"), lax.axis_size("yz")
     inner = 4 if devices >= 16 else 2
     strides, counts = [1, 2, 2 * inner], [2, inner, devices // (2 * inner)]
+    two_left = counts[-1] == 2
     slab, half = 2 * cells, rows // 2
     points = probe_heads.shape[0]
     grid = (slab, half, lanes)
@@ -775,28 +802,26 @@
     )
 
     cuts = 4
-    piece = (cuts, slab * half // cuts, lanes)
-    levels = lanes.bit_length() - 1
-    bounds = [0, 4, levels]
-    split = len(bounds) - 1
-    carried, z_parts, waits = [cond, storage], [], []
+    tiles = slab * half // lanes
+    upright = (tiles, lanes, lanes)
+    z_cell = (tiles, chunks, lanes)
     for i, (stride, count) in enumerate(zip(strides[1:], counts[1:])):
         arrivals = exchange(joined, stride, count)
-        waits = [ends]
-        if i < split:
-            first, last = bounds[i:i + 2]
-            from_back, from_ahead, *carried = run(
-                make_z_factor(cuts, first, last, levels),
-                [(last - first,) + piece] * 2 + [piece] * 2,
-                carried,
+        waits = []
+        if i == 0:
+            z_factors, joints, inverse = run(
+                z_factor,
+                [(lanes // chunks, 3) + z_cell, (chunks.bit_length() - 1, 2) + z_cell, z_cell],
+                [cond, storage],
+                [(upright, f32), (upright, f32)],
                 after=[joined],
             )
-            z_parts += [from_back, from_ahead]
-            waits.append(carried[1])
+            waits = [ends, inverse]
         if i < len(strides) - 2:
             joined, steps = run(
-                make_join(stride, count),
-                [(5,) + plane, (count - 1, 4) + plane],
+                make_join(stride, count, i == len(strides) - 3 and two_left),
+                [(2 if i == len(strides) - 3 and two_left else 5,) + plane,
+                 (count - 1, 4) + plane],
                 arrivals,
                 [((count, 5) + plane, f32)],
                 after=waits,
@@ -810,7 +835,6 @@
         after=waits,
     )
     x_levels.append(steps)
-    inverse = carried[1]
     head_first, scaled_cells, scaled_chunks, message = run(
         y_forward,
         [grid, cell, (chunks - 1,) + line, (5,) + line],
@@ -824,17 +848,19 @@
         after=[message],
     )
     extra, blocks = points // lanes, 2 * columns
-    (y_factors, head_second, head_edges, head_third, head_send, adjoint_third, message,
+    (y_factors, head_second, head_edges, head_up, adjoint_third, message,
      scaled_cells, scaled_chunks) = run(
-        make_z(blocks, cuts, split),
-        [(blocks - 1, 3) + line, cell, (2,) + cell[1:], grid, (cells,) + plane, grid,
+        make_z(blocks),
+        [(blocks - 1, 3) + line, cell, (2,) + cell[1:], upright, grid,
          (2 * slab + extra, lanes), cell, (chunks - 1,) + line],
         exchange_rows(message)
-        + z_parts
         + [cell_factors, chunk_factors, scaled_cells, scaled_chunks, storage,
-           inverse, at_row, at_depth, here, observed],
+           z_factors, joints, inverse, at_row, at_depth, here, observed],
         [((blocks, 5) + line, f32), ((blocks + 1,) + line, f32), ((2,) + turned, f32),
-         (piece, f32), (grid, f32), ((slab * half, 2 * lanes), jnp.bfloat16)],
+         (upright, f32), (grid, f32)],
+    )
+    head_third, head_send = run(
+        lay_head, [grid, (cells,) + plane], [head_up], after=[message]
     )
     note = (2 * half + extra, lanes)
     adjoint_second, adjoint_edges, scaled_x, scaled, message = run(
@@ -856,8 +882,9 @@
     for i in range(1, len(strides) - 1):
         arrivals = exchange(message, strides[i], counts[i])
         message, scaled = run(
-            make_join_loads(strides[i], counts[i]),
-            [note, (counts[i] - 1,) + plane],
+            make_join_loads(strides[i], counts[i], i == len(strides) - 2 and two_left),
+            [(half + extra, lanes) if i == len(strides) - 2 and two_left else note,
+             (counts[i] - 1,) + plane],
             arrivals + [x_levels[i]],
             [((counts[i], 2) + plane, f32)],
         )

time: 47.6 us -> 43.9 us (0.922)
  Pallas kernels: 13.9 us -> 7.66 us
  waiting for transfers between devices: 13.7 us -> 16.7 us
    pallas_call x18, Pallas kernels: 13.9 us -> 7.66 us  [run(): pl.pallas_call(ordered, out_shape=shapes, in_specs=[pl.BlockSpec(memory_s...]
    ppermute x13, waiting for transfers between devices: 8.56 us -> 11.5 us  [exchange(): lax.ppermute(value, 'gx', [(i, i ^ turn * stride) for i in range(size)])]
  transfers between devices with their start and end apart: 19 -> 19, of which waited for: 14 -> 15; matrix products, arithmetic and copies ran while one was open for 0% -> 0% of each run, Pallas kernels for 16% -> 7%
where the time goes in v3:
time: 43.9 us; the launch traced here: 43.8 us
  starting transfers between devices  18.5 us (42%)
  waiting for transfers between devices  16.7 us (38%)
  Pallas kernels  7.66 us (17%)
  between operations  0.82 us (2%)
    ppermute x13, starting transfers between devices, exchange(): lax.ppermute(value, 'gx', [(i, i ^ turn * stride) for i in range(size)])  14.6 us
    ppermute x13, waiting for transfers between devices, exchange(): lax.ppermute(value, 'gx', [(i, i ^ turn * stride) for i in range(size)])  11.5 us
    pallas_call x18, Pallas kernels, run(): pl.pallas_call(ordered, out_shape=shapes, in_specs=[pl.BlockSpec(memory_s...  7.66 us
    ppermute x6, waiting for transfers between devices, exchange_rows(): lax.ppermute(value, ('gx', 'yz'), [(i * columns + j, (i ^ turn % 2) * col...  5.15 us
    ppermute x6, starting transfers between devices, exchange_rows(): lax.ppermute(value, ('gx', 'yz'), [(i * columns + j, (i ^ turn % 2) * col...  3.85 us
  transfers between devices with their start and end apart: 19, of which 15 were waited for; matrix products, arithmetic and copies ran while one was open for 0% of the time, Pallas kernels for 7%

profile of v3, /device:TPU:0, one launch (start us, length us, event | category | flops | bytes accessed | tf_op | source)
XLA Modules:
  0.0 43.8 jit_solution(9135558020272500447)
XLA Ops:
  0.6 1.3 %shard_map.130 = (f32[8,32,128]{2,1,0:T(8,128)S(1)}, f32[8,32,128]{2,1,0:T(8,128)S(1)}, f32[8,32,128]{2,1,0:T(8,128)S(1)}, f32[8,32,128]{2,1,0:T(8,128)S(1)}, f3...) custom-call(f32[8,64,128]{2,1,0:T(8,128)} %refs_0_.1, f32[8,64,128]{2,1,0:T(8,128)} %refs_1_.1, f32[8,64,128]{2,1,0:T(8,128)} %refs_2_.1), custom_call_target="tpu_custom_call" | custom-call | flops 1000000 | bytes 1572864 | tf_op jit(solution)/shard_map/pallas_call | solution.py:128
  1.9 0.5 %collective-permute-start.1 = (f32[8,32,128]{2,1,0:T(8,128)S(1)}, f32[8,32,128]{2,1,0:T(8,128)S(1)}, u32[]{:S(2)}, u32[]{:S(2)}) collective-permute-start(f32[8,32,128]{2,1,0:T(8,128)S(1)} %get-tuple-element.59), channel_id=1, source_target_pairs={{0,2},{2,0},{4,6},{6,4},{8,10},{10,8},{12,14},{14,12},{16,18},{18,... | collective-permute-start | bytes 393224 | tf_op jit(solution)/shard_map/ppermute | solution.py:154
  2.6 0.5 %collective-permute-start = (f32[8,32,128]{2,1,0:T(8,128)S(1)}, f32[8,32,128]{2,1,0:T(8,128)S(1)}, u32[]{:S(2)}, u32[]{:S(2)}) collective-permute-start(f32[8,32,128]{2,1,0:T(8,128)S(1)} %get-tuple-element.58.refs_2_), channel_id=1, source_target_pairs={{0,2},{2,0},{4,6},{6,4},{8,10},{10,8},{12,14},{14,12},{16,18},{18,... | collective-permute-start | bytes 393224 | tf_op jit(solution)/shard_map/ppermute | solution.py:154
  3.4 0.4 collective-permute-done.2.refs_5_
  4.0 0.4 shard_map.132
  4.4 3.9 %collective-permute-start.5 = (f32[5,32,128]{2,1,0:T(8,128)S(1)}, f32[5,32,128]{2,1,0:T(8,128)S(1)}, u32[]{:S(2)}, u32[]{:S(2)}) collective-permute-start(f32[5,32,128]{2,1,0:T(8,128)S(1)} %get-tuple-element.61.refs_2_.refs_0_), channel_id=1, source_target_pairs={{0,12},{2,14},{4,8},{6,10},{8,4},{10,6},{12,0},{14,2},{16,28},{18,... | collective-permute-start | bytes 245768 | tf_op jit(solution)/shard_map/ppermute | solution.py:154
  8.3 0.4 %collective-permute-start.4 = (f32[5,32,128]{2,1,0:T(8,128)S(1)}, f32[5,32,128]{2,1,0:T(8,128)S(1)}, u32[]{:S(2)}, u32[]{:S(2)}) collective-permute-start(f32[5,32,128]{2,1,0:T(8,128)S(1)} %get-tuple-element.61.refs_2_.refs_0_), channel_id=1, source_target_pairs={{0,8},{2,10},{4,12},{6,14},{8,0},{10,2},{12,4},{14,6},{16,24},{18,... | collective-permute-start | bytes 245768 | tf_op jit(solution)/shard_map/ppermute | solution.py:154
  9.0 0.4 shard_map.134
  9.7 1.8 %collective-permute-done.5.refs_3_ = f32[5,32,128]{2,1,0:T(8,128)S(1)} collective-permute-done((f32[5,32,128]{2,1,0:T(8,128)S(1)}, f32[5,32,128]{2,1,0:T(8,128)S(1)}, u32[]{:S(2)}, u32[]{:S(2)}) %collective-permute-start.5) | collective-permute-done | bytes 81952 | tf_op jit(solution)/shard_map/ppermute | solution.py:154
  11.5 1.6 %collective-permute-done.4.refs_2_ = f32[5,32,128]{2,1,0:T(8,128)S(1)} collective-permute-done((f32[5,32,128]{2,1,0:T(8,128)S(1)}, f32[5,32,128]{2,1,0:T(8,128)S(1)}, u32[]{:S(2)}, u32[]{:S(2)}) %collective-permute-start.4) | collective-permute-done | bytes 81952 | tf_op jit(solution)/shard_map/ppermute | solution.py:154
  13.3 2.7 %collective-permute-start.6 = (f32[2,32,128]{2,1,0:T(8,128)S(1)}, f32[2,32,128]{2,1,0:T(8,128)S(1)}, u32[]{:S(2)}, u32[]{:S(2)}) collective-permute-start(f32[2,32,128]{2,1,0:T(8,128)S(1)} %get-tuple-element.66.refs_0_), channel_id=1, source_target_pairs={{0,16},{2,18},{4,20},{6,22},{8,24},{10,26},{12,28},{14,30},{16,0},... | collective-permute-start | bytes 98312 | tf_op jit(solution)/shard_map/ppermute | solution.py:154
  16.0 2.2 %collective-permute-done.6.refs_1_ = f32[2,32,128]{2,1,0:T(8,128)S(1)} collective-permute-done((f32[2,32,128]{2,1,0:T(8,128)S(1)}, f32[2,32,128]{2,1,0:T(8,128)S(1)}, u32[]{:S(2)}, u32[]{:S(2)}) %collective-permute-start.6) | collective-permute-done | bytes 32800 | tf_op jit(solution)/shard_map/ppermute | solution.py:154
  18.5 1.6 %collective-permute-start.8 = (f32[5,16,128]{2,1,0:T(8,128)S(1)}, f32[5,16,128]{2,1,0:T(8,128)S(1)}, u32[]{:S(2)}, u32[]{:S(2)}) collective-permute-start(f32[5,16,128]{2,1,0:T(8,128)S(1)} %get-tuple-element.73.refs_4_.refs_0_), channel_id=1, source_target_pairs={{0,1},{1,0},{2,3},{3,2},{4,5},{5,4},{6,7},{7,6},{8,9},{9,8},{10,11... | collective-permute-start | bytes 122888 | tf_op jit(solution)/shard_map/ppermute | solution.py:166
  20.7 1.7 %collective-permute-done.9.refs_3_ = f32[5,16,128]{2,1,0:T(8,128)S(1)} collective-permute-done((f32[5,16,128]{2,1,0:T(8,128)S(1)}, f32[5,16,128]{2,1,0:T(8,128)S(1)}, u32[]{:S(2)}, u32[]{:S(2)}) %collective-permute-start.9) | collective-permute-done | bytes 40992 | tf_op jit(solution)/shard_map/ppermute | solution.py:166
  22.4 0.6 %collective-permute-done.8.refs_2_ = f32[5,16,128]{2,1,0:T(8,128)S(1)} collective-permute-done((f32[5,16,128]{2,1,0:T(8,128)S(1)}, f32[5,16,128]{2,1,0:T(8,128)S(1)}, u32[]{:S(2)}, u32[]{:S(2)}) %collective-permute-start.8) | collective-permute-done | bytes 40992 | tf_op jit(solution)/shard_map/ppermute | solution.py:166
  22.9 1.8 %shard_map.139 = (f32[3,3,16,128]{3,2,1,0:T(8,128)S(1)}, f32[4,16,8,128]{3,2,1,0:T(8,128)S(1)}, f32[2,16,8,128]{3,2,1,0:T(8,128)S(1)}, f32[4,128,128]{2,1,0:T(8,...) custom-call(f32[5,16,128]{2,1,0:T(8,128)S(1)} %get-tuple-element.73., ...), custom_call_target="tpu_custom_call" | custom-call | flops 1000000 | bytes 6565888 | tf_op jit(solution)/shard_map/pallas_call | solution.py:128
  24.7 1.0 %collective-permute-start.13 = (f32[40,128]{1,0:T(8,128)S(1)}, f32[40,128]{1,0:T(8,128)S(1)}, u32[]{:S(2)}, u32[]{:S(2)}) collective-permute-start(f32[40,128]{1,0:T(8,128)S(1)} %get-tuple-element.83.refs_1_.refs_0_), channel_id=1, source_target_pairs={{0,3},{1,2},{2,1},{3,0},{4,7},{5,6},{6,5},{7,4},{8,11},{9,10},{10,... | collective-permute-start | bytes 61448 | tf_op jit(solution)/shard_map/ppermute | solution.py:166
  25.7 0.9 %collective-permute-start.12 = (f32[40,128]{1,0:T(8,128)S(1)}, f32[40,128]{1,0:T(8,128)S(1)}, u32[]{:S(2)}, u32[]{:S(2)}) collective-permute-start(f32[40,128]{1,0:T(8,128)S(1)} %get-tuple-element.83.refs_1_.refs_0_), channel_id=1, source_target_pairs={{0,1},{1,0},{2,3},{3,2},{4,5},{5,4},{6,7},{7,6},{8,9},{9,8},{10,11... | collective-permute-start | bytes 61448 | tf_op jit(solution)/shard_map/ppermute | solution.py:166
  26.6 1.3 %collective-permute-done.13.refs_3_ = f32[40,128]{1,0:T(8,128)S(1)} collective-permute-done((f32[40,128]{1,0:T(8,128)S(1)}, f32[40,128]{1,0:T(8,128)S(1)}, u32[]{:S(2)}, u32[]{:S(2)}) %collective-permute-start.13) | collective-permute-done | bytes 20512 | tf_op jit(solution)/shard_map/ppermute | solution.py:166
  28.0 1.5 %collective-permute-done.12.refs_2_ = f32[40,128]{1,0:T(8,128)S(1)} collective-permute-done((f32[40,128]{1,0:T(8,128)S(1)}, f32[40,128]{1,0:T(8,128)S(1)}, u32[]{:S(2)}, u32[]{:S(2)}) %collective-permute-start.12) | collective-permute-done | bytes 20512 | tf_op jit(solution)/shard_map/ppermute | solution.py:166
  29.7 2.4 %collective-permute-start.16 = (f32[72,128]{1,0:T(8,128)S(1)}, f32[72,128]{1,0:T(8,128)S(1)}, u32[]{:S(2)}, u32[]{:S(2)}) collective-permute-start(f32[72,128]{1,0:T(8,128)S(1)} %get-tuple-element.89.refs_0_), channel_id=1, source_target_pairs={{0,12},{2,14},{4,8},{6,10},{8,4},{10,6},{12,0},{14,2},{16,28},{18,... | collective-permute-start | bytes 110600 | tf_op jit(solution)/shard_map/ppermute | solution.py:154
  32.1 0.5 %collective-permute-start.15 = (f32[72,128]{1,0:T(8,128)S(1)}, f32[72,128]{1,0:T(8,128)S(1)}, u32[]{:S(2)}, u32[]{:S(2)}) collective-permute-start(f32[72,128]{1,0:T(8,128)S(1)} %get-tuple-element.89.refs_0_), channel_id=1, source_target_pairs={{0,8},{2,10},{4,12},{6,14},{8,0},{10,2},{12,4},{14,6},{16,24},{18,... | collective-permute-start | bytes 110600 | tf_op jit(solution)/shard_map/ppermute | solution.py:154
  32.6 0.7 %collective-permute-start.14 = (f32[72,128]{1,0:T(8,128)S(1)}, f32[72,128]{1,0:T(8,128)S(1)}, u32[]{:S(2)}, u32[]{:S(2)}) collective-permute-start(f32[72,128]{1,0:T(8,128)S(1)} %get-tuple-element.89.refs_0_), channel_id=1, source_target_pairs={{0,4},{2,6},{4,0},{6,2},{8,12},{10,14},{12,8},{14,10},{16,20},{18,... | collective-permute-start | bytes 110600 | tf_op jit(solution)/shard_map/ppermute | solution.py:154
  33.3 1.5 %collective-permute-done.16.refs_3_ = f32[72,128]{1,0:T(8,128)S(1)} collective-permute-done((f32[72,128]{1,0:T(8,128)S(1)}, f32[72,128]{1,0:T(8,128)S(1)}, u32[]{:S(2)}, u32[]{:S(2)}) %collective-permute-start.16) | collective-permute-done | bytes 36896 | tf_op jit(solution)/shard_map/ppermute | solution.py:154
  34.8 1.2 %collective-permute-done.15.refs_2_ = f32[72,128]{1,0:T(8,128)S(1)} collective-permute-done((f32[72,128]{1,0:T(8,128)S(1)}, f32[72,128]{1,0:T(8,128)S(1)}, u32[]{:S(2)}, u32[]{:S(2)}) %collective-permute-start.15) | collective-permute-done | bytes 36896 | tf_op jit(solution)/shard_map/ppermute | solution.py:154
  36.1 0.5 %collective-permute-done.14.refs_1_ = f32[72,128]{1,0:T(8,128)S(1)} collective-permute-done((f32[72,128]{1,0:T(8,128)S(1)}, f32[72,128]{1,0:T(8,128)S(1)}, u32[]{:S(2)}, u32[]{:S(2)}) %collective-permute-start.14) | collective-permute-done | bytes 36896 | tf_op jit(solution)/shard_map/ppermute | solution.py:154
  36.6 2.6 %collective-permute-start.17 = (f32[40,128]{1,0:T(8,128)S(1)}, f32[40,128]{1,0:T(8,128)S(1)}, u32[]{:S(2)}, u32[]{:S(2)}) collective-permute-start(f32[40,128]{1,0:T(8,128)S(1)} %get-tuple-element.90.refs_0_), channel_id=1, source_target_pairs={{0,16},{2,18},{4,20},{6,22},{8,24},{10,26},{12,28},{14,30},{16,0},... | collective-permute-start | bytes 61448 | tf_op jit(solution)/shard_map/ppermute | solution.py:154
  39.5 0.6 %shard_map.144.refs_7_.refs_6_ = f32[16,32,128]{2,1,0:T(8,128)S(1)} custom-call(f32[16,32,128]{2,1,0:T(8,128)S(1)} %get-tuple-element.62.refs_0_.refs_4_, f32[16,32,128]{2,1,0:T(8,128)S(1)} %get-tuple-element.84.refs_0_.refs_1_, f32[16,32,128]{2,1,0:T(8,128)S(1)} %get-tuple-element.94.refs_2_, f32[4,16,8,128]{3,2,1,0:T(8,128)S(1)} %get-tuple-element.95.refs_3_, ...), custom_call_target="tpu_custom_call" | custom-call | flops 1000000 | bytes 1835008 | tf_op jit(solution)/shard_map/pallas_call | solution.py:128
  40.0 1.3 %collective-permute-done.17.refs_1_ = f32[40,128]{1,0:T(8,128)S(1)} collective-permute-done((f32[40,128]{1,0:T(8,128)S(1)}, f32[40,128]{1,0:T(8,128)S(1)}, u32[]{:S(2)}, u32[]{:S(2)}) %collective-permute-start.17) | collective-permute-done | bytes 20512 | tf_op jit(solution)/shard_map/ppermute | solution.py:154
  41.7 0.8 %shard_map.141 = f32[8,64,128]{2,1,0:T(8,128)} custom-call(f32[16,32,128]{2,1,0:T(8,128)S(1)} %get-tuple-element.84.refs_0_.refs_1_, f32[8,32,128]{2,1,0:T(8,128)S(1)} %collective-permute-done.10.refs_1_), custom_call_target="tpu_custom_call" | custom-call | flops 1000000 | bytes 655360 | tf_op jit(solution)/shard_map/pallas_call | solution.py:128
  42.5 0.6 %collective-permute-done.18.refs_1_ = f32[8,32,128]{2,1,0:T(8,128)S(1)} collective-permute-done((f32[8,32,128]{2,1,0:T(8,128)S(1)}, f32[8,32,128]{2,1,0:T(8,128)S(1)}, u32[]{:S(2)}, u32[]{:S(2)}) %collective-permute-start.18) | collective-permute-done | bytes 131104 | tf_op jit(solution)/shard_map/ppermute | solution.py:154
  43.0 0.8 %shard_map.147 = (f32[8,64,128]{2,1,0:T(8,128)}, f32[8,128]{1,0:T(8,128)}) custom-call(f32[8,32,128]{2,1,0:T(8,128)S(1)} %get-tuple-element.102.refs_0_, f32[8,32,128]{2,1,0:T(8,128)S(1)} %collective-permute-done.18.refs_1_, f32[8,128]{1,0:T(8,128)S(1)} %get-tuple-element.104.refs_2_), custom_call_target="tpu_custom_call" | custom-call | flops 1000000 | bytes 532480 | tf_op jit(solution)/shard_map/pallas_call | solution.py:128
  (41 shorter events, 3.2 us)
Async XLA Ops:
  1.9 1.5 %collective-permute-start.1 = (f32[8,32,128]{2,1,0:T(8,128)S(1)}, f32[8,32,128]{2,1,0:T(8,128)S(1)}, u32[]{:S(2)}, u32[]{:S(2)}) collective-permute-start(f32[8,32,128]{2,1,0:T(8,128)S(1)} %get-tuple-element.59), channel_id=1, source_target_pairs={{0,2},{2,0},{4,6},{6,4},{8,10},{10,8},{12,14},{14,12},{16,18},{18,... | collective-permute-start | bytes 393224 | tf_op jit(solution)/shard_map/ppermute | solution.py:154
  2.4 0.7 %copy-start.7 = (s32[32]{0:T(128)S(1)}, s32[32]{0:T(128)}, u32[]{:S(2)}) copy-start(s32[32]{0:T(128)} %param.14) | copy-start | bytes 388
  2.4 0.7 %copy-start.4 = (f32[32]{0:T(128)S(1)}, f32[32]{0:T(128)}, u32[]{:S(2)}) copy-start(f32[32]{0:T(128)} %param.17) | copy-start | bytes 388
  2.4 0.7 %copy-start.5 = (s32[32]{0:T(128)S(1)}, s32[32]{0:T(128)}, u32[]{:S(2)}) copy-start(s32[32]{0:T(128)} %param.16) | copy-start | bytes 388
  2.4 0.7 %copy-start.6 = (s32[32]{0:T(128)S(1)}, s32[32]{0:T(128)}, u32[]{:S(2)}) copy-start(s32[32]{0:T(128)} %param.15) | copy-start | bytes 388
  2.4 1.4 %collective-permute-start.2 = (f32[8,32,128]{2,1,0:T(8,128)S(1)}, f32[8,32,128]{2,1,0:T(8,128)S(1)}, u32[]{:S(2)}, u32[]{:S(2)}) collective-permute-start(f32[8,32,128]{2,1,0:T(8,128)S(1)} %get-tuple-element.60), channel_id=1, source_target_pairs={{0,2},{2,0},{4,6},{6,4},{8,10},{10,8},{12,14},{14,12},{16,18},{18,... | collective-permute-start | bytes 393224 | tf_op jit(solution)/shard_map/ppermute | solution.py:154
  2.6 1.5 %collective-permute-start = (f32[8,32,128]{2,1,0:T(8,128)S(1)}, f32[8,32,128]{2,1,0:T(8,128)S(1)}, u32[]{:S(2)}, u32[]{:S(2)}) collective-permute-start(f32[8,32,128]{2,1,0:T(8,128)S(1)} %get-tuple-element.58.refs_2_), channel_id=1, source_target_pairs={{0,2},{2,0},{4,6},{6,4},{8,10},{10,8},{12,14},{14,12},{16,18},{18,... | collective-permute-start | bytes 393224 | tf_op jit(solution)/shard_map/ppermute | solution.py:154
  4.4 7.1 %collective-permute-start.5 = (f32[5,32,128]{2,1,0:T(8,128)S(1)}, f32[5,32,128]{2,1,0:T(8,128)S(1)}, u32[]{:S(2)}, u32[]{:S(2)}) collective-permute-start(f32[5,32,128]{2,1,0:T(8,128)S(1)} %get-tuple-element.61.refs_2_.refs_0_), channel_id=1, source_target_pairs={{0,12},{2,14},{4,8},{6,10},{8,4},{10,6},{12,0},{14,2},{16,28},{18,... | collective-permute-start | bytes 245768 | tf_op jit(solution)/shard_map/ppermute | solution.py:154
  8.3 4.7 %collective-permute-start.4 = (f32[5,32,128]{2,1,0:T(8,128)S(1)}, f32[5,32,128]{2,1,0:T(8,128)S(1)}, u32[]{:S(2)}, u32[]{:S(2)}) collective-permute-start(f32[5,32,128]{2,1,0:T(8,128)S(1)} %get-tuple-element.61.refs_2_.refs_0_), channel_id=1, source_target_pairs={{0,8},{2,10},{4,12},{6,14},{8,0},{10,2},{12,4},{14,6},{16,24},{18,... | collective-permute-start | bytes 245768 | tf_op jit(solution)/shard_map/ppermute | solution.py:154
  8.8 4.4 %collective-permute-start.3 = (f32[5,32,128]{2,1,0:T(8,128)S(1)}, f32[5,32,128]{2,1,0:T(8,128)S(1)}, u32[]{:S(2)}, u32[]{:S(2)}) collective-permute-start(f32[5,32,128]{2,1,0:T(8,128)S(1)} %get-tuple-element.61.refs_2_.refs_0_), channel_id=1, source_target_pairs={{0,4},{2,6},{4,0},{6,2},{8,12},{10,14},{12,8},{14,10},{16,20},{18,... | collective-permute-start | bytes 245768 | tf_op jit(solution)/shard_map/ppermute | solution.py:154
  13.3 4.9 %collective-permute-start.6 = (f32[2,32,128]{2,1,0:T(8,128)S(1)}, f32[2,32,128]{2,1,0:T(8,128)S(1)}, u32[]{:S(2)}, u32[]{:S(2)}) collective-permute-start(f32[2,32,128]{2,1,0:T(8,128)S(1)} %get-tuple-element.66.refs_0_), channel_id=1, source_target_pairs={{0,16},{2,18},{4,20},{6,22},{8,24},{10,26},{12,28},{14,30},{16,0},... | collective-permute-start | bytes 98312 | tf_op jit(solution)/shard_map/ppermute | solution.py:154
  18.2 2.2 %copy-start.2 = (s32[1024]{0:T(1024)S(1)}, s32[1024]{0:T(1024)}, u32[]{:S(2)}) copy-start(s32[1024]{0:T(1024)} %param.20) | copy-start | bytes 12292
  18.2 2.2 %copy-start.3 = (f32[1024]{0:T(1024)S(1)}, f32[1024]{0:T(1024)}, u32[]{:S(2)}) copy-start(f32[1024]{0:T(1024)} %param.21) | copy-start | bytes 12292
  18.4 2.0 %copy-start.1 = (s32[1024]{0:T(1024)S(1)}, s32[1024]{0:T(1024)}, u32[]{:S(2)}) copy-start(s32[1024]{0:T(1024)} %param.19) | copy-start | bytes 12292
  18.5 1.9 %copy-start = (s32[1024]{0:T(1024)S(1)}, s32[1024]{0:T(1024)}, u32[]{:S(2)}) copy-start(s32[1024]{0:T(1024)} %param.18) | copy-start | bytes 12292
  18.5 3.9 %collective-permute-start.9 = (f32[5,16,128]{2,1,0:T(8,128)S(1)}, f32[5,16,128]{2,1,0:T(8,128)S(1)}, u32[]{:S(2)}, u32[]{:S(2)}) collective-permute-start(f32[5,16,128]{2,1,0:T(8,128)S(1)} %get-tuple-element.73.refs_4_.refs_0_), channel_id=1, source_target_pairs={{0,3},{1,2},{2,1},{3,0},{4,7},{5,6},{6,5},{7,4},{8,11},{9,10},{10,... | collective-permute-start | bytes 122888 | tf_op jit(solution)/shard_map/ppermute | solution.py:166
  18.5 4.4 %collective-permute-start.8 = (f32[5,16,128]{2,1,0:T(8,128)S(1)}, f32[5,16,128]{2,1,0:T(8,128)S(1)}, u32[]{:S(2)}, u32[]{:S(2)}) collective-permute-start(f32[5,16,128]{2,1,0:T(8,128)S(1)} %get-tuple-element.73.refs_4_.refs_0_), channel_id=1, source_target_pairs={{0,1},{1,0},{2,3},{3,2},{4,5},{5,4},{6,7},{7,6},{8,9},{9,8},{10,11... | collective-permute-start | bytes 122888 | tf_op jit(solution)/shard_map/ppermute | solution.py:166
  20.1 2.8 %collective-permute-start.7 = (f32[5,16,128]{2,1,0:T(8,128)S(1)}, f32[5,16,128]{2,1,0:T(8,128)S(1)}, u32[]{:S(2)}, u32[]{:S(2)}) collective-permute-start(f32[5,16,128]{2,1,0:T(8,128)S(1)} %get-tuple-element.73.refs_4_.refs_0_), channel_id=1, source_target_pairs={{0,2},{1,3},{2,0},{3,1},{4,6},{5,7},{6,4},{7,5},{8,10},{9,11},{10,... | collective-permute-start | bytes 122888 | tf_op jit(solution)/shard_map/ppermute | solution.py:166
  24.7 3.3 %collective-permute-start.13 = (f32[40,128]{1,0:T(8,128)S(1)}, f32[40,128]{1,0:T(8,128)S(1)}, u32[]{:S(2)}, u32[]{:S(2)}) collective-permute-start(f32[40,128]{1,0:T(8,128)S(1)} %get-tuple-element.83.refs_1_.refs_0_), channel_id=1, source_target_pairs={{0,3},{1,2},{2,1},{3,0},{4,7},{5,6},{6,5},{7,4},{8,11},{9,10},{10,... | collective-permute-start | bytes 61448 | tf_op jit(solution)/shard_map/ppermute | solution.py:166
  25.7 3.8 %collective-permute-start.12 = (f32[40,128]{1,0:T(8,128)S(1)}, f32[40,128]{1,0:T(8,128)S(1)}, u32[]{:S(2)}, u32[]{:S(2)}) collective-permute-start(f32[40,128]{1,0:T(8,128)S(1)} %get-tuple-element.83.refs_1_.refs_0_), channel_id=1, source_target_pairs={{0,1},{1,0},{2,3},{3,2},{4,5},{5,4},{6,7},{7,6},{8,9},{9,8},{10,11... | collective-permute-start | bytes 61448 | tf_op jit(solution)/shard_map/ppermute | solution.py:166
  26.6 2.9 %collective-permute-start.11 = (f32[40,128]{1,0:T(8,128)S(1)}, f32[40,128]{1,0:T(8,128)S(1)}, u32[]{:S(2)}, u32[]{:S(2)}) collective-permute-start(f32[40,128]{1,0:T(8,128)S(1)} %get-tuple-element.83.refs_1_.refs_0_), channel_id=1, source_target_pairs={{0,2},{1,3},{2,0},{3,1},{4,6},{5,7},{6,4},{7,5},{8,10},{9,11},{10,... | collective-permute-start | bytes 61448 | tf_op jit(solution)/shard_map/ppermute | solution.py:166
  29.7 5.1 %collective-permute-start.16 = (f32[72,128]{1,0:T(8,128)S(1)}, f32[72,128]{1,0:T(8,128)S(1)}, u32[]{:S(2)}, u32[]{:S(2)}) collective-permute-start(f32[72,128]{1,0:T(8,128)S(1)} %get-tuple-element.89.refs_0_), channel_id=1, source_target_pairs={{0,12},{2,14},{4,8},{6,10},{8,4},{10,6},{12,0},{14,2},{16,28},{18,... | collective-permute-start | bytes 110600 | tf_op jit(solution)/shard_map/ppermute | solution.py:154
  32.1 4.0 %collective-permute-start.15 = (f32[72,128]{1,0:T(8,128)S(1)}, f32[72,128]{1,0:T(8,128)S(1)}, u32[]{:S(2)}, u32[]{:S(2)}) collective-permute-start(f32[72,128]{1,0:T(8,128)S(1)} %get-tuple-element.89.refs_0_), channel_id=1, source_target_pairs={{0,8},{2,10},{4,12},{6,14},{8,0},{10,2},{12,4},{14,6},{16,24},{18,... | collective-permute-start | bytes 110600 | tf_op jit(solution)/shard_map/ppermute | solution.py:154
  32.6 4.0 %collective-permute-start.14 = (f32[72,128]{1,0:T(8,128)S(1)}, f32[72,128]{1,0:T(8,128)S(1)}, u32[]{:S(2)}, u32[]{:S(2)}) collective-permute-start(f32[72,128]{1,0:T(8,128)S(1)} %get-tuple-element.89.refs_0_), channel_id=1, source_target_pairs={{0,4},{2,6},{4,0},{6,2},{8,12},{10,14},{12,8},{14,10},{16,20},{18,... | collective-permute-start | bytes 110600 | tf_op jit(solution)/shard_map/ppermute | solution.py:154
  36.6 4.7 %collective-permute-start.17 = (f32[40,128]{1,0:T(8,128)S(1)}, f32[40,128]{1,0:T(8,128)S(1)}, u32[]{:S(2)}, u32[]{:S(2)}) collective-permute-start(f32[40,128]{1,0:T(8,128)S(1)} %get-tuple-element.90.refs_0_), channel_id=1, source_target_pairs={{0,16},{2,18},{4,20},{6,22},{8,24},{10,26},{12,28},{14,30},{16,0},... | collective-permute-start | bytes 61448 | tf_op jit(solution)/shard_map/ppermute | solution.py:154
  39.4 2.3 %collective-permute-start.10 = (f32[8,32,128]{2,1,0:T(8,128)S(1)}, f32[8,32,128]{2,1,0:T(8,128)S(1)}, u32[]{:S(2)}, u32[]{:S(2)}) collective-permute-start(f32[8,32,128]{2,1,0:T(8,128)S(1)} %get-tuple-element.85), channel_id=1, source_target_pairs={{0,2},{2,0},{4,6},{6,4},{8,10},{10,8},{12,14},{14,12},{16,18},{18,... | collective-permute-start | bytes 393224 | tf_op jit(solution)/shard_map/ppermute | solution.py:154
  41.6 1.4 %collective-permute-start.18 = (f32[8,32,128]{2,1,0:T(8,128)S(1)}, f32[8,32,128]{2,1,0:T(8,128)S(1)}, u32[]{:S(2)}, u32[]{:S(2)}) collective-permute-start(f32[8,32,128]{2,1,0:T(8,128)S(1)} %get-tuple-element.103), channel_id=1, source_target_pairs={{0,2},{2,0},{4,6},{6,4},{8,10},{10,8},{12,14},{14,12},{16,18},{18,... | collective-permute-start | bytes 393224 | tf_op jit(solution)/shard_map/ppermute | solution.py:154

commit v4 on v3

--- a/solution.py
+++ b/solution.py
@@ -253,19 +253,22 @@
     return wells
 
 
-def x_reduce(*refs):
-    parts, (sources, cond, storage, steps_ref, pair_steps, block_ref, raw, loads) = (
-        refs[:6], refs[6:]
-    )
-    cells = cond.shape[0] // 2
-    for i in range(3):
-        raw[side(), i] = parts[i][...]
-        raw[1 - side(), i] = parts[3 + i][...]
-    for i in range(2):
-        part = slice(i * cells, (i + 1) * cells)
-        cond[part] = jnp.exp(raw[i, 0])
-        storage[part] = raw[i, 1]
-        loads[part] = raw[i, 1] * raw[i, 2] + sources[part]
+def x_prepare(log_cond, storage, head, sources, cond_own, load_own):
+    cells = log_cond.shape[0]
+    cond_own[...] = jnp.exp(log_cond[...])
+    load_own[...] = storage[...] * head[...] + sources[pl.ds(side() * cells, cells)]
+
+
+def x_reduce(cond_own, storage_own, load_own, log_cond_other, storage_other, head_other, sources,
+             cond, storage, steps_ref, pair_steps, block_ref, loads):
+    cells = cond_own.shape[0]
+    mine, rest = pl.ds(side() * cells, cells), pl.ds((1 - side()) * cells, cells)
+    cond[mine] = cond_own[...]
+    storage[mine] = storage_own[...]
+    loads[mine] = load_own[...]
+    cond[rest] = jnp.exp(log_cond_other[...])
+    storage[rest] = storage_other[...]
+    loads[rest] = storage_other[...] * head_other[...] + sources[rest]
     near, far = x_ends(cond)
     conds = [pair_cells(cond, i) for i in range(cells)]
     links = [harmonic(conds[i], conds[i + 1]) for i in range(cells - 1)] + [far]
@@ -744,17 +747,16 @@
     send[...] = gradient[pl.ds((1 - side()) * cells, cells)]
 
 
-def settle(own, other, whole, full):
+def settle(own, other, whole):
     cells, half, _ = other.shape
     start = (own.shape[0] - cells) // cells * side() * cells
-    full[:, pl.ds(pl.multiple_of(side() * half, half), half), :] = own[pl.ds(start, cells)]
-    full[:, pl.ds(pl.multiple_of((1 - side()) * half, half), half), :] = other[...]
-    whole[...] = full[...]
-
-
-def settle_last(own, other, misfits, whole, misfits_out, full):
+    whole[:, pl.ds(pl.multiple_of(side() * half, half), half), :] = own[pl.ds(start, cells)]
+    whole[:, pl.ds(pl.multiple_of((1 - side()) * half, half), half), :] = other[...]
+
+
+def settle_last(own, other, misfits, whole, misfits_out):
     misfits_out[...] = misfits[...]
-    settle(own, other, whole, full)
+    settle(own, other, whole)
 
 
 def shards(log_cond, storage, head, well_east, well_north, well_depth, pump_rates,
@@ -786,11 +788,14 @@
     (sources,) = run(
         make_wells(slab, half), [grid], [places, jnp.where(places >= 0, pump_rates.reshape(1, -1), 0.0)], after=[parts[3]]
     )
+    cond_own, load_own = run(
+        x_prepare, [(cells,) + plane] * 2, list(parts[:3]) + [sources], after=[parts[3]]
+    )
     cond, storage, x_steps, pair_steps, joined = run(
         x_reduce,
         [grid, grid, (cells, 4, 2) + plane, (1, 4) + plane, (5,) + plane],
-        list(parts[:3]) + [swap(part) for part in parts[3:]] + [sources],
-        [((2, 3, cells) + plane, f32), (grid, f32)],
+        [cond_own, parts[1], load_own] + [swap(part) for part in parts[3:]] + [sources],
+        [(grid, f32)],
     )
     x_levels = [pair_steps]
     cell_factors, chunk_factors, ends = run(
@@ -897,7 +902,7 @@
         after=[terms],
     )
     whole = (cells, rows, lanes)
-    (head_next,) = run(settle, [whole], [head_third, swap(head_send)], [(whole, f32)])
+    (head_next,) = run(settle, [whole], [head_third, swap(head_send)])
     own, send = run(
         x_back,
         [(cells,) + plane, (cells,) + plane],
@@ -905,7 +910,7 @@
         [(grid, f32)],
     )
     gradient, misfits = run(
-        settle_last, [whole, (extra, lanes)], [own, swap(send), misfits], [(whole, f32)]
+        settle_last, [whole, (extra, lanes)], [own, swap(send), misfits]
     )
     return head_next, gradient, misfits.reshape(-1)
 

time: 43.9 us -> 43.8 us (level)
    pallas_call x18 -> x19, Pallas kernels: 7.66 us -> 7.57 us  [run(): pl.pallas_call(ordered, out_shape=shapes, in_specs=[pl.BlockSpec(memory_s...]
where the time goes in v4:
time: 43.8 us; the launch traced here: 43.7 us
  starting transfers between devices  18.5 us (42%)
  waiting for transfers between devices  16.6 us (38%)
  Pallas kernels  7.57 us (17%)
  between operations  0.83 us (2%)
    ppermute x13, starting transfers between devices, exchange(): lax.ppermute(value, 'gx', [(i, i ^ turn * stride) for i in range(size)])  14.6 us
    ppermute x13, waiting for transfers between devices, exchange(): lax.ppermute(value, 'gx', [(i, i ^ turn * stride) for i in range(size)])  11.5 us
    pallas_call x19, Pallas kernels, run(): pl.pallas_call(ordered, out_shape=shapes, in_specs=[pl.BlockSpec(memory_s...  7.57 us
    ppermute x6, waiting for transfers between devices, exchange_rows(): lax.ppermute(value, ('gx', 'yz'), [(i * columns + j, (i ^ turn % 2) * col...  5.15 us
    ppermute x6, starting transfers between devices, exchange_rows(): lax.ppermute(value, ('gx', 'yz'), [(i * columns + j, (i ^ turn % 2) * col...  3.85 us
  transfers between devices with their start and end apart: 19, of which 15 were waited for; matrix products, arithmetic and copies ran while one was open for 0% of the time, Pallas kernels for 7%

profile of v4, /device:TPU:0, one launch (start us, length us, event | category | flops | bytes accessed | tf_op | source)
XLA Modules:
  0.0 43.7 jit_solution(3755273111628014471)
XLA Ops:
  0.6 1.3 %shard_map.130 = (f32[8,32,128]{2,1,0:T(8,128)S(1)}, f32[8,32,128]{2,1,0:T(8,128)S(1)}, f32[8,32,128]{2,1,0:T(8,128)S(1)}, f32[8,32,128]{2,1,0:T(8,128)S(1)}, f3...) custom-call(f32[8,64,128]{2,1,0:T(8,128)} %refs_0_.1, f32[8,64,128]{2,1,0:T(8,128)} %refs_1_.1, f32[8,64,128]{2,1,0:T(8,128)} %refs_2_.1), custom_call_target="tpu_custom_call" | custom-call | flops 1000000 | bytes 1572864 | tf_op jit(solution)/shard_map/pallas_call | solution.py:128
  1.9 0.5 %collective-permute-start.1 = (f32[8,32,128]{2,1,0:T(8,128)S(1)}, f32[8,32,128]{2,1,0:T(8,128)S(1)}, u32[]{:S(2)}, u32[]{:S(2)}) collective-permute-start(f32[8,32,128]{2,1,0:T(8,128)S(1)} %get-tuple-element.63), channel_id=1, source_target_pairs={{0,2},{2,0},{4,6},{6,4},{8,10},{10,8},{12,14},{14,12},{16,18},{18,... | collective-permute-start | bytes 393224 | tf_op jit(solution)/shard_map/ppermute | solution.py:154
  2.6 0.5 %collective-permute-start = (f32[8,32,128]{2,1,0:T(8,128)S(1)}, f32[8,32,128]{2,1,0:T(8,128)S(1)}, u32[]{:S(2)}, u32[]{:S(2)}) collective-permute-start(f32[8,32,128]{2,1,0:T(8,128)S(1)} %get-tuple-element.60.refs_2_.refs_4_), channel_id=1, source_target_pairs={{0,2},{2,0},{4,6},{6,4},{8,10},{10,8},{12,14},{14,12},{16,18},{18,... | collective-permute-start | bytes 393224 | tf_op jit(solution)/shard_map/ppermute | solution.py:154
  3.5 0.4 collective-permute-done.2.refs_5_
  4.0 0.3 shard_map.133
  4.3 3.9 %collective-permute-start.5 = (f32[5,32,128]{2,1,0:T(8,128)S(1)}, f32[5,32,128]{2,1,0:T(8,128)S(1)}, u32[]{:S(2)}, u32[]{:S(2)}) collective-permute-start(f32[5,32,128]{2,1,0:T(8,128)S(1)} %get-tuple-element.65.refs_2_.refs_0_), channel_id=1, source_target_pairs={{0,12},{2,14},{4,8},{6,10},{8,4},{10,6},{12,0},{14,2},{16,28},{18,... | collective-permute-start | bytes 245768 | tf_op jit(solution)/shard_map/ppermute | solution.py:154
  8.3 0.4 %collective-permute-start.4 = (f32[5,32,128]{2,1,0:T(8,128)S(1)}, f32[5,32,128]{2,1,0:T(8,128)S(1)}, u32[]{:S(2)}, u32[]{:S(2)}) collective-permute-start(f32[5,32,128]{2,1,0:T(8,128)S(1)} %get-tuple-element.65.refs_2_.refs_0_), channel_id=1, source_target_pairs={{0,8},{2,10},{4,12},{6,14},{8,0},{10,2},{12,4},{14,6},{16,24},{18,... | collective-permute-start | bytes 245768 | tf_op jit(solution)/shard_map/ppermute | solution.py:154
  8.9 0.4 shard_map.135
  9.6 1.8 %collective-permute-done.5.refs_3_ = f32[5,32,128]{2,1,0:T(8,128)S(1)} collective-permute-done((f32[5,32,128]{2,1,0:T(8,128)S(1)}, f32[5,32,128]{2,1,0:T(8,128)S(1)}, u32[]{:S(2)}, u32[]{:S(2)}) %collective-permute-start.5) | collective-permute-done | bytes 81952 | tf_op jit(solution)/shard_map/ppermute | solution.py:154
  11.4 1.6 %collective-permute-done.4.refs_2_ = f32[5,32,128]{2,1,0:T(8,128)S(1)} collective-permute-done((f32[5,32,128]{2,1,0:T(8,128)S(1)}, f32[5,32,128]{2,1,0:T(8,128)S(1)}, u32[]{:S(2)}, u32[]{:S(2)}) %collective-permute-start.4) | collective-permute-done | bytes 81952 | tf_op jit(solution)/shard_map/ppermute | solution.py:154
  13.2 2.7 %collective-permute-start.6 = (f32[2,32,128]{2,1,0:T(8,128)S(1)}, f32[2,32,128]{2,1,0:T(8,128)S(1)}, u32[]{:S(2)}, u32[]{:S(2)}) collective-permute-start(f32[2,32,128]{2,1,0:T(8,128)S(1)} %get-tuple-element.70.refs_0_), channel_id=1, source_target_pairs={{0,16},{2,18},{4,20},{6,22},{8,24},{10,26},{12,28},{14,30},{16,0},... | collective-permute-start | bytes 98312 | tf_op jit(solution)/shard_map/ppermute | solution.py:154
  15.9 2.2 %collective-permute-done.6.refs_1_ = f32[2,32,128]{2,1,0:T(8,128)S(1)} collective-permute-done((f32[2,32,128]{2,1,0:T(8,128)S(1)}, f32[2,32,128]{2,1,0:T(8,128)S(1)}, u32[]{:S(2)}, u32[]{:S(2)}) %collective-permute-start.6) | collective-permute-done | bytes 32800 | tf_op jit(solution)/shard_map/ppermute | solution.py:154
  18.5 1.6 %collective-permute-start.8 = (f32[5,16,128]{2,1,0:T(8,128)S(1)}, f32[5,16,128]{2,1,0:T(8,128)S(1)}, u32[]{:S(2)}, u32[]{:S(2)}) collective-permute-start(f32[5,16,128]{2,1,0:T(8,128)S(1)} %get-tuple-element.77.refs_4_.refs_0_), channel_id=1, source_target_pairs={{0,1},{1,0},{2,3},{3,2},{4,5},{5,4},{6,7},{7,6},{8,9},{9,8},{10,11... | collective-permute-start | bytes 122888 | tf_op jit(solution)/shard_map/ppermute | solution.py:166
  20.6 1.7 %collective-permute-done.9.refs_3_ = f32[5,16,128]{2,1,0:T(8,128)S(1)} collective-permute-done((f32[5,16,128]{2,1,0:T(8,128)S(1)}, f32[5,16,128]{2,1,0:T(8,128)S(1)}, u32[]{:S(2)}, u32[]{:S(2)}) %collective-permute-start.9) | collective-permute-done | bytes 40992 | tf_op jit(solution)/shard_map/ppermute | solution.py:166
  22.3 0.6 %collective-permute-done.8.refs_2_ = f32[5,16,128]{2,1,0:T(8,128)S(1)} collective-permute-done((f32[5,16,128]{2,1,0:T(8,128)S(1)}, f32[5,16,128]{2,1,0:T(8,128)S(1)}, u32[]{:S(2)}, u32[]{:S(2)}) %collective-permute-start.8) | collective-permute-done | bytes 40992 | tf_op jit(solution)/shard_map/ppermute | solution.py:166
  22.8 1.8 %shard_map.140 = (f32[3,3,16,128]{3,2,1,0:T(8,128)S(1)}, f32[4,16,8,128]{3,2,1,0:T(8,128)S(1)}, f32[2,16,8,128]{3,2,1,0:T(8,128)S(1)}, f32[4,128,128]{2,1,0:T(8,...) custom-call(f32[5,16,128]{2,1,0:T(8,128)S(1)} %get-tuple-element.77., ...), custom_call_target="tpu_custom_call" | custom-call | flops 1000000 | bytes 6565888 | tf_op jit(solution)/shard_map/pallas_call | solution.py:128
  24.6 1.0 %collective-permute-start.13 = (f32[40,128]{1,0:T(8,128)S(1)}, f32[40,128]{1,0:T(8,128)S(1)}, u32[]{:S(2)}, u32[]{:S(2)}) collective-permute-start(f32[40,128]{1,0:T(8,128)S(1)} %get-tuple-element.87.refs_1_.refs_0_), channel_id=1, source_target_pairs={{0,3},{1,2},{2,1},{3,0},{4,7},{5,6},{6,5},{7,4},{8,11},{9,10},{10,... | collective-permute-start | bytes 61448 | tf_op jit(solution)/shard_map/ppermute | solution.py:166
  25.6 0.9 %collective-permute-start.12 = (f32[40,128]{1,0:T(8,128)S(1)}, f32[40,128]{1,0:T(8,128)S(1)}, u32[]{:S(2)}, u32[]{:S(2)}) collective-permute-start(f32[40,128]{1,0:T(8,128)S(1)} %get-tuple-element.87.refs_1_.refs_0_), channel_id=1, source_target_pairs={{0,1},{1,0},{2,3},{3,2},{4,5},{5,4},{6,7},{7,6},{8,9},{9,8},{10,11... | collective-permute-start | bytes 61448 | tf_op jit(solution)/shard_map/ppermute | solution.py:166
  26.5 1.3 %collective-permute-done.13.refs_3_ = f32[40,128]{1,0:T(8,128)S(1)} collective-permute-done((f32[40,128]{1,0:T(8,128)S(1)}, f32[40,128]{1,0:T(8,128)S(1)}, u32[]{:S(2)}, u32[]{:S(2)}) %collective-permute-start.13) | collective-permute-done | bytes 20512 | tf_op jit(solution)/shard_map/ppermute | solution.py:166
  27.9 1.5 %collective-permute-done.12.refs_2_ = f32[40,128]{1,0:T(8,128)S(1)} collective-permute-done((f32[40,128]{1,0:T(8,128)S(1)}, f32[40,128]{1,0:T(8,128)S(1)}, u32[]{:S(2)}, u32[]{:S(2)}) %collective-permute-start.12) | collective-permute-done | bytes 20512 | tf_op jit(solution)/shard_map/ppermute | solution.py:166
  29.7 2.4 %collective-permute-start.16 = (f32[72,128]{1,0:T(8,128)S(1)}, f32[72,128]{1,0:T(8,128)S(1)}, u32[]{:S(2)}, u32[]{:S(2)}) collective-permute-start(f32[72,128]{1,0:T(8,128)S(1)} %get-tuple-element.93.refs_0_), channel_id=1, source_target_pairs={{0,12},{2,14},{4,8},{6,10},{8,4},{10,6},{12,0},{14,2},{16,28},{18,... | collective-permute-start | bytes 110600 | tf_op jit(solution)/shard_map/ppermute | solution.py:154
  32.0 0.5 %collective-permute-start.15 = (f32[72,128]{1,0:T(8,128)S(1)}, f32[72,128]{1,0:T(8,128)S(1)}, u32[]{:S(2)}, u32[]{:S(2)}) collective-permute-start(f32[72,128]{1,0:T(8,128)S(1)} %get-tuple-element.93.refs_0_), channel_id=1, source_target_pairs={{0,8},{2,10},{4,12},{6,14},{8,0},{10,2},{12,4},{14,6},{16,24},{18,... | collective-permute-start | bytes 110600 | tf_op jit(solution)/shard_map/ppermute | solution.py:154
  32.5 0.7 %collective-permute-start.14 = (f32[72,128]{1,0:T(8,128)S(1)}, f32[72,128]{1,0:T(8,128)S(1)}, u32[]{:S(2)}, u32[]{:S(2)}) collective-permute-start(f32[72,128]{1,0:T(8,128)S(1)} %get-tuple-element.93.refs_0_), channel_id=1, source_target_pairs={{0,4},{2,6},{4,0},{6,2},{8,12},{10,14},{12,8},{14,10},{16,20},{18,... | collective-permute-start | bytes 110600 | tf_op jit(solution)/shard_map/ppermute | solution.py:154
  33.2 1.5 %collective-permute-done.16.refs_3_ = f32[72,128]{1,0:T(8,128)S(1)} collective-permute-done((f32[72,128]{1,0:T(8,128)S(1)}, f32[72,128]{1,0:T(8,128)S(1)}, u32[]{:S(2)}, u32[]{:S(2)}) %collective-permute-start.16) | collective-permute-done | bytes 36896 | tf_op jit(solution)/shard_map/ppermute | solution.py:154
  34.8 1.2 %collective-permute-done.15.refs_2_ = f32[72,128]{1,0:T(8,128)S(1)} collective-permute-done((f32[72,128]{1,0:T(8,128)S(1)}, f32[72,128]{1,0:T(8,128)S(1)}, u32[]{:S(2)}, u32[]{:S(2)}) %collective-permute-start.15) | collective-permute-done | bytes 36896 | tf_op jit(solution)/shard_map/ppermute | solution.py:154
  36.0 0.5 %collective-permute-done.14.refs_1_ = f32[72,128]{1,0:T(8,128)S(1)} collective-permute-done((f32[72,128]{1,0:T(8,128)S(1)}, f32[72,128]{1,0:T(8,128)S(1)}, u32[]{:S(2)}, u32[]{:S(2)}) %collective-permute-start.14) | collective-permute-done | bytes 36896 | tf_op jit(solution)/shard_map/ppermute | solution.py:154
  36.5 2.6 %collective-permute-start.17 = (f32[40,128]{1,0:T(8,128)S(1)}, f32[40,128]{1,0:T(8,128)S(1)}, u32[]{:S(2)}, u32[]{:S(2)}) collective-permute-start(f32[40,128]{1,0:T(8,128)S(1)} %get-tuple-element.94.refs_0_), channel_id=1, source_target_pairs={{0,16},{2,18},{4,20},{6,22},{8,24},{10,26},{12,28},{14,30},{16,0},... | collective-permute-start | bytes 61448 | tf_op jit(solution)/shard_map/ppermute | solution.py:154
  39.4 0.6 %shard_map.145.refs_7_.refs_6_ = f32[16,32,128]{2,1,0:T(8,128)S(1)} custom-call(f32[16,32,128]{2,1,0:T(8,128)S(1)} %get-tuple-element.66.refs_0_.refs_4_, f32[16,32,128]{2,1,0:T(8,128)S(1)} %get-tuple-element.88.refs_0_.refs_1_, f32[16,32,128]{2,1,0:T(8,128)S(1)} %get-tuple-element.98.refs_2_, f32[4,16,8,128]{3,2,1,0:T(8,128)S(1)} %get-tuple-element.99.refs_3_, ...), custom_call_target="tpu_custom_call" | custom-call | flops 1000000 | bytes 1835008 | tf_op jit(solution)/shard_map/pallas_call | solution.py:128
  40.0 1.3 %collective-permute-done.17.refs_1_ = f32[40,128]{1,0:T(8,128)S(1)} collective-permute-done((f32[40,128]{1,0:T(8,128)S(1)}, f32[40,128]{1,0:T(8,128)S(1)}, u32[]{:S(2)}, u32[]{:S(2)}) %collective-permute-start.17) | collective-permute-done | bytes 20512 | tf_op jit(solution)/shard_map/ppermute | solution.py:154
  41.6 0.7 %shard_map.142 = f32[8,64,128]{2,1,0:T(8,128)} custom-call(f32[16,32,128]{2,1,0:T(8,128)S(1)} %get-tuple-element.88.refs_0_.refs_1_, f32[8,32,128]{2,1,0:T(8,128)S(1)} %collective-permute-done.10.refs_1_), custom_call_target="tpu_custom_call" | custom-call | flops 1000000 | bytes 655360 | tf_op jit(solution)/shard_map/pallas_call | solution.py:128
  42.4 0.6 %collective-permute-done.18.refs_1_ = f32[8,32,128]{2,1,0:T(8,128)S(1)} collective-permute-done((f32[8,32,128]{2,1,0:T(8,128)S(1)}, f32[8,32,128]{2,1,0:T(8,128)S(1)}, u32[]{:S(2)}, u32[]{:S(2)}) %collective-permute-start.18) | collective-permute-done | bytes 131104 | tf_op jit(solution)/shard_map/ppermute | solution.py:154
  42.9 0.7 %shard_map.148 = (f32[8,64,128]{2,1,0:T(8,128)}, f32[8,128]{1,0:T(8,128)}) custom-call(f32[8,32,128]{2,1,0:T(8,128)S(1)} %get-tuple-element.106.refs_0_, f32[8,32,128]{2,1,0:T(8,128)S(1)} %collective-permute-done.18.refs_1_, f32[8,128]{1,0:T(8,128)S(1)} %get-tuple-element.108.refs_2_), custom_call_target="tpu_custom_call" | custom-call | flops 1000000 | bytes 532480 | tf_op jit(solution)/shard_map/pallas_call | solution.py:128
  (42 shorter events, 3.2 us)
Async XLA Ops:
  1.9 1.6 %collective-permute-start.1 = (f32[8,32,128]{2,1,0:T(8,128)S(1)}, f32[8,32,128]{2,1,0:T(8,128)S(1)}, u32[]{:S(2)}, u32[]{:S(2)}) collective-permute-start(f32[8,32,128]{2,1,0:T(8,128)S(1)} %get-tuple-element.63), channel_id=1, source_target_pairs={{0,2},{2,0},{4,6},{6,4},{8,10},{10,8},{12,14},{14,12},{16,18},{18,... | collective-permute-start | bytes 393224 | tf_op jit(solution)/shard_map/ppermute | solution.py:154
  2.4 0.7 %copy-start.7 = (s32[32]{0:T(128)S(1)}, s32[32]{0:T(128)}, u32[]{:S(2)}) copy-start(s32[32]{0:T(128)} %param.14) | copy-start | bytes 388
  2.4 0.7 %copy-start.4 = (f32[32]{0:T(128)S(1)}, f32[32]{0:T(128)}, u32[]{:S(2)}) copy-start(f32[32]{0:T(128)} %param.17) | copy-start | bytes 388
  2.4 0.7 %copy-start.5 = (s32[32]{0:T(128)S(1)}, s32[32]{0:T(128)}, u32[]{:S(2)}) copy-start(s32[32]{0:T(128)} %param.16) | copy-start | bytes 388
  2.4 0.7 %copy-start.6 = (s32[32]{0:T(128)S(1)}, s32[32]{0:T(128)}, u32[]{:S(2)}) copy-start(s32[32]{0:T(128)} %param.15) | copy-start | bytes 388
  2.4 1.4 %collective-permute-start.2 = (f32[8,32,128]{2,1,0:T(8,128)S(1)}, f32[8,32,128]{2,1,0:T(8,128)S(1)}, u32[]{:S(2)}, u32[]{:S(2)}) collective-permute-start(f32[8,32,128]{2,1,0:T(8,128)S(1)} %get-tuple-element.64), channel_id=1, source_target_pairs={{0,2},{2,0},{4,6},{6,4},{8,10},{10,8},{12,14},{14,12},{16,18},{18,... | collective-permute-start | bytes 393224 | tf_op jit(solution)/shard_map/ppermute | solution.py:154
  2.6 1.5 %collective-permute-start = (f32[8,32,128]{2,1,0:T(8,128)S(1)}, f32[8,32,128]{2,1,0:T(8,128)S(1)}, u32[]{:S(2)}, u32[]{:S(2)}) collective-permute-start(f32[8,32,128]{2,1,0:T(8,128)S(1)} %get-tuple-element.60.refs_2_.refs_4_), channel_id=1, source_target_pairs={{0,2},{2,0},{4,6},{6,4},{8,10},{10,8},{12,14},{14,12},{16,18},{18,... | collective-permute-start | bytes 393224 | tf_op jit(solution)/shard_map/ppermute | solution.py:154
  4.3 7.1 %collective-permute-start.5 = (f32[5,32,128]{2,1,0:T(8,128)S(1)}, f32[5,32,128]{2,1,0:T(8,128)S(1)}, u32[]{:S(2)}, u32[]{:S(2)}) collective-permute-start(f32[5,32,128]{2,1,0:T(8,128)S(1)} %get-tuple-element.65.refs_2_.refs_0_), channel_id=1, source_target_pairs={{0,12},{2,14},{4,8},{6,10},{8,4},{10,6},{12,0},{14,2},{16,28},{18,... | collective-permute-start | bytes 245768 | tf_op jit(solution)/shard_map/ppermute | solution.py:154
  8.3 4.7 %collective-permute-start.4 = (f32[5,32,128]{2,1,0:T(8,128)S(1)}, f32[5,32,128]{2,1,0:T(8,128)S(1)}, u32[]{:S(2)}, u32[]{:S(2)}) collective-permute-start(f32[5,32,128]{2,1,0:T(8,128)S(1)} %get-tuple-element.65.refs_2_.refs_0_), channel_id=1, source_target_pairs={{0,8},{2,10},{4,12},{6,14},{8,0},{10,2},{12,4},{14,6},{16,24},{18,... | collective-permute-start | bytes 245768 | tf_op jit(solution)/shard_map/ppermute | solution.py:154
  8.7 4.4 %collective-permute-start.3 = (f32[5,32,128]{2,1,0:T(8,128)S(1)}, f32[5,32,128]{2,1,0:T(8,128)S(1)}, u32[]{:S(2)}, u32[]{:S(2)}) collective-permute-start(f32[5,32,128]{2,1,0:T(8,128)S(1)} %get-tuple-element.65.refs_2_.refs_0_), channel_id=1, source_target_pairs={{0,4},{2,6},{4,0},{6,2},{8,12},{10,14},{12,8},{14,10},{16,20},{18,... | collective-permute-start | bytes 245768 | tf_op jit(solution)/shard_map/ppermute | solution.py:154
  13.2 4.9 %collective-permute-start.6 = (f32[2,32,128]{2,1,0:T(8,128)S(1)}, f32[2,32,128]{2,1,0:T(8,128)S(1)}, u32[]{:S(2)}, u32[]{:S(2)}) collective-permute-start(f32[2,32,128]{2,1,0:T(8,128)S(1)} %get-tuple-element.70.refs_0_), channel_id=1, source_target_pairs={{0,16},{2,18},{4,20},{6,22},{8,24},{10,26},{12,28},{14,30},{16,0},... | collective-permute-start | bytes 98312 | tf_op jit(solution)/shard_map/ppermute | solution.py:154
  18.2 2.2 %copy-start.2 = (s32[1024]{0:T(1024)S(1)}, s32[1024]{0:T(1024)}, u32[]{:S(2)}) copy-start(s32[1024]{0:T(1024)} %param.20) | copy-start | bytes 12292
  18.2 2.2 %copy-start.3 = (f32[1024]{0:T(1024)S(1)}, f32[1024]{0:T(1024)}, u32[]{:S(2)}) copy-start(f32[1024]{0:T(1024)} %param.21) | copy-start | bytes 12292
  18.4 2.0 %copy-start.1 = (s32[1024]{0:T(1024)S(1)}, s32[1024]{0:T(1024)}, u32[]{:S(2)}) copy-start(s32[1024]{0:T(1024)} %param.19) | copy-start | bytes 12292
  18.4 1.9 %copy-start = (s32[1024]{0:T(1024)S(1)}, s32[1024]{0:T(1024)}, u32[]{:S(2)}) copy-start(s32[1024]{0:T(1024)} %param.18) | copy-start | bytes 12292
  18.4 3.9 %collective-permute-start.9 = (f32[5,16,128]{2,1,0:T(8,128)S(1)}, f32[5,16,128]{2,1,0:T(8,128)S(1)}, u32[]{:S(2)}, u32[]{:S(2)}) collective-permute-start(f32[5,16,128]{2,1,0:T(8,128)S(1)} %get-tuple-element.77.refs_4_.refs_0_), channel_id=1, source_target_pairs={{0,3},{1,2},{2,1},{3,0},{4,7},{5,6},{6,5},{7,4},{8,11},{9,10},{10,... | collective-permute-start | bytes 122888 | tf_op jit(solution)/shard_map/ppermute | solution.py:166
  18.5 4.4 %collective-permute-start.8 = (f32[5,16,128]{2,1,0:T(8,128)S(1)}, f32[5,16,128]{2,1,0:T(8,128)S(1)}, u32[]{:S(2)}, u32[]{:S(2)}) collective-permute-start(f32[5,16,128]{2,1,0:T(8,128)S(1)} %get-tuple-element.77.refs_4_.refs_0_), channel_id=1, source_target_pairs={{0,1},{1,0},{2,3},{3,2},{4,5},{5,4},{6,7},{7,6},{8,9},{9,8},{10,11... | collective-permute-start | bytes 122888 | tf_op jit(solution)/shard_map/ppermute | solution.py:166
  20.0 2.8 %collective-permute-start.7 = (f32[5,16,128]{2,1,0:T(8,128)S(1)}, f32[5,16,128]{2,1,0:T(8,128)S(1)}, u32[]{:S(2)}, u32[]{:S(2)}) collective-permute-start(f32[5,16,128]{2,1,0:T(8,128)S(1)} %get-tuple-element.77.refs_4_.refs_0_), channel_id=1, source_target_pairs={{0,2},{1,3},{2,0},{3,1},{4,6},{5,7},{6,4},{7,5},{8,10},{9,11},{10,... | collective-permute-start | bytes 122888 | tf_op jit(solution)/shard_map/ppermute | solution.py:166
  24.6 3.3 %collective-permute-start.13 = (f32[40,128]{1,0:T(8,128)S(1)}, f32[40,128]{1,0:T(8,128)S(1)}, u32[]{:S(2)}, u32[]{:S(2)}) collective-permute-start(f32[40,128]{1,0:T(8,128)S(1)} %get-tuple-element.87.refs_1_.refs_0_), channel_id=1, source_target_pairs={{0,3},{1,2},{2,1},{3,0},{4,7},{5,6},{6,5},{7,4},{8,11},{9,10},{10,... | collective-permute-start | bytes 61448 | tf_op jit(solution)/shard_map/ppermute | solution.py:166
  25.6 3.8 %collective-permute-start.12 = (f32[40,128]{1,0:T(8,128)S(1)}, f32[40,128]{1,0:T(8,128)S(1)}, u32[]{:S(2)}, u32[]{:S(2)}) collective-permute-start(f32[40,128]{1,0:T(8,128)S(1)} %get-tuple-element.87.refs_1_.refs_0_), channel_id=1, source_target_pairs={{0,1},{1,0},{2,3},{3,2},{4,5},{5,4},{6,7},{7,6},{8,9},{9,8},{10,11... | collective-permute-start | bytes 61448 | tf_op jit(solution)/shard_map/ppermute | solution.py:166
  26.5 2.9 %collective-permute-start.11 = (f32[40,128]{1,0:T(8,128)S(1)}, f32[40,128]{1,0:T(8,128)S(1)}, u32[]{:S(2)}, u32[]{:S(2)}) collective-permute-start(f32[40,128]{1,0:T(8,128)S(1)} %get-tuple-element.87.refs_1_.refs_0_), channel_id=1, source_target_pairs={{0,2},{1,3},{2,0},{3,1},{4,6},{5,7},{6,4},{7,5},{8,10},{9,11},{10,... | collective-permute-start | bytes 61448 | tf_op jit(solution)/shard_map/ppermute | solution.py:166
  29.7 5.1 %collective-permute-start.16 = (f32[72,128]{1,0:T(8,128)S(1)}, f32[72,128]{1,0:T(8,128)S(1)}, u32[]{:S(2)}, u32[]{:S(2)}) collective-permute-start(f32[72,128]{1,0:T(8,128)S(1)} %get-tuple-element.93.refs_0_), channel_id=1, source_target_pairs={{0,12},{2,14},{4,8},{6,10},{8,4},{10,6},{12,0},{14,2},{16,28},{18,... | collective-permute-start | bytes 110600 | tf_op jit(solution)/shard_map/ppermute | solution.py:154
  32.0 4.0 %collective-permute-start.15 = (f32[72,128]{1,0:T(8,128)S(1)}, f32[72,128]{1,0:T(8,128)S(1)}, u32[]{:S(2)}, u32[]{:S(2)}) collective-permute-start(f32[72,128]{1,0:T(8,128)S(1)} %get-tuple-element.93.refs_0_), channel_id=1, source_target_pairs={{0,8},{2,10},{4,12},{6,14},{8,0},{10,2},{12,4},{14,6},{16,24},{18,... | collective-permute-start | bytes 110600 | tf_op jit(solution)/shard_map/ppermute | solution.py:154
  32.5 4.0 %collective-permute-start.14 = (f32[72,128]{1,0:T(8,128)S(1)}, f32[72,128]{1,0:T(8,128)S(1)}, u32[]{:S(2)}, u32[]{:S(2)}) collective-permute-start(f32[72,128]{1,0:T(8,128)S(1)} %get-tuple-element.93.refs_0_), channel_id=1, source_target_pairs={{0,4},{2,6},{4,0},{6,2},{8,12},{10,14},{12,8},{14,10},{16,20},{18,... | collective-permute-start | bytes 110600 | tf_op jit(solution)/shard_map/ppermute | solution.py:154
  36.5 4.7 %collective-permute-start.17 = (f32[40,128]{1,0:T(8,128)S(1)}, f32[40,128]{1,0:T(8,128)S(1)}, u32[]{:S(2)}, u32[]{:S(2)}) collective-permute-start(f32[40,128]{1,0:T(8,128)S(1)} %get-tuple-element.94.refs_0_), channel_id=1, source_target_pairs={{0,16},{2,18},{4,20},{6,22},{8,24},{10,26},{12,28},{14,30},{16,0},... | collective-permute-start | bytes 61448 | tf_op jit(solution)/shard_map/ppermute | solution.py:154
  39.3 2.3 %collective-permute-start.10 = (f32[8,32,128]{2,1,0:T(8,128)S(1)}, f32[8,32,128]{2,1,0:T(8,128)S(1)}, u32[]{:S(2)}, u32[]{:S(2)}) collective-permute-start(f32[8,32,128]{2,1,0:T(8,128)S(1)} %get-tuple-element.89), channel_id=1, source_target_pairs={{0,2},{2,0},{4,6},{6,4},{8,10},{10,8},{12,14},{14,12},{16,18},{18,... | collective-permute-start | bytes 393224 | tf_op jit(solution)/shard_map/ppermute | solution.py:154
  41.5 1.4 %collective-permute-start.18 = (f32[8,32,128]{2,1,0:T(8,128)S(1)}, f32[8,32,128]{2,1,0:T(8,128)S(1)}, u32[]{:S(2)}, u32[]{:S(2)}) collective-permute-start(f32[8,32,128]{2,1,0:T(8,128)S(1)} %get-tuple-element.107), channel_id=1, source_target_pairs={{0,2},{2,0},{4,6},{6,4},{8,10},{10,8},{12,14},{14,12},{16,18},{18,... | collective-permute-start | bytes 393224 | tf_op jit(solution)/shard_map/ppermute | solution.py:154

commit v5 on v4

--- a/solution.py
+++ b/solution.py
@@ -457,7 +457,7 @@
 
 
 def make_points(slab, rows):
-    def points(east, north, depth, heads, at_row, at_depth, here, observed):
+    def points(east, north, depth, heads, at_row, at_depth, at_depth_short, here, observed):
         inside, spot = local_spot(east[...], north[...], slab, rows)
         at_row[...] = jnp.where(
             lax.broadcasted_iota(jnp.int32, at_row.shape, 0) == spot, 1.0, 0.0
@@ -465,6 +465,7 @@
         at_depth[...] = jnp.where(
             lax.broadcasted_iota(jnp.int32, at_depth.shape, 0) == depth[...], 1.0, 0.0
         )
+        at_depth_short[...] = at_depth[...].astype(jnp.bfloat16)
         here[...] = jnp.where(inside, 1.0, 0.0)
         observed[...] = heads[...]
 
@@ -519,7 +520,7 @@
     def z_solve(*refs):
         arrivals = refs[:count]
         (cell_factors, chunk_factors, scaled_cells, scaled_chunks, storage,
-         z_factors, joints, inverse, at_row, at_depth, here, observed,
+         z_factors, joints, inverse, at_row, at_depth, at_depth_short, here, observed,
          y_factors, head_second, y_edges, head_up, adjoint_third, message,
          next_cells, next_chunks,
          scratch, edges, turned, loads, second) = refs[count:]
@@ -552,7 +553,7 @@
             row = 2 * slab + i
             message[row:row + 1, :] = misfit[:, i * lanes:(i + 1) * lanes]
         parts = [
-            (at_depth[...] * part.astype(f32)).astype(jnp.bfloat16)
+            at_depth_short[...] * part
             for part in bf16_parts(misfit_weight * misfit, 2)
         ]
         source = lax.dot_general(
@@ -846,9 +847,10 @@
         [x_faces, x_steps, storage, cell_factors, chunk_factors, ends],
         [(grid, f32), ((2,) + turned, f32)],
     )
-    at_row, at_depth, here, observed = run(
+    at_row, at_depth, at_depth_short, here, observed = run(
         make_points(slab, half),
-        [((slab * half, points), jnp.bfloat16), (lanes, points), (1, points), (1, points)],
+        [((slab * half, points), jnp.bfloat16), (lanes, points), ((lanes, points), jnp.bfloat16),
+         (1, points), (1, points)],
         probes,
         after=[message],
     )
@@ -860,7 +862,7 @@
          (2 * slab + extra, lanes), cell, (chunks - 1,) + line],
         exchange_rows(message)
         + [cell_factors, chunk_factors, scaled_cells, scaled_chunks, storage,
-           z_factors, joints, inverse, at_row, at_depth, here, observed],
+           z_factors, joints, inverse, at_row, at_depth, at_depth_short, here, observed],
         [((blocks, 5) + line, f32), ((blocks + 1,) + line, f32), ((2,) + turned, f32),
          (upright, f32), (grid, f32)],
     )

time: 43.8 us -> 43.8 us (level)
  transfers between devices with their start and end apart: 19 -> 19, of which waited for: 15 -> 15; matrix products, arithmetic and copies ran while one was open for 0% -> 0% of each run, Pallas kernels for 7% -> 8%
where the time goes in v5:
time: 43.8 us; the launch traced here: 43.7 us
  starting transfers between devices  18.5 us (42%)
  waiting for transfers between devices  16.3 us (37%)
  Pallas kernels  7.92 us (18%)
  between operations  0.83 us (2%)
    ppermute x13, starting transfers between devices, exchange(): lax.ppermute(value, 'gx', [(i, i ^ turn * stride) for i in range(size)])  14.6 us
    ppermute x13, waiting for transfers between devices, exchange(): lax.ppermute(value, 'gx', [(i, i ^ turn * stride) for i in range(size)])  11.5 us
    pallas_call x19, Pallas kernels, run(): pl.pallas_call(ordered, out_shape=shapes, in_specs=[pl.BlockSpec(memory_s...  7.92 us
    ppermute x6, waiting for transfers between devices, exchange_rows(): lax.ppermute(value, ('gx', 'yz'), [(i * columns + j, (i ^ turn % 2) * col...  4.81 us
    ppermute x6, starting transfers between devices, exchange_rows(): lax.ppermute(value, ('gx', 'yz'), [(i * columns + j, (i ^ turn % 2) * col...  3.85 us
  transfers between devices with their start and end apart: 19, of which 15 were waited for; matrix products, arithmetic and copies ran while one was open for 0% of the time, Pallas kernels for 8%

profile of v5, /device:TPU:0, one launch (start us, length us, event | category | flops | bytes accessed | tf_op | source)
XLA Modules:
  0.0 43.7 jit_solution(18093994653498913698)
XLA Ops:
  0.6 1.3 %shard_map.130 = (f32[8,32,128]{2,1,0:T(8,128)S(1)}, f32[8,32,128]{2,1,0:T(8,128)S(1)}, f32[8,32,128]{2,1,0:T(8,128)S(1)}, f32[8,32,128]{2,1,0:T(8,128)S(1)}, f3...) custom-call(f32[8,64,128]{2,1,0:T(8,128)} %refs_0_.1, f32[8,64,128]{2,1,0:T(8,128)} %refs_1_.1, f32[8,64,128]{2,1,0:T(8,128)} %refs_2_.1), custom_call_target="tpu_custom_call" | custom-call | flops 1000000 | bytes 1572864 | tf_op jit(solution)/shard_map/pallas_call | solution.py:128
  1.9 0.5 %collective-permute-start.1 = (f32[8,32,128]{2,1,0:T(8,128)S(1)}, f32[8,32,128]{2,1,0:T(8,128)S(1)}, u32[]{:S(2)}, u32[]{:S(2)}) collective-permute-start(f32[8,32,128]{2,1,0:T(8,128)S(1)} %get-tuple-element.64), channel_id=1, source_target_pairs={{0,2},{2,0},{4,6},{6,4},{8,10},{10,8},{12,14},{14,12},{16,18},{18,... | collective-permute-start | bytes 393224 | tf_op jit(solution)/shard_map/ppermute | solution.py:154
  2.6 0.5 %collective-permute-start = (f32[8,32,128]{2,1,0:T(8,128)S(1)}, f32[8,32,128]{2,1,0:T(8,128)S(1)}, u32[]{:S(2)}, u32[]{:S(2)}) collective-permute-start(f32[8,32,128]{2,1,0:T(8,128)S(1)} %get-tuple-element.61.refs_2_.refs_4_), channel_id=1, source_target_pairs={{0,2},{2,0},{4,6},{6,4},{8,10},{10,8},{12,14},{14,12},{16,18},{18,... | collective-permute-start | bytes 393224 | tf_op jit(solution)/shard_map/ppermute | solution.py:154
  3.5 0.4 collective-permute-done.2.refs_5_
  4.3 3.9 %collective-permute-start.5 = (f32[5,32,128]{2,1,0:T(8,128)S(1)}, f32[5,32,128]{2,1,0:T(8,128)S(1)}, u32[]{:S(2)}, u32[]{:S(2)}) collective-permute-start(f32[5,32,128]{2,1,0:T(8,128)S(1)} %get-tuple-element.66.refs_2_.refs_0_), channel_id=1, source_target_pairs={{0,12},{2,14},{4,8},{6,10},{8,4},{10,6},{12,0},{14,2},{16,28},{18,... | collective-permute-start | bytes 245768 | tf_op jit(solution)/shard_map/ppermute | solution.py:154
  8.3 0.4 %collective-permute-start.4 = (f32[5,32,128]{2,1,0:T(8,128)S(1)}, f32[5,32,128]{2,1,0:T(8,128)S(1)}, u32[]{:S(2)}, u32[]{:S(2)}) collective-permute-start(f32[5,32,128]{2,1,0:T(8,128)S(1)} %get-tuple-element.66.refs_2_.refs_0_), channel_id=1, source_target_pairs={{0,8},{2,10},{4,12},{6,14},{8,0},{10,2},{12,4},{14,6},{16,24},{18,... | collective-permute-start | bytes 245768 | tf_op jit(solution)/shard_map/ppermute | solution.py:154
  8.9 0.4 shard_map.135
  9.6 1.8 %collective-permute-done.5.refs_3_ = f32[5,32,128]{2,1,0:T(8,128)S(1)} collective-permute-done((f32[5,32,128]{2,1,0:T(8,128)S(1)}, f32[5,32,128]{2,1,0:T(8,128)S(1)}, u32[]{:S(2)}, u32[]{:S(2)}) %collective-permute-start.5) | collective-permute-done | bytes 81952 | tf_op jit(solution)/shard_map/ppermute | solution.py:154
  11.4 1.6 %collective-permute-done.4.refs_2_ = f32[5,32,128]{2,1,0:T(8,128)S(1)} collective-permute-done((f32[5,32,128]{2,1,0:T(8,128)S(1)}, f32[5,32,128]{2,1,0:T(8,128)S(1)}, u32[]{:S(2)}, u32[]{:S(2)}) %collective-permute-start.4) | collective-permute-done | bytes 81952 | tf_op jit(solution)/shard_map/ppermute | solution.py:154
  13.2 2.7 %collective-permute-start.6 = (f32[2,32,128]{2,1,0:T(8,128)S(1)}, f32[2,32,128]{2,1,0:T(8,128)S(1)}, u32[]{:S(2)}, u32[]{:S(2)}) collective-permute-start(f32[2,32,128]{2,1,0:T(8,128)S(1)} %get-tuple-element.71.refs_0_), channel_id=1, source_target_pairs={{0,16},{2,18},{4,20},{6,22},{8,24},{10,26},{12,28},{14,30},{16,0},... | collective-permute-start | bytes 98312 | tf_op jit(solution)/shard_map/ppermute | solution.py:154
  15.9 2.2 %collective-permute-done.6.refs_1_ = f32[2,32,128]{2,1,0:T(8,128)S(1)} collective-permute-done((f32[2,32,128]{2,1,0:T(8,128)S(1)}, f32[2,32,128]{2,1,0:T(8,128)S(1)}, u32[]{:S(2)}, u32[]{:S(2)}) %collective-permute-start.6) | collective-permute-done | bytes 32800 | tf_op jit(solution)/shard_map/ppermute | solution.py:154
  18.5 1.6 %collective-permute-start.8 = (f32[5,16,128]{2,1,0:T(8,128)S(1)}, f32[5,16,128]{2,1,0:T(8,128)S(1)}, u32[]{:S(2)}, u32[]{:S(2)}) collective-permute-start(f32[5,16,128]{2,1,0:T(8,128)S(1)} %get-tuple-element.78.refs_4_.refs_0_), channel_id=1, source_target_pairs={{0,1},{1,0},{2,3},{3,2},{4,5},{5,4},{6,7},{7,6},{8,9},{9,8},{10,11... | collective-permute-start | bytes 122888 | tf_op jit(solution)/shard_map/ppermute | solution.py:166
  20.3 0.6 %shard_map.139 = (bf16[512,1024]{1,0:T(8,128)(2,1)S(1)}, f32[128,1024]{1,0:T(8,128)S(1)}, bf16[128,1024]{1,0:T(8,128)(2,1)S(1)}, f32[1,1024]{1,0:T(1,128)S(1)}, f32[1,1024]{1,0:T(1,128)S(1)}) custom-call(s32[1,1024]{1,0:T(1,128)S(1)} %bitcast.8, s32[1,1024]{1,0:T(1,128)S(1)} %bitcast.9, s32[1,1024]{1,0:T(1,128)S(1)} %bitcast.10, f32[1,1024]{1,0:T(1,128)S(1)} %bitcast.11, ...), custom_call_target="tpu_custom_call" | custom-call | flops 1000000 | bytes 3170304 | tf_op jit(solution)/shard_map/pallas_call | solution.py:128
  20.9 1.4 %collective-permute-done.9.refs_3_ = f32[5,16,128]{2,1,0:T(8,128)S(1)} collective-permute-done((f32[5,16,128]{2,1,0:T(8,128)S(1)}, f32[5,16,128]{2,1,0:T(8,128)S(1)}, u32[]{:S(2)}, u32[]{:S(2)}) %collective-permute-start.9) | collective-permute-done | bytes 40992 | tf_op jit(solution)/shard_map/ppermute | solution.py:166
  22.3 0.6 %collective-permute-done.8.refs_2_ = f32[5,16,128]{2,1,0:T(8,128)S(1)} collective-permute-done((f32[5,16,128]{2,1,0:T(8,128)S(1)}, f32[5,16,128]{2,1,0:T(8,128)S(1)}, u32[]{:S(2)}, u32[]{:S(2)}) %collective-permute-start.8) | collective-permute-done | bytes 40992 | tf_op jit(solution)/shard_map/ppermute | solution.py:166
  22.8 1.8 %shard_map.140 = (f32[3,3,16,128]{3,2,1,0:T(8,128)S(1)}, f32[4,16,8,128]{3,2,1,0:T(8,128)S(1)}, f32[2,16,8,128]{3,2,1,0:T(8,128)S(1)}, f32[4,128,128]{2,1,0:T(8,...) custom-call(f32[5,16,128]{2,1,0:T(8,128)S(1)} %get-tuple-element.78., ...), custom_call_target="tpu_custom_call" | custom-call | flops 1000000 | bytes 7090176 | tf_op jit(solution)/shard_map/pallas_call | solution.py:128
  24.6 1.0 %collective-permute-start.13 = (f32[40,128]{1,0:T(8,128)S(1)}, f32[40,128]{1,0:T(8,128)S(1)}, u32[]{:S(2)}, u32[]{:S(2)}) collective-permute-start(f32[40,128]{1,0:T(8,128)S(1)} %get-tuple-element.89.refs_1_.refs_0_), channel_id=1, source_target_pairs={{0,3},{1,2},{2,1},{3,0},{4,7},{5,6},{6,5},{7,4},{8,11},{9,10},{10,... | collective-permute-start | bytes 61448 | tf_op jit(solution)/shard_map/ppermute | solution.py:166
  25.6 0.9 %collective-permute-start.12 = (f32[40,128]{1,0:T(8,128)S(1)}, f32[40,128]{1,0:T(8,128)S(1)}, u32[]{:S(2)}, u32[]{:S(2)}) collective-permute-start(f32[40,128]{1,0:T(8,128)S(1)} %get-tuple-element.89.refs_1_.refs_0_), channel_id=1, source_target_pairs={{0,1},{1,0},{2,3},{3,2},{4,5},{5,4},{6,7},{7,6},{8,9},{9,8},{10,11... | collective-permute-start | bytes 61448 | tf_op jit(solution)/shard_map/ppermute | solution.py:166
  26.5 1.3 %collective-permute-done.13.refs_3_ = f32[40,128]{1,0:T(8,128)S(1)} collective-permute-done((f32[40,128]{1,0:T(8,128)S(1)}, f32[40,128]{1,0:T(8,128)S(1)}, u32[]{:S(2)}, u32[]{:S(2)}) %collective-permute-start.13) | collective-permute-done | bytes 20512 | tf_op jit(solution)/shard_map/ppermute | solution.py:166
  27.9 1.5 %collective-permute-done.12.refs_2_ = f32[40,128]{1,0:T(8,128)S(1)} collective-permute-done((f32[40,128]{1,0:T(8,128)S(1)}, f32[40,128]{1,0:T(8,128)S(1)}, u32[]{:S(2)}, u32[]{:S(2)}) %collective-permute-start.12) | collective-permute-done | bytes 20512 | tf_op jit(solution)/shard_map/ppermute | solution.py:166
  29.7 2.4 %collective-permute-start.16 = (f32[72,128]{1,0:T(8,128)S(1)}, f32[72,128]{1,0:T(8,128)S(1)}, u32[]{:S(2)}, u32[]{:S(2)}) collective-permute-start(f32[72,128]{1,0:T(8,128)S(1)} %get-tuple-element.95.refs_0_), channel_id=1, source_target_pairs={{0,12},{2,14},{4,8},{6,10},{8,4},{10,6},{12,0},{14,2},{16,28},{18,... | collective-permute-start | bytes 110600 | tf_op jit(solution)/shard_map/ppermute | solution.py:154
  32.0 0.5 %collective-permute-start.15 = (f32[72,128]{1,0:T(8,128)S(1)}, f32[72,128]{1,0:T(8,128)S(1)}, u32[]{:S(2)}, u32[]{:S(2)}) collective-permute-start(f32[72,128]{1,0:T(8,128)S(1)} %get-tuple-element.95.refs_0_), channel_id=1, source_target_pairs={{0,8},{2,10},{4,12},{6,14},{8,0},{10,2},{12,4},{14,6},{16,24},{18,... | collective-permute-start | bytes 110600 | tf_op jit(solution)/shard_map/ppermute | solution.py:154
  32.5 0.7 %collective-permute-start.14 = (f32[72,128]{1,0:T(8,128)S(1)}, f32[72,128]{1,0:T(8,128)S(1)}, u32[]{:S(2)}, u32[]{:S(2)}) collective-permute-start(f32[72,128]{1,0:T(8,128)S(1)} %get-tuple-element.95.refs_0_), channel_id=1, source_target_pairs={{0,4},{2,6},{4,0},{6,2},{8,12},{10,14},{12,8},{14,10},{16,20},{18,... | collective-permute-start | bytes 110600 | tf_op jit(solution)/shard_map/ppermute | solution.py:154
  33.2 1.5 %collective-permute-done.16.refs_3_ = f32[72,128]{1,0:T(8,128)S(1)} collective-permute-done((f32[72,128]{1,0:T(8,128)S(1)}, f32[72,128]{1,0:T(8,128)S(1)}, u32[]{:S(2)}, u32[]{:S(2)}) %collective-permute-start.16) | collective-permute-done | bytes 36896 | tf_op jit(solution)/shard_map/ppermute | solution.py:154
  34.8 1.2 %collective-permute-done.15.refs_2_ = f32[72,128]{1,0:T(8,128)S(1)} collective-permute-done((f32[72,128]{1,0:T(8,128)S(1)}, f32[72,128]{1,0:T(8,128)S(1)}, u32[]{:S(2)}, u32[]{:S(2)}) %collective-permute-start.15) | collective-permute-done | bytes 36896 | tf_op jit(solution)/shard_map/ppermute | solution.py:154
  36.0 0.5 %collective-permute-done.14.refs_1_ = f32[72,128]{1,0:T(8,128)S(1)} collective-permute-done((f32[72,128]{1,0:T(8,128)S(1)}, f32[72,128]{1,0:T(8,128)S(1)}, u32[]{:S(2)}, u32[]{:S(2)}) %collective-permute-start.14) | collective-permute-done | bytes 36896 | tf_op jit(solution)/shard_map/ppermute | solution.py:154
  36.5 2.6 %collective-permute-start.17 = (f32[40,128]{1,0:T(8,128)S(1)}, f32[40,128]{1,0:T(8,128)S(1)}, u32[]{:S(2)}, u32[]{:S(2)}) collective-permute-start(f32[40,128]{1,0:T(8,128)S(1)} %get-tuple-element.96.refs_0_), channel_id=1, source_target_pairs={{0,16},{2,18},{4,20},{6,22},{8,24},{10,26},{12,28},{14,30},{16,0},... | collective-permute-start | bytes 61448 | tf_op jit(solution)/shard_map/ppermute | solution.py:154
  39.4 0.6 %shard_map.145.refs_7_.refs_6_ = f32[16,32,128]{2,1,0:T(8,128)S(1)} custom-call(f32[16,32,128]{2,1,0:T(8,128)S(1)} %get-tuple-element.67.refs_0_.refs_4_, f32[16,32,128]{2,1,0:T(8,128)S(1)} %get-tuple-element.90.refs_0_.refs_1_, f32[16,32,128]{2,1,0:T(8,128)S(1)} %get-tuple-element.100.refs_2_, f32[4,16,8,128]{3,2,1,0:T(8,128)S(1)} %get-tuple-element.101.refs_3_, ...), custom_call_target="tpu_custom_call" | custom-call | flops 1000000 | bytes 1835008 | tf_op jit(solution)/shard_map/pallas_call | solution.py:128
  40.0 1.3 %collective-permute-done.17.refs_1_ = f32[40,128]{1,0:T(8,128)S(1)} collective-permute-done((f32[40,128]{1,0:T(8,128)S(1)}, f32[40,128]{1,0:T(8,128)S(1)}, u32[]{:S(2)}, u32[]{:S(2)}) %collective-permute-start.17) | collective-permute-done | bytes 20512 | tf_op jit(solution)/shard_map/ppermute | solution.py:154
  41.6 0.7 %shard_map.142 = f32[8,64,128]{2,1,0:T(8,128)} custom-call(f32[16,32,128]{2,1,0:T(8,128)S(1)} %get-tuple-element.90.refs_0_.refs_1_, f32[8,32,128]{2,1,0:T(8,128)S(1)} %collective-permute-done.10.refs_1_), custom_call_target="tpu_custom_call" | custom-call | flops 1000000 | bytes 655360 | tf_op jit(solution)/shard_map/pallas_call | solution.py:128
  42.4 0.6 %collective-permute-done.18.refs_1_ = f32[8,32,128]{2,1,0:T(8,128)S(1)} collective-permute-done((f32[8,32,128]{2,1,0:T(8,128)S(1)}, f32[8,32,128]{2,1,0:T(8,128)S(1)}, u32[]{:S(2)}, u32[]{:S(2)}) %collective-permute-start.18) | collective-permute-done | bytes 131104 | tf_op jit(solution)/shard_map/ppermute | solution.py:154
  42.9 0.7 %shard_map.148 = (f32[8,64,128]{2,1,0:T(8,128)}, f32[8,128]{1,0:T(8,128)}) custom-call(f32[8,32,128]{2,1,0:T(8,128)S(1)} %get-tuple-element.108.refs_0_, f32[8,32,128]{2,1,0:T(8,128)S(1)} %collective-permute-done.18.refs_1_, f32[8,128]{1,0:T(8,128)S(1)} %get-tuple-element.110.refs_2_), custom_call_target="tpu_custom_call" | custom-call | flops 1000000 | bytes 532480 | tf_op jit(solution)/shard_map/pallas_call | solution.py:128
  (42 shorter events, 3.3 us)
Async XLA Ops:
  1.9 1.6 %collective-permute-start.1 = (f32[8,32,128]{2,1,0:T(8,128)S(1)}, f32[8,32,128]{2,1,0:T(8,128)S(1)}, u32[]{:S(2)}, u32[]{:S(2)}) collective-permute-start(f32[8,32,128]{2,1,0:T(8,128)S(1)} %get-tuple-element.64), channel_id=1, source_target_pairs={{0,2},{2,0},{4,6},{6,4},{8,10},{10,8},{12,14},{14,12},{16,18},{18,... | collective-permute-start | bytes 393224 | tf_op jit(solution)/shard_map/ppermute | solution.py:154
  2.4 0.7 %copy-start.7 = (s32[32]{0:T(128)S(1)}, s32[32]{0:T(128)}, u32[]{:S(2)}) copy-start(s32[32]{0:T(128)} %param.14) | copy-start | bytes 388
  2.4 0.7 %copy-start.4 = (f32[32]{0:T(128)S(1)}, f32[32]{0:T(128)}, u32[]{:S(2)}) copy-start(f32[32]{0:T(128)} %param.17) | copy-start | bytes 388
  2.4 0.7 %copy-start.5 = (s32[32]{0:T(128)S(1)}, s32[32]{0:T(128)}, u32[]{:S(2)}) copy-start(s32[32]{0:T(128)} %param.16) | copy-start | bytes 388
  2.4 0.7 %copy-start.6 = (s32[32]{0:T(128)S(1)}, s32[32]{0:T(128)}, u32[]{:S(2)}) copy-start(s32[32]{0:T(128)} %param.15) | copy-start | bytes 388
  2.4 1.4 %collective-permute-start.2 = (f32[8,32,128]{2,1,0:T(8,128)S(1)}, f32[8,32,128]{2,1,0:T(8,128)S(1)}, u32[]{:S(2)}, u32[]{:S(2)}) collective-permute-start(f32[8,32,128]{2,1,0:T(8,128)S(1)} %get-tuple-element.65), channel_id=1, source_target_pairs={{0,2},{2,0},{4,6},{6,4},{8,10},{10,8},{12,14},{14,12},{16,18},{18,... | collective-permute-start | bytes 393224 | tf_op jit(solution)/shard_map/ppermute | solution.py:154
  2.6 1.5 %collective-permute-start = (f32[8,32,128]{2,1,0:T(8,128)S(1)}, f32[8,32,128]{2,1,0:T(8,128)S(1)}, u32[]{:S(2)}, u32[]{:S(2)}) collective-permute-start(f32[8,32,128]{2,1,0:T(8,128)S(1)} %get-tuple-element.61.refs_2_.refs_4_), channel_id=1, source_target_pairs={{0,2},{2,0},{4,6},{6,4},{8,10},{10,8},{12,14},{14,12},{16,18},{18,... | collective-permute-start | bytes 393224 | tf_op jit(solution)/shard_map/ppermute | solution.py:154
  4.3 7.1 %collective-permute-start.5 = (f32[5,32,128]{2,1,0:T(8,128)S(1)}, f32[5,32,128]{2,1,0:T(8,128)S(1)}, u32[]{:S(2)}, u32[]{:S(2)}) collective-permute-start(f32[5,32,128]{2,1,0:T(8,128)S(1)} %get-tuple-element.66.refs_2_.refs_0_), channel_id=1, source_target_pairs={{0,12},{2,14},{4,8},{6,10},{8,4},{10,6},{12,0},{14,2},{16,28},{18,... | collective-permute-start | bytes 245768 | tf_op jit(solution)/shard_map/ppermute | solution.py:154
  8.3 4.7 %collective-permute-start.4 = (f32[5,32,128]{2,1,0:T(8,128)S(1)}, f32[5,32,128]{2,1,0:T(8,128)S(1)}, u32[]{:S(2)}, u32[]{:S(2)}) collective-permute-start(f32[5,32,128]{2,1,0:T(8,128)S(1)} %get-tuple-element.66.refs_2_.refs_0_), channel_id=1, source_target_pairs={{0,8},{2,10},{4,12},{6,14},{8,0},{10,2},{12,4},{14,6},{16,24},{18,... | collective-permute-start | bytes 245768 | tf_op jit(solution)/shard_map/ppermute | solution.py:154
  8.7 4.4 %collective-permute-start.3 = (f32[5,32,128]{2,1,0:T(8,128)S(1)}, f32[5,32,128]{2,1,0:T(8,128)S(1)}, u32[]{:S(2)}, u32[]{:S(2)}) collective-permute-start(f32[5,32,128]{2,1,0:T(8,128)S(1)} %get-tuple-element.66.refs_2_.refs_0_), channel_id=1, source_target_pairs={{0,4},{2,6},{4,0},{6,2},{8,12},{10,14},{12,8},{14,10},{16,20},{18,... | collective-permute-start | bytes 245768 | tf_op jit(solution)/shard_map/ppermute | solution.py:154
  13.2 4.9 %collective-permute-start.6 = (f32[2,32,128]{2,1,0:T(8,128)S(1)}, f32[2,32,128]{2,1,0:T(8,128)S(1)}, u32[]{:S(2)}, u32[]{:S(2)}) collective-permute-start(f32[2,32,128]{2,1,0:T(8,128)S(1)} %get-tuple-element.71.refs_0_), channel_id=1, source_target_pairs={{0,16},{2,18},{4,20},{6,22},{8,24},{10,26},{12,28},{14,30},{16,0},... | collective-permute-start | bytes 98312 | tf_op jit(solution)/shard_map/ppermute | solution.py:154
  18.2 2.2 %copy-start.2 = (s32[1024]{0:T(1024)S(1)}, s32[1024]{0:T(1024)}, u32[]{:S(2)}) copy-start(s32[1024]{0:T(1024)} %param.20) | copy-start | bytes 12292
  18.2 2.2 %copy-start.3 = (f32[1024]{0:T(1024)S(1)}, f32[1024]{0:T(1024)}, u32[]{:S(2)}) copy-start(f32[1024]{0:T(1024)} %param.21) | copy-start | bytes 12292
  18.4 2.0 %copy-start.1 = (s32[1024]{0:T(1024)S(1)}, s32[1024]{0:T(1024)}, u32[]{:S(2)}) copy-start(s32[1024]{0:T(1024)} %param.19) | copy-start | bytes 12292
  18.4 1.9 %copy-start = (s32[1024]{0:T(1024)S(1)}, s32[1024]{0:T(1024)}, u32[]{:S(2)}) copy-start(s32[1024]{0:T(1024)} %param.18) | copy-start | bytes 12292
  18.4 3.9 %collective-permute-start.9 = (f32[5,16,128]{2,1,0:T(8,128)S(1)}, f32[5,16,128]{2,1,0:T(8,128)S(1)}, u32[]{:S(2)}, u32[]{:S(2)}) collective-permute-start(f32[5,16,128]{2,1,0:T(8,128)S(1)} %get-tuple-element.78.refs_4_.refs_0_), channel_id=1, source_target_pairs={{0,3},{1,2},{2,1},{3,0},{4,7},{5,6},{6,5},{7,4},{8,11},{9,10},{10,... | collective-permute-start | bytes 122888 | tf_op jit(solution)/shard_map/ppermute | solution.py:166
  18.5 4.4 %collective-permute-start.8 = (f32[5,16,128]{2,1,0:T(8,128)S(1)}, f32[5,16,128]{2,1,0:T(8,128)S(1)}, u32[]{:S(2)}, u32[]{:S(2)}) collective-permute-start(f32[5,16,128]{2,1,0:T(8,128)S(1)} %get-tuple-element.78.refs_4_.refs_0_), channel_id=1, source_target_pairs={{0,1},{1,0},{2,3},{3,2},{4,5},{5,4},{6,7},{7,6},{8,9},{9,8},{10,11... | collective-permute-start | bytes 122888 | tf_op jit(solution)/shard_map/ppermute | solution.py:166
  20.0 2.8 %collective-permute-start.7 = (f32[5,16,128]{2,1,0:T(8,128)S(1)}, f32[5,16,128]{2,1,0:T(8,128)S(1)}, u32[]{:S(2)}, u32[]{:S(2)}) collective-permute-start(f32[5,16,128]{2,1,0:T(8,128)S(1)} %get-tuple-element.78.refs_4_.refs_0_), channel_id=1, source_target_pairs={{0,2},{1,3},{2,0},{3,1},{4,6},{5,7},{6,4},{7,5},{8,10},{9,11},{10,... | collective-permute-start | bytes 122888 | tf_op jit(solution)/shard_map/ppermute | solution.py:166
  24.6 3.3 %collective-permute-start.13 = (f32[40,128]{1,0:T(8,128)S(1)}, f32[40,128]{1,0:T(8,128)S(1)}, u32[]{:S(2)}, u32[]{:S(2)}) collective-permute-start(f32[40,128]{1,0:T(8,128)S(1)} %get-tuple-element.89.refs_1_.refs_0_), channel_id=1, source_target_pairs={{0,3},{1,2},{2,1},{3,0},{4,7},{5,6},{6,5},{7,4},{8,11},{9,10},{10,... | collective-permute-start | bytes 61448 | tf_op jit(solution)/shard_map/ppermute | solution.py:166
  25.6 3.8 %collective-permute-start.12 = (f32[40,128]{1,0:T(8,128)S(1)}, f32[40,128]{1,0:T(8,128)S(1)}, u32[]{:S(2)}, u32[]{:S(2)}) collective-permute-start(f32[40,128]{1,0:T(8,128)S(1)} %get-tuple-element.89.refs_1_.refs_0_), channel_id=1, source_target_pairs={{0,1},{1,0},{2,3},{3,2},{4,5},{5,4},{6,7},{7,6},{8,9},{9,8},{10,11... | collective-permute-start | bytes 61448 | tf_op jit(solution)/shard_map/ppermute | solution.py:166
  26.5 2.9 %collective-permute-start.11 = (f32[40,128]{1,0:T(8,128)S(1)}, f32[40,128]{1,0:T(8,128)S(1)}, u32[]{:S(2)}, u32[]{:S(2)}) collective-permute-start(f32[40,128]{1,0:T(8,128)S(1)} %get-tuple-element.89.refs_1_.refs_0_), channel_id=1, source_target_pairs={{0,2},{1,3},{2,0},{3,1},{4,6},{5,7},{6,4},{7,5},{8,10},{9,11},{10,... | collective-permute-start | bytes 61448 | tf_op jit(solution)/shard_map/ppermute | solution.py:166
  29.7 5.1 %collective-permute-start.16 = (f32[72,128]{1,0:T(8,128)S(1)}, f32[72,128]{1,0:T(8,128)S(1)}, u32[]{:S(2)}, u32[]{:S(2)}) collective-permute-start(f32[72,128]{1,0:T(8,128)S(1)} %get-tuple-element.95.refs_0_), channel_id=1, source_target_pairs={{0,12},{2,14},{4,8},{6,10},{8,4},{10,6},{12,0},{14,2},{16,28},{18,... | collective-permute-start | bytes 110600 | tf_op jit(solution)/shard_map/ppermute | solution.py:154
  32.0 4.0 %collective-permute-start.15 = (f32[72,128]{1,0:T(8,128)S(1)}, f32[72,128]{1,0:T(8,128)S(1)}, u32[]{:S(2)}, u32[]{:S(2)}) collective-permute-start(f32[72,128]{1,0:T(8,128)S(1)} %get-tuple-element.95.refs_0_), channel_id=1, source_target_pairs={{0,8},{2,10},{4,12},{6,14},{8,0},{10,2},{12,4},{14,6},{16,24},{18,... | collective-permute-start | bytes 110600 | tf_op jit(solution)/shard_map/ppermute | solution.py:154
  32.5 4.0 %collective-permute-start.14 = (f32[72,128]{1,0:T(8,128)S(1)}, f32[72,128]{1,0:T(8,128)S(1)}, u32[]{:S(2)}, u32[]{:S(2)}) collective-permute-start(f32[72,128]{1,0:T(8,128)S(1)} %get-tuple-element.95.refs_0_), channel_id=1, source_target_pairs={{0,4},{2,6},{4,0},{6,2},{8,12},{10,14},{12,8},{14,10},{16,20},{18,... | collective-permute-start | bytes 110600 | tf_op jit(solution)/shard_map/ppermute | solution.py:154
  36.5 4.7 %collective-permute-start.17 = (f32[40,128]{1,0:T(8,128)S(1)}, f32[40,128]{1,0:T(8,128)S(1)}, u32[]{:S(2)}, u32[]{:S(2)}) collective-permute-start(f32[40,128]{1,0:T(8,128)S(1)} %get-tuple-element.96.refs_0_), channel_id=1, source_target_pairs={{0,16},{2,18},{4,20},{6,22},{8,24},{10,26},{12,28},{14,30},{16,0},... | collective-permute-start | bytes 61448 | tf_op jit(solution)/shard_map/ppermute | solution.py:154
  39.3 2.3 %collective-permute-start.10 = (f32[8,32,128]{2,1,0:T(8,128)S(1)}, f32[8,32,128]{2,1,0:T(8,128)S(1)}, u32[]{:S(2)}, u32[]{:S(2)}) collective-permute-start(f32[8,32,128]{2,1,0:T(8,128)S(1)} %get-tuple-element.91), channel_id=1, source_target_pairs={{0,2},{2,0},{4,6},{6,4},{8,10},{10,8},{12,14},{14,12},{16,18},{18,... | collective-permute-start | bytes 393224 | tf_op jit(solution)/shard_map/ppermute | solution.py:154
  41.5 1.4 %collective-permute-start.18 = (f32[8,32,128]{2,1,0:T(8,128)S(1)}, f32[8,32,128]{2,1,0:T(8,128)S(1)}, u32[]{:S(2)}, u32[]{:S(2)}) collective-permute-start(f32[8,32,128]{2,1,0:T(8,128)S(1)} %get-tuple-element.109), channel_id=1, source_target_pairs={{0,2},{2,0},{4,6},{6,4},{8,10},{10,8},{12,14},{14,12},{16,18},{18,... | collective-permute-start | bytes 393224 | tf_op jit(solution)/shard_map/ppermute | solution.py:154

commit v6 on v4

--- a/solution.py
+++ b/solution.py
@@ -599,10 +599,9 @@
         near, far = own_edges(edges, me, nothing, faces, nothing)
         y_expand(near, far, cell_factors, chunk_factors, scaled_cells, scaled_chunks,
                  turned, adjoint_second, y_edges, second)
-        for i in range(slab):
-            second[i] = storage[i] * second[i]
         near, far, scaled = eliminate_loads(
-            factors_of(x_steps), [pair_cells(second, i) for i in range(slab // 2)]
+            factors_of(x_steps),
+            [pair_cells(storage, i) * pair_cells(second, i) for i in range(slab // 2)],
         )
         for i, value in enumerate(scaled):
             scaled_x[i] = value

time: 43.8 us -> 43.8 us (level)
  no operation moved by 1% of the time
where the time goes in v6:
time: 43.8 us; the launch traced here: 43.7 us
  starting transfers between devices  18.5 us (42%)
  waiting for transfers between devices  16.6 us (38%)
  Pallas kernels  7.57 us (17%)
  between operations  0.83 us (2%)
    ppermute x13, starting transfers between devices, exchange(): lax.ppermute(value, 'gx', [(i, i ^ turn * stride) for i in range(size)])  14.6 us
    ppermute x13, waiting for transfers between devices, exchange(): lax.ppermute(value, 'gx', [(i, i ^ turn * stride) for i in range(size)])  11.5 us
    pallas_call x19, Pallas kernels, run(): pl.pallas_call(ordered, out_shape=shapes, in_specs=[pl.BlockSpec(memory_s...  7.57 us
    ppermute x6, waiting for transfers between devices, exchange_rows(): lax.ppermute(value, ('gx', 'yz'), [(i * columns + j, (i ^ turn % 2) * col...  5.15 us
    ppermute x6, starting transfers between devices, exchange_rows(): lax.ppermute(value, ('gx', 'yz'), [(i * columns + j, (i ^ turn % 2) * col...  3.85 us
  transfers between devices with their start and end apart: 19, of which 15 were waited for; matrix products, arithmetic and copies ran while one was open for 0% of the time, Pallas kernels for 7%

profile of v6, /device:TPU:0, one launch (start us, length us, event | category | flops | bytes accessed | tf_op | source)
XLA Modules:
  0.0 43.7 jit_solution(10728177509460358281)
XLA Ops:
  0.6 1.3 %shard_map.130 = (f32[8,32,128]{2,1,0:T(8,128)S(1)}, f32[8,32,128]{2,1,0:T(8,128)S(1)}, f32[8,32,128]{2,1,0:T(8,128)S(1)}, f32[8,32,128]{2,1,0:T(8,128)S(1)}, f3...) custom-call(f32[8,64,128]{2,1,0:T(8,128)} %refs_0_.1, f32[8,64,128]{2,1,0:T(8,128)} %refs_1_.1, f32[8,64,128]{2,1,0:T(8,128)} %refs_2_.1), custom_call_target="tpu_custom_call" | custom-call | flops 1000000 | bytes 1572864 | tf_op jit(solution)/shard_map/pallas_call | solution.py:128
  1.9 0.5 %collective-permute-start.1 = (f32[8,32,128]{2,1,0:T(8,128)S(1)}, f32[8,32,128]{2,1,0:T(8,128)S(1)}, u32[]{:S(2)}, u32[]{:S(2)}) collective-permute-start(f32[8,32,128]{2,1,0:T(8,128)S(1)} %get-tuple-element.63), channel_id=1, source_target_pairs={{0,2},{2,0},{4,6},{6,4},{8,10},{10,8},{12,14},{14,12},{16,18},{18,... | collective-permute-start | bytes 393224 | tf_op jit(solution)/shard_map/ppermute | solution.py:154
  2.6 0.5 %collective-permute-start = (f32[8,32,128]{2,1,0:T(8,128)S(1)}, f32[8,32,128]{2,1,0:T(8,128)S(1)}, u32[]{:S(2)}, u32[]{:S(2)}) collective-permute-start(f32[8,32,128]{2,1,0:T(8,128)S(1)} %get-tuple-element.60.refs_2_.refs_4_), channel_id=1, source_target_pairs={{0,2},{2,0},{4,6},{6,4},{8,10},{10,8},{12,14},{14,12},{16,18},{18,... | collective-permute-start | bytes 393224 | tf_op jit(solution)/shard_map/ppermute | solution.py:154
  3.5 0.4 collective-permute-done.2.refs_5_
  4.0 0.3 shard_map.133
  4.3 3.9 %collective-permute-start.5 = (f32[5,32,128]{2,1,0:T(8,128)S(1)}, f32[5,32,128]{2,1,0:T(8,128)S(1)}, u32[]{:S(2)}, u32[]{:S(2)}) collective-permute-start(f32[5,32,128]{2,1,0:T(8,128)S(1)} %get-tuple-element.65.refs_2_.refs_0_), channel_id=1, source_target_pairs={{0,12},{2,14},{4,8},{6,10},{8,4},{10,6},{12,0},{14,2},{16,28},{18,... | collective-permute-start | bytes 245768 | tf_op jit(solution)/shard_map/ppermute | solution.py:154
  8.3 0.4 %collective-permute-start.4 = (f32[5,32,128]{2,1,0:T(8,128)S(1)}, f32[5,32,128]{2,1,0:T(8,128)S(1)}, u32[]{:S(2)}, u32[]{:S(2)}) collective-permute-start(f32[5,32,128]{2,1,0:T(8,128)S(1)} %get-tuple-element.65.refs_2_.refs_0_), channel_id=1, source_target_pairs={{0,8},{2,10},{4,12},{6,14},{8,0},{10,2},{12,4},{14,6},{16,24},{18,... | collective-permute-start | bytes 245768 | tf_op jit(solution)/shard_map/ppermute | solution.py:154
  8.9 0.4 shard_map.135
  9.6 1.8 %collective-permute-done.5.refs_3_ = f32[5,32,128]{2,1,0:T(8,128)S(1)} collective-permute-done((f32[5,32,128]{2,1,0:T(8,128)S(1)}, f32[5,32,128]{2,1,0:T(8,128)S(1)}, u32[]{:S(2)}, u32[]{:S(2)}) %collective-permute-start.5) | collective-permute-done | bytes 81952 | tf_op jit(solution)/shard_map/ppermute | solution.py:154
  11.4 1.6 %collective-permute-done.4.refs_2_ = f32[5,32,128]{2,1,0:T(8,128)S(1)} collective-permute-done((f32[5,32,128]{2,1,0:T(8,128)S(1)}, f32[5,32,128]{2,1,0:T(8,128)S(1)}, u32[]{:S(2)}, u32[]{:S(2)}) %collective-permute-start.4) | collective-permute-done | bytes 81952 | tf_op jit(solution)/shard_map/ppermute | solution.py:154
  13.2 2.7 %collective-permute-start.6 = (f32[2,32,128]{2,1,0:T(8,128)S(1)}, f32[2,32,128]{2,1,0:T(8,128)S(1)}, u32[]{:S(2)}, u32[]{:S(2)}) collective-permute-start(f32[2,32,128]{2,1,0:T(8,128)S(1)} %get-tuple-element.70.refs_0_), channel_id=1, source_target_pairs={{0,16},{2,18},{4,20},{6,22},{8,24},{10,26},{12,28},{14,30},{16,0},... | collective-permute-start | bytes 98312 | tf_op jit(solution)/shard_map/ppermute | solution.py:154
  15.9 2.2 %collective-permute-done.6.refs_1_ = f32[2,32,128]{2,1,0:T(8,128)S(1)} collective-permute-done((f32[2,32,128]{2,1,0:T(8,128)S(1)}, f32[2,32,128]{2,1,0:T(8,128)S(1)}, u32[]{:S(2)}, u32[]{:S(2)}) %collective-permute-start.6) | collective-permute-done | bytes 32800 | tf_op jit(solution)/shard_map/ppermute | solution.py:154
  18.5 1.6 %collective-permute-start.8 = (f32[5,16,128]{2,1,0:T(8,128)S(1)}, f32[5,16,128]{2,1,0:T(8,128)S(1)}, u32[]{:S(2)}, u32[]{:S(2)}) collective-permute-start(f32[5,16,128]{2,1,0:T(8,128)S(1)} %get-tuple-element.77.refs_4_.refs_0_), channel_id=1, source_target_pairs={{0,1},{1,0},{2,3},{3,2},{4,5},{5,4},{6,7},{7,6},{8,9},{9,8},{10,11... | collective-permute-start | bytes 122888 | tf_op jit(solution)/shard_map/ppermute | solution.py:166
  20.6 1.7 %collective-permute-done.9.refs_3_ = f32[5,16,128]{2,1,0:T(8,128)S(1)} collective-permute-done((f32[5,16,128]{2,1,0:T(8,128)S(1)}, f32[5,16,128]{2,1,0:T(8,128)S(1)}, u32[]{:S(2)}, u32[]{:S(2)}) %collective-permute-start.9) | collective-permute-done | bytes 40992 | tf_op jit(solution)/shard_map/ppermute | solution.py:166
  22.3 0.6 %collective-permute-done.8.refs_2_ = f32[5,16,128]{2,1,0:T(8,128)S(1)} collective-permute-done((f32[5,16,128]{2,1,0:T(8,128)S(1)}, f32[5,16,128]{2,1,0:T(8,128)S(1)}, u32[]{:S(2)}, u32[]{:S(2)}) %collective-permute-start.8) | collective-permute-done | bytes 40992 | tf_op jit(solution)/shard_map/ppermute | solution.py:166
  22.8 1.8 %shard_map.140 = (f32[3,3,16,128]{3,2,1,0:T(8,128)S(1)}, f32[4,16,8,128]{3,2,1,0:T(8,128)S(1)}, f32[2,16,8,128]{3,2,1,0:T(8,128)S(1)}, f32[4,128,128]{2,1,0:T(8,...) custom-call(f32[5,16,128]{2,1,0:T(8,128)S(1)} %get-tuple-element.77., ...), custom_call_target="tpu_custom_call" | custom-call | flops 1000000 | bytes 6565888 | tf_op jit(solution)/shard_map/pallas_call | solution.py:128
  24.6 1.0 %collective-permute-start.13 = (f32[40,128]{1,0:T(8,128)S(1)}, f32[40,128]{1,0:T(8,128)S(1)}, u32[]{:S(2)}, u32[]{:S(2)}) collective-permute-start(f32[40,128]{1,0:T(8,128)S(1)} %get-tuple-element.87.refs_1_.refs_0_), channel_id=1, source_target_pairs={{0,3},{1,2},{2,1},{3,0},{4,7},{5,6},{6,5},{7,4},{8,11},{9,10},{10,... | collective-permute-start | bytes 61448 | tf_op jit(solution)/shard_map/ppermute | solution.py:166
  25.6 0.9 %collective-permute-start.12 = (f32[40,128]{1,0:T(8,128)S(1)}, f32[40,128]{1,0:T(8,128)S(1)}, u32[]{:S(2)}, u32[]{:S(2)}) collective-permute-start(f32[40,128]{1,0:T(8,128)S(1)} %get-tuple-element.87.refs_1_.refs_0_), channel_id=1, source_target_pairs={{0,1},{1,0},{2,3},{3,2},{4,5},{5,4},{6,7},{7,6},{8,9},{9,8},{10,11... | collective-permute-start | bytes 61448 | tf_op jit(solution)/shard_map/ppermute | solution.py:166
  26.5 1.3 %collective-permute-done.13.refs_3_ = f32[40,128]{1,0:T(8,128)S(1)} collective-permute-done((f32[40,128]{1,0:T(8,128)S(1)}, f32[40,128]{1,0:T(8,128)S(1)}, u32[]{:S(2)}, u32[]{:S(2)}) %collective-permute-start.13) | collective-permute-done | bytes 20512 | tf_op jit(solution)/shard_map/ppermute | solution.py:166
  27.9 1.5 %collective-permute-done.12.refs_2_ = f32[40,128]{1,0:T(8,128)S(1)} collective-permute-done((f32[40,128]{1,0:T(8,128)S(1)}, f32[40,128]{1,0:T(8,128)S(1)}, u32[]{:S(2)}, u32[]{:S(2)}) %collective-permute-start.12) | collective-permute-done | bytes 20512 | tf_op jit(solution)/shard_map/ppermute | solution.py:166
  29.7 2.4 %collective-permute-start.16 = (f32[72,128]{1,0:T(8,128)S(1)}, f32[72,128]{1,0:T(8,128)S(1)}, u32[]{:S(2)}, u32[]{:S(2)}) collective-permute-start(f32[72,128]{1,0:T(8,128)S(1)} %get-tuple-element.93.refs_0_), channel_id=1, source_target_pairs={{0,12},{2,14},{4,8},{6,10},{8,4},{10,6},{12,0},{14,2},{16,28},{18,... | collective-permute-start | bytes 110600 | tf_op jit(solution)/shard_map/ppermute | solution.py:154
  32.0 0.5 %collective-permute-start.15 = (f32[72,128]{1,0:T(8,128)S(1)}, f32[72,128]{1,0:T(8,128)S(1)}, u32[]{:S(2)}, u32[]{:S(2)}) collective-permute-start(f32[72,128]{1,0:T(8,128)S(1)} %get-tuple-element.93.refs_0_), channel_id=1, source_target_pairs={{0,8},{2,10},{4,12},{6,14},{8,0},{10,2},{12,4},{14,6},{16,24},{18,... | collective-permute-start | bytes 110600 | tf_op jit(solution)/shard_map/ppermute | solution.py:154
  32.5 0.7 %collective-permute-start.14 = (f32[72,128]{1,0:T(8,128)S(1)}, f32[72,128]{1,0:T(8,128)S(1)}, u32[]{:S(2)}, u32[]{:S(2)}) collective-permute-start(f32[72,128]{1,0:T(8,128)S(1)} %get-tuple-element.93.refs_0_), channel_id=1, source_target_pairs={{0,4},{2,6},{4,0},{6,2},{8,12},{10,14},{12,8},{14,10},{16,20},{18,... | collective-permute-start | bytes 110600 | tf_op jit(solution)/shard_map/ppermute | solution.py:154
  33.2 1.5 %collective-permute-done.16.refs_3_ = f32[72,128]{1,0:T(8,128)S(1)} collective-permute-done((f32[72,128]{1,0:T(8,128)S(1)}, f32[72,128]{1,0:T(8,128)S(1)}, u32[]{:S(2)}, u32[]{:S(2)}) %collective-permute-start.16) | collective-permute-done | bytes 36896 | tf_op jit(solution)/shard_map/ppermute | solution.py:154
  34.8 1.2 %collective-permute-done.15.refs_2_ = f32[72,128]{1,0:T(8,128)S(1)} collective-permute-done((f32[72,128]{1,0:T(8,128)S(1)}, f32[72,128]{1,0:T(8,128)S(1)}, u32[]{:S(2)}, u32[]{:S(2)}) %collective-permute-start.15) | collective-permute-done | bytes 36896 | tf_op jit(solution)/shard_map/ppermute | solution.py:154
  36.0 0.5 %collective-permute-done.14.refs_1_ = f32[72,128]{1,0:T(8,128)S(1)} collective-permute-done((f32[72,128]{1,0:T(8,128)S(1)}, f32[72,128]{1,0:T(8,128)S(1)}, u32[]{:S(2)}, u32[]{:S(2)}) %collective-permute-start.14) | collective-permute-done | bytes 36896 | tf_op jit(solution)/shard_map/ppermute | solution.py:154
  36.5 2.6 %collective-permute-start.17 = (f32[40,128]{1,0:T(8,128)S(1)}, f32[40,128]{1,0:T(8,128)S(1)}, u32[]{:S(2)}, u32[]{:S(2)}) collective-permute-start(f32[40,128]{1,0:T(8,128)S(1)} %get-tuple-element.94.refs_0_), channel_id=1, source_target_pairs={{0,16},{2,18},{4,20},{6,22},{8,24},{10,26},{12,28},{14,30},{16,0},... | collective-permute-start | bytes 61448 | tf_op jit(solution)/shard_map/ppermute | solution.py:154
  39.4 0.6 %shard_map.145.refs_7_.refs_6_ = f32[16,32,128]{2,1,0:T(8,128)S(1)} custom-call(f32[16,32,128]{2,1,0:T(8,128)S(1)} %get-tuple-element.66.refs_0_.refs_4_, f32[16,32,128]{2,1,0:T(8,128)S(1)} %get-tuple-element.88.refs_0_.refs_1_, f32[16,32,128]{2,1,0:T(8,128)S(1)} %get-tuple-element.98.refs_2_, f32[4,16,8,128]{3,2,1,0:T(8,128)S(1)} %get-tuple-element.99.refs_3_, ...), custom_call_target="tpu_custom_call" | custom-call | flops 1000000 | bytes 1835008 | tf_op jit(solution)/shard_map/pallas_call | solution.py:128
  40.0 1.3 %collective-permute-done.17.refs_1_ = f32[40,128]{1,0:T(8,128)S(1)} collective-permute-done((f32[40,128]{1,0:T(8,128)S(1)}, f32[40,128]{1,0:T(8,128)S(1)}, u32[]{:S(2)}, u32[]{:S(2)}) %collective-permute-start.17) | collective-permute-done | bytes 20512 | tf_op jit(solution)/shard_map/ppermute | solution.py:154
  41.6 0.7 %shard_map.142 = f32[8,64,128]{2,1,0:T(8,128)} custom-call(f32[16,32,128]{2,1,0:T(8,128)S(1)} %get-tuple-element.88.refs_0_.refs_1_, f32[8,32,128]{2,1,0:T(8,128)S(1)} %collective-permute-done.10.refs_1_), custom_call_target="tpu_custom_call" | custom-call | flops 1000000 | bytes 655360 | tf_op jit(solution)/shard_map/pallas_call | solution.py:128
  42.4 0.6 %collective-permute-done.18.refs_1_ = f32[8,32,128]{2,1,0:T(8,128)S(1)} collective-permute-done((f32[8,32,128]{2,1,0:T(8,128)S(1)}, f32[8,32,128]{2,1,0:T(8,128)S(1)}, u32[]{:S(2)}, u32[]{:S(2)}) %collective-permute-start.18) | collective-permute-done | bytes 131104 | tf_op jit(solution)/shard_map/ppermute | solution.py:154
  42.9 0.7 %shard_map.148 = (f32[8,64,128]{2,1,0:T(8,128)}, f32[8,128]{1,0:T(8,128)}) custom-call(f32[8,32,128]{2,1,0:T(8,128)S(1)} %get-tuple-element.106.refs_0_, f32[8,32,128]{2,1,0:T(8,128)S(1)} %collective-permute-done.18.refs_1_, f32[8,128]{1,0:T(8,128)S(1)} %get-tuple-element.108.refs_2_), custom_call_target="tpu_custom_call" | custom-call | flops 1000000 | bytes 532480 | tf_op jit(solution)/shard_map/pallas_call | solution.py:128
  (42 shorter events, 3.2 us)
Async XLA Ops:
  1.9 1.6 %collective-permute-start.1 = (f32[8,32,128]{2,1,0:T(8,128)S(1)}, f32[8,32,128]{2,1,0:T(8,128)S(1)}, u32[]{:S(2)}, u32[]{:S(2)}) collective-permute-start(f32[8,32,128]{2,1,0:T(8,128)S(1)} %get-tuple-element.63), channel_id=1, source_target_pairs={{0,2},{2,0},{4,6},{6,4},{8,10},{10,8},{12,14},{14,12},{16,18},{18,... | collective-permute-start | bytes 393224 | tf_op jit(solution)/shard_map/ppermute | solution.py:154
  2.4 0.7 %copy-start.7 = (s32[32]{0:T(128)S(1)}, s32[32]{0:T(128)}, u32[]{:S(2)}) copy-start(s32[32]{0:T(128)} %param.14) | copy-start | bytes 388
  2.4 0.7 %copy-start.4 = (f32[32]{0:T(128)S(1)}, f32[32]{0:T(128)}, u32[]{:S(2)}) copy-start(f32[32]{0:T(128)} %param.17) | copy-start | bytes 388
  2.4 0.7 %copy-start.5 = (s32[32]{0:T(128)S(1)}, s32[32]{0:T(128)}, u32[]{:S(2)}) copy-start(s32[32]{0:T(128)} %param.16) | copy-start | bytes 388
  2.4 0.7 %copy-start.6 = (s32[32]{0:T(128)S(1)}, s32[32]{0:T(128)}, u32[]{:S(2)}) copy-start(s32[32]{0:T(128)} %param.15) | copy-start | bytes 388
  2.4 1.4 %collective-permute-start.2 = (f32[8,32,128]{2,1,0:T(8,128)S(1)}, f32[8,32,128]{2,1,0:T(8,128)S(1)}, u32[]{:S(2)}, u32[]{:S(2)}) collective-permute-start(f32[8,32,128]{2,1,0:T(8,128)S(1)} %get-tuple-element.64), channel_id=1, source_target_pairs={{0,2},{2,0},{4,6},{6,4},{8,10},{10,8},{12,14},{14,12},{16,18},{18,... | collective-permute-start | bytes 393224 | tf_op jit(solution)/shard_map/ppermute | solution.py:154
  2.6 1.5 %collective-permute-start = (f32[8,32,128]{2,1,0:T(8,128)S(1)}, f32[8,32,128]{2,1,0:T(8,128)S(1)}, u32[]{:S(2)}, u32[]{:S(2)}) collective-permute-start(f32[8,32,128]{2,1,0:T(8,128)S(1)} %get-tuple-element.60.refs_2_.refs_4_), channel_id=1, source_target_pairs={{0,2},{2,0},{4,6},{6,4},{8,10},{10,8},{12,14},{14,12},{16,18},{18,... | collective-permute-start | bytes 393224 | tf_op jit(solution)/shard_map/ppermute | solution.py:154
  4.3 7.1 %collective-permute-start.5 = (f32[5,32,128]{2,1,0:T(8,128)S(1)}, f32[5,32,128]{2,1,0:T(8,128)S(1)}, u32[]{:S(2)}, u32[]{:S(2)}) collective-permute-start(f32[5,32,128]{2,1,0:T(8,128)S(1)} %get-tuple-element.65.refs_2_.refs_0_), channel_id=1, source_target_pairs={{0,12},{2,14},{4,8},{6,10},{8,4},{10,6},{12,0},{14,2},{16,28},{18,... | collective-permute-start | bytes 245768 | tf_op jit(solution)/shard_map/ppermute | solution.py:154
  8.3 4.7 %collective-permute-start.4 = (f32[5,32,128]{2,1,0:T(8,128)S(1)}, f32[5,32,128]{2,1,0:T(8,128)S(1)}, u32[]{:S(2)}, u32[]{:S(2)}) collective-permute-start(f32[5,32,128]{2,1,0:T(8,128)S(1)} %get-tuple-element.65.refs_2_.refs_0_), channel_id=1, source_target_pairs={{0,8},{2,10},{4,12},{6,14},{8,0},{10,2},{12,4},{14,6},{16,24},{18,... | collective-permute-start | bytes 245768 | tf_op jit(solution)/shard_map/ppermute | solution.py:154
  8.7 4.4 %collective-permute-start.3 = (f32[5,32,128]{2,1,0:T(8,128)S(1)}, f32[5,32,128]{2,1,0:T(8,128)S(1)}, u32[]{:S(2)}, u32[]{:S(2)}) collective-permute-start(f32[5,32,128]{2,1,0:T(8,128)S(1)} %get-tuple-element.65.refs_2_.refs_0_), channel_id=1, source_target_pairs={{0,4},{2,6},{4,0},{6,2},{8,12},{10,14},{12,8},{14,10},{16,20},{18,... | collective-permute-start | bytes 245768 | tf_op jit(solution)/shard_map/ppermute | solution.py:154
  13.2 4.9 %collective-permute-start.6 = (f32[2,32,128]{2,1,0:T(8,128)S(1)}, f32[2,32,128]{2,1,0:T(8,128)S(1)}, u32[]{:S(2)}, u32[]{:S(2)}) collective-permute-start(f32[2,32,128]{2,1,0:T(8,128)S(1)} %get-tuple-element.70.refs_0_), channel_id=1, source_target_pairs={{0,16},{2,18},{4,20},{6,22},{8,24},{10,26},{12,28},{14,30},{16,0},... | collective-permute-start | bytes 98312 | tf_op jit(solution)/shard_map/ppermute | solution.py:154
  18.2 2.2 %copy-start.2 = (s32[1024]{0:T(1024)S(1)}, s32[1024]{0:T(1024)}, u32[]{:S(2)}) copy-start(s32[1024]{0:T(1024)} %param.20) | copy-start | bytes 12292
  18.2 2.2 %copy-start.3 = (f32[1024]{0:T(1024)S(1)}, f32[1024]{0:T(1024)}, u32[]{:S(2)}) copy-start(f32[1024]{0:T(1024)} %param.21) | copy-start | bytes 12292
  18.4 2.0 %copy-start.1 = (s32[1024]{0:T(1024)S(1)}, s32[1024]{0:T(1024)}, u32[]{:S(2)}) copy-start(s32[1024]{0:T(1024)} %param.19) | copy-start | bytes 12292
  18.4 1.9 %copy-start = (s32[1024]{0:T(1024)S(1)}, s32[1024]{0:T(1024)}, u32[]{:S(2)}) copy-start(s32[1024]{0:T(1024)} %param.18) | copy-start | bytes 12292
  18.4 3.9 %collective-permute-start.9 = (f32[5,16,128]{2,1,0:T(8,128)S(1)}, f32[5,16,128]{2,1,0:T(8,128)S(1)}, u32[]{:S(2)}, u32[]{:S(2)}) collective-permute-start(f32[5,16,128]{2,1,0:T(8,128)S(1)} %get-tuple-element.77.refs_4_.refs_0_), channel_id=1, source_target_pairs={{0,3},{1,2},{2,1},{3,0},{4,7},{5,6},{6,5},{7,4},{8,11},{9,10},{10,... | collective-permute-start | bytes 122888 | tf_op jit(solution)/shard_map/ppermute | solution.py:166
  18.5 4.4 %collective-permute-start.8 = (f32[5,16,128]{2,1,0:T(8,128)S(1)}, f32[5,16,128]{2,1,0:T(8,128)S(1)}, u32[]{:S(2)}, u32[]{:S(2)}) collective-permute-start(f32[5,16,128]{2,1,0:T(8,128)S(1)} %get-tuple-element.77.refs_4_.refs_0_), channel_id=1, source_target_pairs={{0,1},{1,0},{2,3},{3,2},{4,5},{5,4},{6,7},{7,6},{8,9},{9,8},{10,11... | collective-permute-start | bytes 122888 | tf_op jit(solution)/shard_map/ppermute | solution.py:166
  20.0 2.8 %collective-permute-start.7 = (f32[5,16,128]{2,1,0:T(8,128)S(1)}, f32[5,16,128]{2,1,0:T(8,128)S(1)}, u32[]{:S(2)}, u32[]{:S(2)}) collective-permute-start(f32[5,16,128]{2,1,0:T(8,128)S(1)} %get-tuple-element.77.refs_4_.refs_0_), channel_id=1, source_target_pairs={{0,2},{1,3},{2,0},{3,1},{4,6},{5,7},{6,4},{7,5},{8,10},{9,11},{10,... | collective-permute-start | bytes 122888 | tf_op jit(solution)/shard_map/ppermute | solution.py:166
  24.6 3.3 %collective-permute-start.13 = (f32[40,128]{1,0:T(8,128)S(1)}, f32[40,128]{1,0:T(8,128)S(1)}, u32[]{:S(2)}, u32[]{:S(2)}) collective-permute-start(f32[40,128]{1,0:T(8,128)S(1)} %get-tuple-element.87.refs_1_.refs_0_), channel_id=1, source_target_pairs={{0,3},{1,2},{2,1},{3,0},{4,7},{5,6},{6,5},{7,4},{8,11},{9,10},{10,... | collective-permute-start | bytes 61448 | tf_op jit(solution)/shard_map/ppermute | solution.py:166
  25.6 3.8 %collective-permute-start.12 = (f32[40,128]{1,0:T(8,128)S(1)}, f32[40,128]{1,0:T(8,128)S(1)}, u32[]{:S(2)}, u32[]{:S(2)}) collective-permute-start(f32[40,128]{1,0:T(8,128)S(1)} %get-tuple-element.87.refs_1_.refs_0_), channel_id=1, source_target_pairs={{0,1},{1,0},{2,3},{3,2},{4,5},{5,4},{6,7},{7,6},{8,9},{9,8},{10,11... | collective-permute-start | bytes 61448 | tf_op jit(solution)/shard_map/ppermute | solution.py:166
  26.5 2.9 %collective-permute-start.11 = (f32[40,128]{1,0:T(8,128)S(1)}, f32[40,128]{1,0:T(8,128)S(1)}, u32[]{:S(2)}, u32[]{:S(2)}) collective-permute-start(f32[40,128]{1,0:T(8,128)S(1)} %get-tuple-element.87.refs_1_.refs_0_), channel_id=1, source_target_pairs={{0,2},{1,3},{2,0},{3,1},{4,6},{5,7},{6,4},{7,5},{8,10},{9,11},{10,... | collective-permute-start | bytes 61448 | tf_op jit(solution)/shard_map/ppermute | solution.py:166
  29.7 5.1 %collective-permute-start.16 = (f32[72,128]{1,0:T(8,128)S(1)}, f32[72,128]{1,0:T(8,128)S(1)}, u32[]{:S(2)}, u32[]{:S(2)}) collective-permute-start(f32[72,128]{1,0:T(8,128)S(1)} %get-tuple-element.93.refs_0_), channel_id=1, source_target_pairs={{0,12},{2,14},{4,8},{6,10},{8,4},{10,6},{12,0},{14,2},{16,28},{18,... | collective-permute-start | bytes 110600 | tf_op jit(solution)/shard_map/ppermute | solution.py:154
  32.0 4.0 %collective-permute-start.15 = (f32[72,128]{1,0:T(8,128)S(1)}, f32[72,128]{1,0:T(8,128)S(1)}, u32[]{:S(2)}, u32[]{:S(2)}) collective-permute-start(f32[72,128]{1,0:T(8,128)S(1)} %get-tuple-element.93.refs_0_), channel_id=1, source_target_pairs={{0,8},{2,10},{4,12},{6,14},{8,0},{10,2},{12,4},{14,6},{16,24},{18,... | collective-permute-start | bytes 110600 | tf_op jit(solution)/shard_map/ppermute | solution.py:154
  32.5 4.0 %collective-permute-start.14 = (f32[72,128]{1,0:T(8,128)S(1)}, f32[72,128]{1,0:T(8,128)S(1)}, u32[]{:S(2)}, u32[]{:S(2)}) collective-permute-start(f32[72,128]{1,0:T(8,128)S(1)} %get-tuple-element.93.refs_0_), channel_id=1, source_target_pairs={{0,4},{2,6},{4,0},{6,2},{8,12},{10,14},{12,8},{14,10},{16,20},{18,... | collective-permute-start | bytes 110600 | tf_op jit(solution)/shard_map/ppermute | solution.py:154
  36.5 4.7 %collective-permute-start.17 = (f32[40,128]{1,0:T(8,128)S(1)}, f32[40,128]{1,0:T(8,128)S(1)}, u32[]{:S(2)}, u32[]{:S(2)}) collective-permute-start(f32[40,128]{1,0:T(8,128)S(1)} %get-tuple-element.94.refs_0_), channel_id=1, source_target_pairs={{0,16},{2,18},{4,20},{6,22},{8,24},{10,26},{12,28},{14,30},{16,0},... | collective-permute-start | bytes 61448 | tf_op jit(solution)/shard_map/ppermute | solution.py:154
  39.3 2.3 %collective-permute-start.10 = (f32[8,32,128]{2,1,0:T(8,128)S(1)}, f32[8,32,128]{2,1,0:T(8,128)S(1)}, u32[]{:S(2)}, u32[]{:S(2)}) collective-permute-start(f32[8,32,128]{2,1,0:T(8,128)S(1)} %get-tuple-element.89), channel_id=1, source_target_pairs={{0,2},{2,0},{4,6},{6,4},{8,10},{10,8},{12,14},{14,12},{16,18},{18,... | collective-permute-start | bytes 393224 | tf_op jit(solution)/shard_map/ppermute | solution.py:154
  41.5 1.4 %collective-permute-start.18 = (f32[8,32,128]{2,1,0:T(8,128)S(1)}, f32[8,32,128]{2,1,0:T(8,128)S(1)}, u32[]{:S(2)}, u32[]{:S(2)}) collective-permute-start(f32[8,32,128]{2,1,0:T(8,128)S(1)} %get-tuple-element.107), channel_id=1, source_target_pairs={{0,2},{2,0},{4,6},{6,4},{8,10},{10,8},{12,14},{14,12},{16,18},{18,... | collective-permute-start | bytes 393224 | tf_op jit(solution)/shard_map/ppermute | solution.py:154
